TPU v7x, 512 devices: a whole 4x4x16 slice. The times are simulated.
512 devices in a mesh: row: 8 (over x, core), col: 16 (over z_lo, y), layer: 4 (over z_hi).
Axes of the slice: x: 4, y: 4, z: 16 (z_hi: 4, z_lo: 4; z = z_hi * 4 + z_lo), core: 2. Of those that a mesh axis runs over, the one named last changes fastest.
Arguments:
- adjacency: bfloat16 [16, 512, 8192], P('col', 'row'), may hold values from 0 to 1.953125, as said below
- block_mask: int32 [64, 64], replicated, may hold values from 0 to 1, as said below
- prune_mask: int32 [64, 64], replicated, may hold values from 0 to 1, as said below
Outputs:
- expanded: float32 [16, 512, 8192], P(None, ('row', 'layer'), 'col')
Inputs may be any that keep to these rules, and one draw needn't show every extreme that they name: `block_mask`: 1 marks a block of 128 x 128 adjacency entries that holds edges, 0 one that is dropped. `prune_mask`: 1 keeps a block of the expanded matrix, 0 prunes it; every diagonal block is kept. `adjacency`: entries are nonnegative.
All inputs are finite; a program needn't handle non-finite values.
Results may differ from a plain program's by a relative error of at most 0.015.
Values may be sent and summed in bfloat16 or wider, within the bound.
No kernel may reach another device: no remote copies, remote signals or barrier semaphores. Data moves between devices by JAX's collectives and lax.ppermute only.
A program may use at most 64 MiB of HBM per device.

v0:
```python
import jax
import jax.numpy as jnp
from jax import lax
from jax.sharding import PartitionSpec as P

BLK = 128


def block_onehot(indices, block_count):
    return (indices[:, None] // BLK == jnp.arange(block_count, dtype=jnp.int32)[None, :]).astype(
        jnp.float32
    )


def unpack_partner(received, row_count, col_count):
    rows_dev = received.shape[1]
    width = received.shape[2]
    arranged = received.reshape(row_count, col_count, rows_dev, width)
    return arranged.transpose(3, 1, 0, 2).reshape(width, row_count * col_count * rows_dev)


def scaled_product(raw_rows, inner_degree, right_rows):
    scaled = (raw_rows.astype(jnp.float32) / inner_degree[None, :]).astype(jnp.bfloat16)
    return lax.dot_general(
        scaled, right_rows, (((1,), (1,)), ((), ())), preferred_element_type=jnp.float32
    )


def on_device(adjacency, block_mask, prune_mask):
    rows_dev = adjacency.shape[1]
    node_count = adjacency.shape[2]
    row_count = lax.axis_size("row")
    col_count = lax.axis_size("col")
    layer_count = lax.axis_size("layer")
    quarter = node_count // layer_count
    part_rows = rows_dev // layer_count
    block_count = block_mask.shape[0]
    row_id = lax.axis_index("row")
    col_id = lax.axis_index("col")
    layer_id = lax.axis_index("layer")
    first_row = (col_id * row_count + row_id) * rows_dev
    own_rows = first_row + jnp.arange(rows_dev, dtype=jnp.int32)
    keep_rows = jnp.dot(block_onehot(own_rows, block_count), block_mask.astype(jnp.float32))
    keep_full = jnp.repeat(keep_rows, BLK, axis=1).astype(jnp.bfloat16)
    masked = adjacency[0] * keep_full
    outgoing = masked.reshape(rows_dev, col_count, row_count, rows_dev).transpose(2, 1, 0, 3)
    outgoing = outgoing.reshape(row_count * col_count, rows_dev, rows_dev)
    column_ids = jnp.arange(node_count, dtype=jnp.int32)
    inner_start = layer_id * quarter
    received = lax.all_to_all(outgoing, ("row", "col"), split_axis=0, concat_axis=0, tiled=True)
    flipped = unpack_partner(received, row_count, col_count)
    diagonal = (column_ids[None, :] == own_rows[:, None]).astype(jnp.float32)
    symmetric = (masked.astype(jnp.float32) + flipped.astype(jnp.float32) + diagonal).astype(
        jnp.bfloat16
    )
    degree_own = jnp.sum(symmetric.astype(jnp.float32), axis=1)
    degree_all = lax.all_gather(degree_own, ("row", "col"), axis=0, tiled=True)
    degree = (
        degree_all.reshape(row_count, col_count, rows_dev).transpose(1, 0, 2).reshape(node_count)
    )
    inner_degree = lax.dynamic_slice_in_dim(degree, inner_start, quarter, 0)
    symmetric_inner = lax.dynamic_slice_in_dim(symmetric, inner_start, quarter, 1)
    right_source = (symmetric_inner.astype(jnp.float32) / degree_own[:, None]).astype(jnp.bfloat16)
    right_rows = lax.all_gather(right_source, "row", axis=0, tiled=True)
    partial_value = scaled_product(
        lax.all_gather(symmetric_inner, "col", axis=0, tiled=True), inner_degree, right_rows
    )
    tile_cols = row_count * rows_dev
    partial_tile = partial_value.reshape(col_count, rows_dev, tile_cols)
    summed = lax.psum_scatter(partial_tile, "layer", scatter_dimension=1, tiled=True)
    inflated = summed * summed
    tile_row_ids = (
        jnp.arange(col_count, dtype=jnp.int32)[:, None] * tile_cols
        + row_id * rows_dev
        + layer_id * part_rows
        + jnp.arange(part_rows, dtype=jnp.int32)[None, :]
    ).reshape(col_count * part_rows)
    tile_col_ids = col_id * tile_cols + jnp.arange(tile_cols, dtype=jnp.int32)
    keep_left = jnp.dot(block_onehot(tile_row_ids, block_count), prune_mask.astype(jnp.float32))
    keep_tile = jnp.dot(keep_left, block_onehot(tile_col_ids, block_count).T)
    pruned = inflated * keep_tile.reshape(col_count, part_rows, tile_cols)
    column_mass = lax.psum(jnp.sum(pruned, axis=(0, 1)), ("row", "layer"))
    return node_count * pruned / column_mass[None, None, :]


def solution(mesh):
    in_specs = (P("col", "row", None), P(), P())
    out_specs = P(None, ("row", "layer"), "col")
    return jax.shard_map(
        on_device, mesh=mesh, in_specs=in_specs, out_specs=out_specs, check_vma=False
    )
```

profile of v0, /device:TPU:16, one launch (start us, length us, event | category | flops | bytes accessed | tf_op | source)
XLA Modules:
  0.0 943.1 jit_solution(3579547021729286582)
XLA Ops:
  6.5 3.3 squeeze.6
  9.8 0.2 convolution_convert_fusion
  10.0 0.1 copy.7
  10.2 4.6 copy_multiply_fusion
  14.8 4.7 reshape.204
  19.5 12.7 %all-to-all-start = ((bf16[128,2,2048]{2,1,0:T(2,128)(2,1)}), bf16[128,2,2048]{2,1,0:T(2,128)(2,1)S(1)}, u32[]{:S(2)}, u32[]{:S(2)}) async-start(bf16[128,2,2048]{2,1,0:T(2,128)(2,1)} %reshape.204), calls=%async_computation | async-start | bytes 2097152 | tf_op jit(solution)/shard_map/all_to_all | solution.py:50
  32.1 0.0 all-gather.5.cloned.1.call-start
  32.2 27.6 %all-to-all-done = bf16[128,2,2048]{2,1,0:T(2,128)(2,1)S(1)} async-done(((bf16[128,2,2048]{2,1,0:T(2,128)(2,1)}), bf16[128,2,2048]{2,1,0:T(2,128)(2,1)S(1)}, u32[]{:S(2)}, u32[]{:S(2)}) %all-to-all-start) | async-done | bytes 1048608 | tf_op jit(solution)/shard_map/all_to_all | solution.py:50
  59.8 1.4 reshape.205
  61.2 2.4 convert_bitcast_fusion
  63.6 5.7 copy.10
  69.3 3.6 reshape.197
  72.9 0.6 broadcast_in_dim.6
  73.5 1.3 convert_reduce_fusion
  74.8 0.8 divide_convert_fusion.2
  75.6 0.0 all-gather.5.cloned.1.call-update
  75.6 0.0 all-gather.3.cloned.1.call-start
  75.7 0.7 all-gather.3.cloned.1.call-update
  76.4 0.0 reduce-scatter.2.cloned.1.call-start
  76.4 1.3 dynamic-slice
  78.4 0.3 dynamic-update-slice
  78.6 0.1 reshape.193
  78.8 0.1 reshape.194
  78.8 662.2 %all-reduce.1 = f32[8192]{0:T(1024)S(1)} all-reduce(f32[8192]{0:T(1024)S(1)} %reshape.194), channel_id=1, replica_groups=mesh['row'=8,'col'=16,'layer'=4] {'row','col'}, use_global_device_ids=true, to_apply=%add | all-reduce | flops 8192 | bytes 65536
  741.0 6.6 fusion
  747.6 0.0 reduce-scatter.2.cloned.1.call-update
  747.6 0.1 iota_add_fusion
  747.7 0.1 add.126
  747.8 96.1 %reduce-scatter.2.cloned.1.call-done = f32[16,16,512]{2,1,0:T(8,128)} async-done(((f32[16,64,512]{2,1,0:T(8,128)}), f32[16,16,512]{2,1,0:T(8,128)}) %reduce-scatter.2.cloned.1.call-update) | async-done | bytes 524304 | tf_op jit(solution)/shard_map/reduce_scatter | solution.py:70
  843.9 1.6 fusion.4
  845.4 89.2 %psum.7 = f32[512]{0:T(512)S(1)} all-reduce(f32[512]{0:T(512)S(1)} %get-tuple-element.9), channel_id=1, replica_groups=mesh['row'=8,'col'=16,'layer'=4] {'row','layer'}, use_global_device_ids=true, to_apply=%region_3.4 | all-reduce | flops 512 | bytes 4096 | tf_op jit(solution)/shard_map/psum | solution.py:82
  934.6 1.9 multiply_divide_fusion
  (17 shorter events, 0.1 us)
Async XLA Ops:
  6.5 3.3 copy-start.2
  19.5 40.3 %all-to-all-start = ((bf16[128,2,2048]{2,1,0:T(2,128)(2,1)}), bf16[128,2,2048]{2,1,0:T(2,128)(2,1)S(1)}, u32[]{:S(2)}, u32[]{:S(2)}) async-start(bf16[128,2,2048]{2,1,0:T(2,128)(2,1)} %reshape.204), calls=%async_computation | async-start | bytes 2097152 | tf_op jit(solution)/shard_map/all_to_all | solution.py:50
  32.1 708.9 %all-gather.5.cloned.1.call-start = ((), (), s32[]{:S(2)}) async-start(), calls=%async_computation.3 | async-start | bytes 2359296 | tf_op jit(solution)/shard_map/all_gather | solution.py:64
  69.2 4.2 copy-start
  75.6 665.4 %all-gather.3.cloned.1.call-start = ((), (), s32[]{:S(2)}) async-start(), calls=%async_computation.2 | async-start | bytes 4456448 | tf_op jit(solution)/shard_map/all_gather | solution.py:66
  76.4 767.5 %reduce-scatter.2.cloned.1.call-start = ((), (), s32[]{:S(2)}) async-start(), calls=%async_computation.4 | async-start | bytes 2621440 | tf_op jit(solution)/shard_map/reduce_scatter | solution.py:70
  747.6 96.3 %copy-start.1 = (s32[64,64]{1,0:T(8,128)S(1)}, s32[64,64]{1,0:T(8,128)}, u32[]{:S(2)}) copy-start(s32[64,64]{1,0:T(8,128)} %param.5) | copy-start | bytes 49156
Sparse Core Ops, SparseCore 0:
  75.8 32.9 all-gather.4
  110.8 89.2 all-gather.2
  747.7 96.0 reduce-scatter.1
where the time goes:
time: 944 us; the launch traced here: 943 us
  blocking collectives  751 us (80%)
  waiting for transfers between devices  124 us (13%)
  local copies, waits for them, and re-layouts  21.2 us (2%)
  between operations  13.9 us (1%)
  starting transfers between devices  12.8 us (1%)
  other arithmetic  11.2 us (1%)
    unnamed x1, blocking collectives  662 us
    reduce_scatter x1, waiting for transfers between devices, on_device(): lax.psum_scatter(partial_tile, 'layer', scatter_dimension=1, tiled=True)  96.1 us
    psum x1, blocking collectives, on_device(): column_mass = lax.psum(jnp.sum(pruned, axis=(0, 1)), ('row', 'layer'))  89.2 us
    all_to_all x1, waiting for transfers between devices, on_device(): lax.all_to_all(outgoing, ('row', 'col'), split_axis=0, concat_axis=0, til...  27.6 us
  transfers between devices with their start and end apart: 4, of which 2 were waited for; matrix products, arithmetic and copies ran while one was open for 0% of the time, Pallas kernels for 0%

commit v1 on v0

v1 whole, which is shorter than its diff:
```python
import jax
import jax.numpy as jnp
from jax import lax
from jax.sharding import Mesh, PartitionSpec as P

BLK = 128


def on_device(adjacency, block_mask, prune_mask):
    bf16, f32 = jnp.bfloat16, jnp.float32
    rows_dev = adjacency.shape[1]
    node_count = adjacency.shape[2]
    nx, nk, nz, ny, nl = (lax.axis_size(a) for a in ("x", "core", "zlo", "y", "zhi"))
    nc = nz * ny
    x_id, k_id = lax.axis_index("x"), lax.axis_index("core")
    c_id = lax.axis_index("zlo") * ny + lax.axis_index("y")
    l_id = lax.axis_index("zhi")
    part = rows_dev // nl
    half = node_count // nk
    own_block = c_id * nx + x_id
    keep = lax.dynamic_slice_in_dim(block_mask, own_block, 1, 0)[0].astype(bf16)
    masked = adjacency[0].reshape(rows_dev, nc, nx, BLK) * keep.reshape(1, nc, nx, 1)
    outgoing = masked.transpose(2, 1, 0, 3).reshape(nx * nc, rows_dev, BLK)
    received = lax.all_to_all(outgoing, ("x", "zlo", "y"), split_axis=0, concat_axis=0, tiled=True)
    flipped = received.reshape(half, BLK).T
    halves = masked.reshape(rows_dev, nc, nx, nk, rows_dev).transpose(3, 0, 2, 1, 4)
    halves = halves.reshape(nk, rows_dev, half)
    kept = jnp.where(k_id == 0, halves[0], halves[1])
    given = jnp.where(k_id == 0, halves[1], halves[0])
    other = lax.ppermute(given, "core", [(0, 1), (1, 0)])
    direct = jnp.concatenate(
        [jnp.where(k_id == 0, kept, other), jnp.where(k_id == 0, other, kept)], axis=0
    )
    own_row = jnp.arange(nk * rows_dev, dtype=jnp.int32)
    own_col = (x_id * nc + c_id) * rows_dev + own_row - k_id * rows_dev
    col_ids = jnp.arange(half, dtype=jnp.int32)
    in_core = (own_row // rows_dev == k_id)[:, None]
    diagonal = ((own_col[:, None] == col_ids[None, :]) & in_core).astype(f32)
    block = (direct.astype(f32) + flipped.astype(f32) + diagonal).astype(bf16)
    block_rows = block.reshape(nk, nl, part, half)
    shard = lax.dynamic_slice_in_dim(block_rows, l_id, 1, 1).reshape(nk * part, half)
    left = lax.all_gather(shard, ("zlo", "y"), axis=0, tiled=True)
    blocks = [block] + [
        lax.ppermute(block, "x", [(i, (i + o) % nx) for i in range(nx)]) for o in range(1, nx)
    ]
    degree_chip = lax.psum(jnp.sum(block.astype(f32), axis=1), "core").reshape(nk, rows_dev)
    degree_own = jnp.where(k_id == 0, degree_chip[0], degree_chip[1])
    spread = jnp.broadcast_to(degree_own[None], (nx * nc, rows_dev))
    degree = lax.all_to_all(spread, ("x", "zlo", "y"), split_axis=0, concat_axis=0, tiled=True)
    scale = 1.0 / degree.reshape(1, half)
    order = (x_id - jnp.arange(nx)) % nx
    right = jnp.stack(blocks)[order].reshape(nx * BLK, half)
    right = (right.astype(f32) * scale).astype(bf16)
    partial = lax.dot_general(left, right, (((1,), (1,)), ((), ())), preferred_element_type=f32)
    partial = partial.reshape(nc, nk, part, nx * BLK)
    mine = jnp.where(k_id == 0, partial[:, 0], partial[:, 1])
    theirs = jnp.where(k_id == 0, partial[:, 1], partial[:, 0])
    summed = mine + lax.ppermute(theirs, "core", [(0, 1), (1, 0)])
    prune = prune_mask.reshape(nc, nx, nc, nx)
    prune = lax.dynamic_index_in_dim(prune, x_id, 1, keepdims=False)
    prune = lax.dynamic_index_in_dim(prune, c_id, 1, keepdims=False)
    prune = jnp.repeat(prune.astype(f32), BLK, axis=1)
    pruned = summed * summed * prune[:, None, :]
    mass = jnp.sum(pruned, axis=(0, 1))
    for axis in ("core", "x", "zhi"):
        mass = lax.psum(mass, axis)
    return pruned * (node_count / mass)[None, None, :]


def solution(mesh):
    rows, cols, layers = mesh.devices.shape
    devices = mesh.devices.reshape(rows // 2, 2, cols // 4, 4, layers)
    split = Mesh(devices, ("x", "core", "zlo", "y", "zhi"))
    in_specs = (P(("zlo", "y"), ("x", "core"), None), P(), P())
    out_specs = P(None, ("x", "core", "zhi"), ("zlo", "y"))
    return jax.shard_map(
        on_device, mesh=split, in_specs=in_specs, out_specs=out_specs, check_vma=False
    )
```

time: 944 us -> 198 us (0.21)
  the two profiles are of different devices: /device:TPU:16 before, /device:TPU:8 now
where the time goes in v1:
time: 198 us
  waiting for transfers between devices  80.7 us (41%)
  starting transfers between devices  32.3 us (16%)
  blocking collectives  31.4 us (16%)
  other arithmetic  17.3 us (9%)
  local copies, waits for them, and re-layouts  16.5 us (8%)
  between operations  13.6 us (7%)
  matrix products  5.83 us (3%)
    all_to_all x1, waiting for transfers between devices, on_device(): lax.all_to_all(spread, ('x', 'zlo', 'y'), split_axis=0, concat_axis=0, ti...  31 us
    psum x3, blocking collectives, on_device(): mass = lax.psum(mass, axis)  29 us
    all_gather x1, waiting for transfers between devices, on_device(): left = lax.all_gather(shard, ('zlo', 'y'), axis=0, tiled=True)  27.6 us
    all_to_all x1, waiting for transfers between devices, on_device(): lax.all_to_all(outgoing, ('x', 'zlo', 'y'), split_axis=0, concat_axis=0,...  19.7 us
    all_to_all x1, starting transfers between devices, on_device(): lax.all_to_all(outgoing, ('x', 'zlo', 'y'), split_axis=0, concat_axis=0,...  12.2 us
    ppermute x3, starting transfers between devices, on_device(): lax.ppermute(block, 'x', [(i, (i + o) % nx) for i in range(nx)])  8.39 us
    all_to_all x1, starting transfers between devices, on_device(): lax.all_to_all(spread, ('x', 'zlo', 'y'), split_axis=0, concat_axis=0, ti...  7.88 us
    dot_general x1, matrix products, on_device(): lax.dot_general(left, right, (((1,), (1,)), ((), ())), preferred_element_...  5.83 us
  transfers between devices with their start and end apart: 8, of which 5 were waited for; matrix products, arithmetic and copies ran while one was open for 10% of the time, Pallas kernels for 0%

profile of v1, /device:TPU:8, one launch (start us, length us, event | category | flops | bytes accessed | tf_op | source)
XLA Modules:
  0.0 197.8 jit_solution(6915983874260592604)
XLA Ops:
  6.5 0.7 fusion.9
  7.3 1.9 reshape_squeeze.6
  9.7 1.7 copy.32
  11.4 12.2 %all-to-all-start = ((bf16[64,64,128]{2,1,0:T(8,128)(2,1)}), bf16[64,64,128]{2,1,0:T(8,128)(2,1)}, u32[]{:S(2)}, u32[]{:S(2)}) async-start(bf16[64,64,128]{2,1,0:T(8,128)(2,1)} %bitcast.2), calls=%async_computation | async-start | bytes 2097152 | tf_op jit(solution)/shard_map/all_to_all | solution.py:24
  23.8 2.3 %reshape_squeeze.5 = bf16[64,16,4,2,64]{4,3,2,1,0:T(2,128)(2,1)S(1)} reshape(bf16[1,64,8192]{2,1,0:T(8,128)(2,1)S(1)} %copy-done) | data formatting | bytes 2097152 | tf_op jit(solution)/shard_map/reshape;squeeze | solution.py:22
  26.5 0.8 select_n.114
  27.3 1.9 collective-permute-start
  29.2 0.8 select_n.112
  30.1 1.0 collective-permute-done
  31.1 1.0 broadcast_select_fusion.3
  32.2 19.7 %all-to-all-done = bf16[64,64,128]{2,1,0:T(8,128)(2,1)} async-done(((bf16[64,64,128]{2,1,0:T(8,128)(2,1)}), bf16[64,64,128]{2,1,0:T(8,128)(2,1)}, u32[]{:S(2)}, u32[]{:S(2)}) %all-to-all-start) | async-done | bytes 1048608 | tf_op jit(solution)/shard_map/all_to_all | solution.py:24
  51.9 2.7 %bitcast_convert_fusion = f32[4096,128]{1,0:T(8,128)} fusion(bf16[64,64,128]{2,1,0:T(8,128)(2,1)} %all-to-all-done), kind=kLoop, calls=%fused_computation.11 | loop fusion | flops 524288 | bytes 3145728 | tf_op jit(solution)/shard_map/convert_element_type | solution.py:39
  54.6 1.9 copy.33
  56.5 2.0 convert_reduce_fusion
  58.5 0.7 constant_dynamic-slice_fusion.1
  59.2 2.5 %collective-permute-start.2 = (bf16[128,4096]{1,0:T(8,128)(2,1)S(1)}, bf16[128,4096]{1,0:T(8,128)(2,1)S(1)}, u32[]{:S(2)}, u32[]{:S(2)}) collective-permute-start(bf16[128,4096]{1,0:T(8,128)(2,1)S(1)} %get-tuple-element.8), channel_id=1, source_target_pairs={{0,256},{128,384},{256,0},{384,128},{1,257},{129,385},{257,1},{385... | collective-permute-start | bytes 3145736 | tf_op jit(solution)/shard_map/ppermute | solution.py:44
  61.8 3.0 %collective-permute-start.3 = (bf16[128,4096]{1,0:T(8,128)(2,1)S(1)}, bf16[128,4096]{1,0:T(8,128)(2,1)S(1)}, u32[]{:S(2)}, u32[]{:S(2)}) collective-permute-start(bf16[128,4096]{1,0:T(8,128)(2,1)S(1)} %get-tuple-element.8), channel_id=1, source_target_pairs={{0,384},{128,0},{256,128},{384,256},{1,385},{129,1},{257,129},{385... | collective-permute-start | bytes 3145736 | tf_op jit(solution)/shard_map/ppermute | solution.py:44
  64.8 2.8 %collective-permute-start.1 = (bf16[128,4096]{1,0:T(8,128)(2,1)S(1)}, bf16[128,4096]{1,0:T(8,128)(2,1)}, u32[]{:S(2)}, u32[]{:S(2)}) collective-permute-start(bf16[128,4096]{1,0:T(8,128)(2,1)S(1)} %get-tuple-element.8), channel_id=1, source_target_pairs={{0,128},{128,256},{256,384},{384,0},{1,129},{129,257},{257,385},{3... | collective-permute-start | bytes 3145736 | tf_op jit(solution)/shard_map/ppermute | solution.py:44
  67.7 2.5 %psum.28 = f32[128]{0:T(128)S(1)} all-reduce(f32[128]{0:T(128)S(1)} %get-tuple-element.7), channel_id=1, replica_groups=mesh['x'=4,'core'=2,'zlo'=4,'y'=4,'zhi'=4] {'core'}, use_global_device_ids=true, to_apply=%region_1.2 | all-reduce | flops 128 | bytes 1024 | tf_op jit(solution)/shard_map/psum | solution.py:46
  70.8 7.9 %all-to-all-start.1 = ((f32[64,1,64]{2,1,0:T(1,128)}), f32[64,1,64]{2,1,0:T(1,128)S(1)}, u32[]{:S(2)}, u32[]{:S(2)}) async-start(f32[64,1,64]{2,1,0:T(1,128)} %broadcast_in_dim.4), calls=%async_computation.1 | async-start | bytes 65536 | tf_op jit(solution)/shard_map/all_to_all | solution.py:49
  78.7 31.0 %all-to-all-done.1 = f32[64,1,64]{2,1,0:T(1,128)S(1)} async-done(((f32[64,1,64]{2,1,0:T(1,128)}), f32[64,1,64]{2,1,0:T(1,128)S(1)}, u32[]{:S(2)}, u32[]{:S(2)}) %all-to-all-start.1) | async-done | bytes 16416 | tf_op jit(solution)/shard_map/all_to_all | solution.py:49
  109.9 3.3 %pad_maximum_fusion = bf16[4,128,4096]{2,1,0:T(8,128)(2,1)} fusion(bf16[1,128,4096]{2,1,0:T(8,128)(2,1)S(1)} %bitcast.75, bf16[1,128,4096]{2,1,0:T(8,128)(2,1)S(1)} %bitcast.74, bf16[1,128,4096]{2,1,0:T(8,128)(2,1)} %bitcast.9, bf16[1,128,4096]{2,1,0:T(8,128)(2,1)S(1)} %bitcast.71), kind=kLoop, calls=%fused_computation.2 | loop fusion | flops 6291456 | bytes 8388608 | tf_op jit(solution)/shard_map/stack | solution.py:52
  113.2 5.0 %gather_fusion = bf16[4,128,4096]{2,1,0:T(8,128)(2,1)} fusion(bf16[4,128,4096]{2,1,0:T(8,128)(2,1)} %pad_maximum_fusion, s32[1024]{0:T(1024)S(1)} %pad_clamp_fusion), kind=kCustom, calls=%fused_computation | custom fusion | bytes 8388624 | tf_op jit(solution)/shard_map/gather | solution.py:52
  118.2 5.3 %multiply_convert_fusion = bf16[4,128,4096]{2,1,0:T(8,128)(2,1)} fusion(bf16[4,128,4096]{2,1,0:T(8,128)(2,1)} %gather_fusion, f32[4096]{0:T(1024)S(1)} %div.32), kind=kLoop, calls=%fused_computation.1 | loop fusion | flops 6291456 | bytes 8404992 | tf_op jit(solution)/shard_map/convert_element_type | solution.py:53
  123.5 27.6 %all-gather.2.cloned.1.call-done = bf16[512,4096]{1,0:T(8,128)(2,1)} async-done(((bf16[32,4096]{1,0:T(8,128)(2,1)}), bf16[512,4096]{1,0:T(8,128)(2,1)}) %all-gather.2.cloned.1.call-update) | async-done | bytes 4194320 | tf_op jit(solution)/shard_map/all_gather | solution.py:42
  151.1 5.8 %fusion.16 = f32[16,2,16,512]{3,2,1,0:T(8,128)S(1)} fusion(bf16[16,2,16,4096]{3,2,1,0:T(8,128)(2,1)} %bitcast.78, bf16[512,4096,1,1]{1,0,3,2:T(8,128)(2,1)} %bitcast.72), kind=kOutput, calls=%fused_computation.48 | convolution fusion | flops 2147483648 | bytes 9437184 | tf_op jit(solution)/shard_map/dot_general | solution.py:54
  157.1 1.9 collective-permute-start.4
  159.6 1.3 collective-permute-done.4
  161.1 2.5 %psum.29 = f32[512]{0:T(512)S(1)} all-reduce(f32[512]{0:T(512)S(1)} %get-tuple-element.5), channel_id=1, replica_groups=mesh['x'=4,'core'=2,'zlo'=4,'y'=4,'zhi'=4] {'core'}, use_global_device_ids=true, to_apply=%region_3.4 | all-reduce | flops 512 | bytes 4096 | tf_op jit(solution)/shard_map/psum | solution.py:66
  163.5 10.1 %psum.30 = f32[512]{0:T(512)S(1)} all-reduce(f32[512]{0:T(512)S(1)} %psum.29), channel_id=1, replica_groups=mesh['x'=4,'core'=2,'zlo'=4,'y'=4,'zhi'=4] {'x'}, use_global_device_ids=true, to_apply=%region_4.5 | all-reduce | flops 512 | bytes 4096 | tf_op jit(solution)/shard_map/psum | solution.py:66
  173.7 16.4 %psum.31 = f32[512]{0:T(512)S(1)} all-reduce(f32[512]{0:T(512)S(1)} %psum.30), channel_id=1, replica_groups=mesh['x'=4,'core'=2,'zlo'=4,'y'=4,'zhi'=4] {'zhi'}, use_global_device_ids=true, to_apply=%region_5.6 | all-reduce | flops 512 | bytes 4096 | tf_op jit(solution)/shard_map/psum | solution.py:66
  190.0 0.9 broadcast_multiply_fusion
  (32 shorter events, 3.0 us)
Async XLA Ops:
  7.3 16.4 %copy-start = (bf16[1,64,8192]{2,1,0:T(8,128)(2,1)S(1)}, bf16[1,64,8192]{2,1,0:T(8,128)(2,1)}, u32[]{:S(2)}) copy-start(bf16[1,64,8192]{2,1,0:T(8,128)(2,1)} %param.3) | copy-start | bytes 3145732
  11.4 40.5 %all-to-all-start = ((bf16[64,64,128]{2,1,0:T(8,128)(2,1)}), bf16[64,64,128]{2,1,0:T(8,128)(2,1)}, u32[]{:S(2)}, u32[]{:S(2)}) async-start(bf16[64,64,128]{2,1,0:T(8,128)(2,1)} %bitcast.2), calls=%async_computation | async-start | bytes 2097152 | tf_op jit(solution)/shard_map/all_to_all | solution.py:24
  23.6 127.5 %all-gather.2.cloned.1.call-start = ((), (), s32[]{:S(2)}) async-start(), calls=%async_computation.2 | async-start | bytes 4456448 | tf_op jit(solution)/shard_map/all_gather | solution.py:42
  27.3 3.8 %collective-permute-start = (bf16[64,4096]{1,0:T(8,128)(2,1)S(1)}, bf16[64,4096]{1,0:T(8,128)(2,1)S(1)}, u32[]{:S(2)}, u32[]{:S(2)}) collective-permute-start(bf16[64,4096]{1,0:T(8,128)(2,1)S(1)} %select_n.114), channel_id=1, source_target_pairs={{0,64},{64,0},{1,65},{65,1},{2,66},{66,2},{3,67},{67,3},{4,68},{68... | collective-permute-start | bytes 1572872 | tf_op jit(solution)/shard_map/ppermute | solution.py:30
  59.2 50.7 %collective-permute-start.2 = (bf16[128,4096]{1,0:T(8,128)(2,1)S(1)}, bf16[128,4096]{1,0:T(8,128)(2,1)S(1)}, u32[]{:S(2)}, u32[]{:S(2)}) collective-permute-start(bf16[128,4096]{1,0:T(8,128)(2,1)S(1)} %get-tuple-element.8), channel_id=1, source_target_pairs={{0,256},{128,384},{256,0},{384,128},{1,257},{129,385},{257,1},{385... | collective-permute-start | bytes 3145736 | tf_op jit(solution)/shard_map/ppermute | solution.py:44
  61.8 48.2 %collective-permute-start.3 = (bf16[128,4096]{1,0:T(8,128)(2,1)S(1)}, bf16[128,4096]{1,0:T(8,128)(2,1)S(1)}, u32[]{:S(2)}, u32[]{:S(2)}) collective-permute-start(bf16[128,4096]{1,0:T(8,128)(2,1)S(1)} %get-tuple-element.8), channel_id=1, source_target_pairs={{0,384},{128,0},{256,128},{384,256},{1,385},{129,1},{257,129},{385... | collective-permute-start | bytes 3145736 | tf_op jit(solution)/shard_map/ppermute | solution.py:44
  64.8 45.1 %collective-permute-start.1 = (bf16[128,4096]{1,0:T(8,128)(2,1)S(1)}, bf16[128,4096]{1,0:T(8,128)(2,1)}, u32[]{:S(2)}, u32[]{:S(2)}) collective-permute-start(bf16[128,4096]{1,0:T(8,128)(2,1)S(1)} %get-tuple-element.8), channel_id=1, source_target_pairs={{0,128},{128,256},{256,384},{384,0},{1,129},{129,257},{257,385},{3... | collective-permute-start | bytes 3145736 | tf_op jit(solution)/shard_map/ppermute | solution.py:44
  70.8 38.9 %all-to-all-start.1 = ((f32[64,1,64]{2,1,0:T(1,128)}), f32[64,1,64]{2,1,0:T(1,128)S(1)}, u32[]{:S(2)}, u32[]{:S(2)}) async-start(f32[64,1,64]{2,1,0:T(1,128)} %broadcast_in_dim.4), calls=%async_computation.1 | async-start | bytes 65536 | tf_op jit(solution)/shard_map/all_to_all | solution.py:49
  151.1 7.9 %copy-start.1 = (s32[64,64]{1,0:T(8,128)S(1)}, s32[64,64]{1,0:T(8,128)}, u32[]{:S(2)}) copy-start(s32[64,64]{1,0:T(8,128)} %param.5) | copy-start | bytes 49156
  157.1 3.8 %collective-permute-start.4 = (f32[16,16,512]{2,1,0:T(8,128)S(1)}, f32[16,16,512]{2,1,0:T(8,128)S(1)}, u32[]{:S(2)}, u32[]{:S(2)}) collective-permute-start(f32[16,16,512]{2,1,0:T(8,128)S(1)} %select_bitcast_fusion), channel_id=1, source_target_pairs={{0,64},{64,0},{1,65},{65,1},{2,66},{66,2},{3,67},{67,3},{4,68},{68... | collective-permute-start | bytes 1572872 | tf_op jit(solution)/shard_map/ppermute | solution.py:58
Sparse Core Ops, SparseCore 0:
  59.3 91.7 all-gather.1

commit v2 on v1

--- a/solution.py
+++ b/solution.py
@@ -38,18 +38,32 @@
     diagonal = ((own_col[:, None] == col_ids[None, :]) & in_core).astype(f32)
     block = (direct.astype(f32) + flipped.astype(f32) + diagonal).astype(bf16)
     block_rows = block.reshape(nk, nl, part, half)
-    shard = lax.dynamic_slice_in_dim(block_rows, l_id, 1, 1).reshape(nk * part, half)
-    left = lax.all_gather(shard, ("zlo", "y"), axis=0, tiled=True)
-    blocks = [block] + [
-        lax.ppermute(block, "x", [(i, (i + o) % nx) for i in range(nx)]) for o in range(1, nx)
-    ]
+    z_id = l_id * nz + lax.axis_index("zlo")
+
+    def shard_for(step):
+        layer = (z_id + step) % (nz * nl) // nz
+        return lax.dynamic_slice_in_dim(block_rows, layer, 1, 1).reshape(nk * part, half)
+
+    def z_pairs(step):
+        spots = [(z, (z + step) % (nz * nl)) for z in range(nz * nl)]
+        return [(a % nz * nl + a // nz, b % nz * nl + b // nz) for a, b in spots]
+
+    def y_pairs(step):
+        return [(i, (i + step) % ny) for i in range(ny)]
+
+    z_steps = [s if s <= nz // 2 else s - nz for s in range(1, nz)]
+    own = shard_for(0)
+    near = [lax.ppermute(shard_for(s), ("zlo", "zhi"), z_pairs(s)) for s in z_steps]
+    own_y = [own] + [lax.ppermute(own, "y", y_pairs(s)) for s in range(1, ny)]
+    near = jnp.concatenate(near, axis=0)
+    near_y = [near] + [lax.ppermute(near, "y", y_pairs(s)) for s in range(1, ny)]
+    left = jnp.concatenate([p for pair in zip(own_y, near_y) for p in pair], axis=0)
+    right = lax.all_gather(block, "x", axis=0, tiled=True)
     degree_chip = lax.psum(jnp.sum(block.astype(f32), axis=1), "core").reshape(nk, rows_dev)
     degree_own = jnp.where(k_id == 0, degree_chip[0], degree_chip[1])
     spread = jnp.broadcast_to(degree_own[None], (nx * nc, rows_dev))
     degree = lax.all_to_all(spread, ("x", "zlo", "y"), split_axis=0, concat_axis=0, tiled=True)
     scale = 1.0 / degree.reshape(1, half)
-    order = (x_id - jnp.arange(nx)) % nx
-    right = jnp.stack(blocks)[order].reshape(nx * BLK, half)
     right = (right.astype(f32) * scale).astype(bf16)
     partial = lax.dot_general(left, right, (((1,), (1,)), ((), ())), preferred_element_type=f32)
     partial = partial.reshape(nc, nk, part, nx * BLK)
@@ -59,6 +73,10 @@
     prune = prune_mask.reshape(nc, nx, nc, nx)
     prune = lax.dynamic_index_in_dim(prune, x_id, 1, keepdims=False)
     prune = lax.dynamic_index_in_dim(prune, c_id, 1, keepdims=False)
+    steps_z = (lax.axis_index("zlo") - jnp.arange(nz)) % nz
+    steps_y = (lax.axis_index("y") - jnp.arange(ny)) % ny
+    spot = (steps_y[None, :] * nz + steps_z[:, None]).reshape(nc)
+    summed = summed[spot]
     prune = jnp.repeat(prune.astype(f32), BLK, axis=1)
     pruned = summed * summed * prune[:, None, :]
     mass = jnp.sum(pruned, axis=(0, 1))

time: 198 us -> 193 us (0.975)
  starting transfers between devices: 32.3 us -> 58.9 us
  waiting for transfers between devices: 80.7 us -> 55.1 us
  other arithmetic: 17.3 us -> 7.67 us
  local copies, waits for them, and re-layouts: 16.5 us -> 20.9 us
    ppermute x3 -> x9, waiting for transfers between devices: 0.01 us -> 30.2 us  [the longest x3 26.1 us: on_device(): lax.ppermute(near, 'y', y_pairs(s))]
    all_to_all x1, waiting for transfers between devices: 31 us -> 1.5 us  [on_device(): lax.all_to_all(spread, ('x', 'zlo', 'y'), split_axis=0, concat_axis=0, ti...]
    all_gather x1, waiting for transfers between devices: 27.6 us -> 0.01 us  [on_device(): right = lax.all_gather(block, 'x', axis=0, tiled=True)]
    ppermute x3 -> x9, starting transfers between devices: 8.39 us -> 31.8 us  [the longest x3 11.5 us: on_device(): lax.ppermute(near, 'y', y_pairs(s))]
    unnamed x6 -> x14, local copies, waits for them, and re-layouts: 0.1 us -> 6.42 us
    convert_element_type x1 -> x0, other arithmetic: 5.3 us -> none  [on_device(): right = (right.astype(f32) * scale).astype(bf16)]
    gather x1, local copies, waits for them, and re-layouts: 5 us -> 0.58 us  [on_device(): summed = summed[spot]]
    another operation x1 -> x0, other arithmetic: 3.29 us -> none  [on_device(): right = jnp.stack(blocks)[order].reshape(nx * BLK, half)]
  transfers between devices with their start and end apart: 8 -> 14, of which waited for: 5 -> 7; matrix products, arithmetic and copies ran while one was open for 10% -> 8% of each run, Pallas kernels for 0% -> 0%
where the time goes in v2:
time: 193 us; the launch traced here: 192 us
  starting transfers between devices  58.9 us (31%)
  waiting for transfers between devices  55.1 us (29%)
  blocking collectives  29.7 us (15%)
  local copies, waits for them, and re-layouts  20.9 us (11%)
  between operations  13.9 us (7%)
  other arithmetic  7.67 us (4%)
  matrix products  5.83 us (3%)
    psum x3, blocking collectives, on_device(): mass = lax.psum(mass, axis)  27.2 us
    ppermute x3, waiting for transfers between devices, on_device(): lax.ppermute(near, 'y', y_pairs(s))  26.1 us
    all_to_all x1, waiting for transfers between devices, on_device(): lax.all_to_all(outgoing, ('x', 'zlo', 'y'), split_axis=0, concat_axis=0,...  20.7 us
    all_to_all x1, starting transfers between devices, on_device(): lax.all_to_all(outgoing, ('x', 'zlo', 'y'), split_axis=0, concat_axis=0,...  12.2 us
    ppermute x3, starting transfers between devices, on_device(): lax.ppermute(near, 'y', y_pairs(s))  11.5 us
    all_to_all x1, starting transfers between devices, on_device(): lax.all_to_all(spread, ('x', 'zlo', 'y'), split_axis=0, concat_axis=0, ti...  11 us
    ppermute x3, starting transfers between devices, on_device(): own_y = [own] + [lax.ppermute(own, 'y', y_pairs(s)) for s in range(1, ny)]  10.4 us
    ppermute x3, starting transfers between devices, on_device(): lax.ppermute(shard_for(s), ('zlo', 'zhi'), z_pairs(s))  9.87 us
  transfers between devices with their start and end apart: 14, of which 7 were waited for; matrix products, arithmetic and copies ran while one was open for 8% of the time, Pallas kernels for 0%

profile of v2, /device:TPU:8, one launch (start us, length us, event | category | flops | bytes accessed | tf_op | source)
XLA Modules:
  0.0 191.8 jit_solution(521976041934839716)
XLA Ops:
  7.3 1.9 reshape_squeeze.6
  9.7 1.6 copy.28
  11.4 12.2 %all-to-all-start = ((bf16[64,64,128]{2,1,0:T(8,128)(2,1)}), bf16[64,64,128]{2,1,0:T(8,128)(2,1)}, u32[]{:S(2)}, u32[]{:S(2)}) async-start(bf16[64,64,128]{2,1,0:T(8,128)(2,1)} %bitcast.2), calls=%async_computation | async-start | bytes 2097152 | tf_op jit(solution)/shard_map/all_to_all | solution.py:24
  23.7 2.3 %reshape_squeeze.5 = bf16[64,16,4,2,64]{4,3,2,1,0:T(2,128)(2,1)S(1)} reshape(bf16[1,64,8192]{2,1,0:T(8,128)(2,1)S(1)} %copy-done) | data formatting | bytes 2097152 | tf_op jit(solution)/shard_map/reshape;squeeze | solution.py:22
  27.3 1.9 %collective-permute-start = (bf16[64,4096]{1,0:T(8,128)(2,1)S(1)}, bf16[64,4096]{1,0:T(8,128)(2,1)S(1)}, u32[]{:S(2)}, u32[]{:S(2)}) collective-permute-start(bf16[64,4096]{1,0:T(8,128)(2,1)S(1)} %select_n.159), channel_id=1, source_target_pairs={{0,64},{64,0},{1,65},{65,1},{2,66},{66,2},{3,67},{67,3},{4,68},{68... | collective-permute-start | bytes 1572872 | tf_op jit(solution)/shard_map/ppermute | solution.py:30
  30.1 1.0 collective-permute-done
  31.2 20.7 %all-to-all-done = bf16[64,64,128]{2,1,0:T(8,128)(2,1)} async-done(((bf16[64,64,128]{2,1,0:T(8,128)(2,1)}), bf16[64,64,128]{2,1,0:T(8,128)(2,1)}, u32[]{:S(2)}, u32[]{:S(2)}) %all-to-all-start) | async-done | bytes 1048608 | tf_op jit(solution)/shard_map/all_to_all | solution.py:24
  51.8 2.7 %bitcast_convert_fusion = f32[4096,128]{1,0:T(8,128)} fusion(bf16[64,64,128]{2,1,0:T(8,128)(2,1)} %all-to-all-done), kind=kLoop, calls=%fused_computation.12 | loop fusion | flops 524288 | bytes 3145728 | tf_op jit(solution)/shard_map/convert_element_type | solution.py:39
  54.5 1.9 %copy.29 = f32[4096,128]{0,1:T(8,128)S(1)} copy(f32[4096,128]{1,0:T(8,128)} %bitcast_convert_fusion) | data formatting | bytes 4194304 | tf_op jit(solution)/shard_map/convert_element_type | solution.py:39
  56.5 1.7 convert_reduce_fusion
  58.9 1.3 constant_dynamic-slice_fusion.1
  60.2 1.9 %collective-permute-start.1 = (bf16[32,4096]{1,0:T(8,128)(2,1)S(1)}, bf16[32,4096]{1,0:T(8,128)(2,1)S(1)}, u32[]{:S(2)}, u32[]{:S(2)}) collective-permute-start(bf16[32,4096]{1,0:T(8,128)(2,1)S(1)} %bitcast.61), channel_id=1, source_target_pairs={{0,16},{16,32},{32,48},{48,1},{1,17},{17,33},{33,49},{49,2},{2,18}... | collective-permute-start | bytes 786440 | tf_op jit(solution)/shard_map/ppermute | solution.py:56
  62.1 2.3 %collective-permute-start.2 = (bf16[32,4096]{1,0:T(8,128)(2,1)S(1)}, bf16[32,4096]{1,0:T(8,128)(2,1)S(1)}, u32[]{:S(2)}, u32[]{:S(2)}) collective-permute-start(bf16[32,4096]{1,0:T(8,128)(2,1)S(1)} %bitcast.60), channel_id=1, source_target_pairs={{0,32},{16,48},{32,1},{48,17},{1,33},{17,49},{33,2},{49,18},{2,34}... | collective-permute-start | bytes 786440 | tf_op jit(solution)/shard_map/ppermute | solution.py:56
  64.4 5.7 %collective-permute-start.3 = (bf16[32,4096]{1,0:T(8,128)(2,1)S(1)}, bf16[32,4096]{1,0:T(8,128)(2,1)S(1)}, u32[]{:S(2)}, u32[]{:S(2)}) collective-permute-start(bf16[32,4096]{1,0:T(8,128)(2,1)S(1)} %bitcast.59), channel_id=1, source_target_pairs={{0,51},{16,0},{32,16},{48,32},{1,48},{17,1},{33,17},{49,33},{2,49}... | collective-permute-start | bytes 786440 | tf_op jit(solution)/shard_map/ppermute | solution.py:56
  70.1 3.0 %collective-permute-start.4 = (bf16[32,4096]{1,0:T(8,128)(2,1)S(1)}, bf16[32,4096]{1,0:T(8,128)(2,1)S(1)}, u32[]{:S(2)}, u32[]{:S(2)}) collective-permute-start(bf16[32,4096]{1,0:T(8,128)(2,1)S(1)} %bitcast.53), channel_id=1, source_target_pairs={{0,4},{4,8},{8,12},{12,0},{1,5},{5,9},{9,13},{13,1},{2,6},{6,10},{... | collective-permute-start | bytes 786440 | tf_op jit(solution)/shard_map/ppermute | solution.py:57
  73.1 2.5 %psum.28 = f32[128]{0:T(128)S(1)} all-reduce(f32[128]{0:T(128)S(1)} %get-tuple-element.5), channel_id=1, replica_groups=mesh['x'=4,'core'=2,'zlo'=4,'y'=4,'zhi'=4] {'core'}, use_global_device_ids=true, to_apply=%region_1.2 | all-reduce | flops 128 | bytes 1024 | tf_op jit(solution)/shard_map/psum | solution.py:62
  77.1 4.1 %collective-permute-done.2 = bf16[32,4096]{1,0:T(8,128)(2,1)S(1)} collective-permute-done((bf16[32,4096]{1,0:T(8,128)(2,1)S(1)}, bf16[32,4096]{1,0:T(8,128)(2,1)S(1)}, u32[]{:S(2)}, u32[]{:S(2)}) %collective-permute-start.2) | collective-permute-done | bytes 262176 | tf_op jit(solution)/shard_map/ppermute | solution.py:56
  82.7 2.7 %collective-permute-start.5 = (bf16[96,4096]{1,0:T(8,128)(2,1)S(1)}, bf16[96,4096]{1,0:T(8,128)(2,1)S(1)}, u32[]{:S(2)}, u32[]{:S(2)}) collective-permute-start(bf16[96,4096]{1,0:T(8,128)(2,1)S(1)} %get-tuple-element.15), channel_id=1, source_target_pairs={{0,4},{4,8},{8,12},{12,0},{1,5},{5,9},{9,13},{13,1},{2,6},{6,10},{... | collective-permute-start | bytes 2359304 | tf_op jit(solution)/shard_map/ppermute | solution.py:59
  86.1 11.0 %all-to-all-start.1 = ((f32[64,1,64]{2,1,0:T(1,128)}), f32[64,1,64]{2,1,0:T(1,128)S(1)}, u32[]{:S(2)}, u32[]{:S(2)}) async-start(f32[64,1,64]{2,1,0:T(1,128)} %broadcast_in_dim.4), calls=%async_computation.1 | async-start | bytes 65536 | tf_op jit(solution)/shard_map/all_to_all | solution.py:65
  97.3 4.0 %collective-permute-start.6 = (bf16[32,4096]{1,0:T(8,128)(2,1)S(1)}, bf16[32,4096]{1,0:T(8,128)(2,1)S(1)}, u32[]{:S(2)}, u32[]{:S(2)}) collective-permute-start(bf16[32,4096]{1,0:T(8,128)(2,1)S(1)} %bitcast.55), channel_id=1, source_target_pairs={{0,8},{4,12},{8,0},{12,4},{1,9},{5,13},{9,1},{13,5},{2,10},{6,14},... | collective-permute-start | bytes 786440 | tf_op jit(solution)/shard_map/ppermute | solution.py:57
  101.3 3.4 %collective-permute-start.8 = (bf16[32,4096]{1,0:T(8,128)(2,1)S(1)}, bf16[32,4096]{1,0:T(8,128)(2,1)S(1)}, u32[]{:S(2)}, u32[]{:S(2)}) collective-permute-start(bf16[32,4096]{1,0:T(8,128)(2,1)S(1)} %bitcast.56), channel_id=1, source_target_pairs={{0,12},{4,0},{8,4},{12,8},{1,13},{5,1},{9,5},{13,9},{2,14},{6,2},{... | collective-permute-start | bytes 786440 | tf_op jit(solution)/shard_map/ppermute | solution.py:57
  104.6 1.5 all-to-all-done.1
  106.3 6.2 %collective-permute-start.7 = (bf16[96,4096]{1,0:T(8,128)(2,1)S(1)}, bf16[96,4096]{1,0:T(8,128)(2,1)S(1)}, u32[]{:S(2)}, u32[]{:S(2)}) collective-permute-start(bf16[96,4096]{1,0:T(8,128)(2,1)S(1)} %get-tuple-element.15), channel_id=1, source_target_pairs={{0,8},{4,12},{8,0},{12,4},{1,9},{5,13},{9,1},{13,5},{2,10},{6,14},... | collective-permute-start | bytes 2359304 | tf_op jit(solution)/shard_map/ppermute | solution.py:59
  112.6 2.6 %collective-permute-start.9 = (bf16[96,4096]{1,0:T(8,128)(2,1)S(1)}, bf16[96,4096]{1,0:T(8,128)(2,1)S(1)}, u32[]{:S(2)}, u32[]{:S(2)}) collective-permute-start(bf16[96,4096]{1,0:T(8,128)(2,1)S(1)} %get-tuple-element.15), channel_id=1, source_target_pairs={{0,12},{4,0},{8,4},{12,8},{1,13},{5,1},{9,5},{13,9},{2,14},{6,2},{... | collective-permute-start | bytes 2359304 | tf_op jit(solution)/shard_map/ppermute | solution.py:59
  117.6 14.1 %collective-permute-done.7 = bf16[96,4096]{1,0:T(8,128)(2,1)S(1)} collective-permute-done((bf16[96,4096]{1,0:T(8,128)(2,1)S(1)}, bf16[96,4096]{1,0:T(8,128)(2,1)S(1)}, u32[]{:S(2)}, u32[]{:S(2)}) %collective-permute-start.7) | collective-permute-done | bytes 786464 | tf_op jit(solution)/shard_map/ppermute | solution.py:59
  133.4 11.9 %collective-permute-done.9 = bf16[96,4096]{1,0:T(8,128)(2,1)S(1)} collective-permute-done((bf16[96,4096]{1,0:T(8,128)(2,1)S(1)}, bf16[96,4096]{1,0:T(8,128)(2,1)S(1)}, u32[]{:S(2)}, u32[]{:S(2)}) %collective-permute-start.9) | collective-permute-done | bytes 786464 | tf_op jit(solution)/shard_map/ppermute | solution.py:59
  146.3 5.8 %fusion = f32[512,512]{1,0:T(8,128)S(1)} fusion(bf16[512,4096]{1,0:T(8,128)(2,1)} %constant_dynamic-update-slice_fusion.3, bf16[512,4096]{1,0:T(8,128)(2,1)} %all-gather.2.cloned.1.call-done, f32[4096]{0:T(1024)S(1)} %div.73), kind=kOutput, calls=%fused_computation.2 | convolution fusion | flops 2153775104 | bytes 9453568 | tf_op jit(solution)/shard_map/dot_general | solution.py:68
  152.2 1.9 %collective-permute-start.10 = (f32[16,16,512]{2,1,0:T(8,128)S(1)}, f32[16,16,512]{2,1,0:T(8,128)S(1)}, u32[]{:S(2)}, u32[]{:S(2)}) collective-permute-start(f32[16,16,512]{2,1,0:T(8,128)S(1)} %select_bitcast_fusion), channel_id=1, source_target_pairs={{0,64},{64,0},{1,65},{65,1},{2,66},{66,2},{3,67},{67,3},{4,68},{68... | collective-permute-start | bytes 1572872 | tf_op jit(solution)/shard_map/ppermute | solution.py:72
  154.4 1.7 collective-permute-done.10
  156.9 2.5 %psum.29 = f32[512]{0:T(512)S(1)} all-reduce(f32[512]{0:T(512)S(1)} %fusion.7), channel_id=1, replica_groups=mesh['x'=4,'core'=2,'zlo'=4,'y'=4,'zhi'=4] {'core'}, use_global_device_ids=true, to_apply=%region_3.4 | all-reduce | flops 512 | bytes 4096 | tf_op jit(solution)/shard_map/psum | solution.py:84
  159.4 10.5 %psum.30 = f32[512]{0:T(512)S(1)} all-reduce(f32[512]{0:T(512)S(1)} %psum.29), channel_id=1, replica_groups=mesh['x'=4,'core'=2,'zlo'=4,'y'=4,'zhi'=4] {'x'}, use_global_device_ids=true, to_apply=%region_4.5 | all-reduce | flops 512 | bytes 4096 | tf_op jit(solution)/shard_map/psum | solution.py:84
  169.9 14.2 %psum.31 = f32[512]{0:T(512)S(1)} all-reduce(f32[512]{0:T(512)S(1)} %psum.30), channel_id=1, replica_groups=mesh['x'=4,'core'=2,'zlo'=4,'y'=4,'zhi'=4] {'zhi'}, use_global_device_ids=true, to_apply=%region_5.6 | all-reduce | flops 512 | bytes 4096 | tf_op jit(solution)/shard_map/psum | solution.py:84
  (56 shorter events, 15.1 us)
Async XLA Ops:
  7.3 16.4 %copy-start = (bf16[1,64,8192]{2,1,0:T(8,128)(2,1)S(1)}, bf16[1,64,8192]{2,1,0:T(8,128)(2,1)}, u32[]{:S(2)}) copy-start(bf16[1,64,8192]{2,1,0:T(8,128)(2,1)} %param.3) | copy-start | bytes 3145732
  11.4 40.5 %all-to-all-start = ((bf16[64,64,128]{2,1,0:T(8,128)(2,1)}), bf16[64,64,128]{2,1,0:T(8,128)(2,1)}, u32[]{:S(2)}, u32[]{:S(2)}) async-start(bf16[64,64,128]{2,1,0:T(8,128)(2,1)} %bitcast.2), calls=%async_computation | async-start | bytes 2097152 | tf_op jit(solution)/shard_map/all_to_all | solution.py:24
  23.6 122.7 %all-gather.2.cloned.1.call-start = ((), (), s32[]{:S(2)}) async-start(), calls=%async_computation.2 | async-start | bytes 5242880 | tf_op jit(solution)/shard_map/all_gather | solution.py:61
  27.3 3.8 %collective-permute-start = (bf16[64,4096]{1,0:T(8,128)(2,1)S(1)}, bf16[64,4096]{1,0:T(8,128)(2,1)S(1)}, u32[]{:S(2)}, u32[]{:S(2)}) collective-permute-start(bf16[64,4096]{1,0:T(8,128)(2,1)S(1)} %select_n.159), channel_id=1, source_target_pairs={{0,64},{64,0},{1,65},{65,1},{2,66},{66,2},{3,67},{67,3},{4,68},{68... | collective-permute-start | bytes 1572872 | tf_op jit(solution)/shard_map/ppermute | solution.py:30
  54.5 4.0 %copy-start.1 = (s32[64,64]{1,0:T(8,128)S(1)}, s32[64,64]{1,0:T(8,128)}, u32[]{:S(2)}) copy-start(s32[64,64]{1,0:T(8,128)} %param.5) | copy-start | bytes 49156
  60.2 16.1 %collective-permute-start.1 = (bf16[32,4096]{1,0:T(8,128)(2,1)S(1)}, bf16[32,4096]{1,0:T(8,128)(2,1)S(1)}, u32[]{:S(2)}, u32[]{:S(2)}) collective-permute-start(bf16[32,4096]{1,0:T(8,128)(2,1)S(1)} %bitcast.61), channel_id=1, source_target_pairs={{0,16},{16,32},{32,48},{48,1},{1,17},{17,33},{33,49},{49,2},{2,18}... | collective-permute-start | bytes 786440 | tf_op jit(solution)/shard_map/ppermute | solution.py:56
  62.1 19.1 %collective-permute-start.2 = (bf16[32,4096]{1,0:T(8,128)(2,1)S(1)}, bf16[32,4096]{1,0:T(8,128)(2,1)S(1)}, u32[]{:S(2)}, u32[]{:S(2)}) collective-permute-start(bf16[32,4096]{1,0:T(8,128)(2,1)S(1)} %bitcast.60), channel_id=1, source_target_pairs={{0,32},{16,48},{32,1},{48,17},{1,33},{17,49},{33,2},{49,18},{2,34}... | collective-permute-start | bytes 786440 | tf_op jit(solution)/shard_map/ppermute | solution.py:56
  64.4 17.6 %collective-permute-start.3 = (bf16[32,4096]{1,0:T(8,128)(2,1)S(1)}, bf16[32,4096]{1,0:T(8,128)(2,1)S(1)}, u32[]{:S(2)}, u32[]{:S(2)}) collective-permute-start(bf16[32,4096]{1,0:T(8,128)(2,1)S(1)} %bitcast.59), channel_id=1, source_target_pairs={{0,51},{16,0},{32,16},{48,32},{1,48},{17,1},{33,17},{49,33},{2,49}... | collective-permute-start | bytes 786440 | tf_op jit(solution)/shard_map/ppermute | solution.py:56
  70.1 42.5 %collective-permute-start.4 = (bf16[32,4096]{1,0:T(8,128)(2,1)S(1)}, bf16[32,4096]{1,0:T(8,128)(2,1)S(1)}, u32[]{:S(2)}, u32[]{:S(2)}) collective-permute-start(bf16[32,4096]{1,0:T(8,128)(2,1)S(1)} %bitcast.53), channel_id=1, source_target_pairs={{0,4},{4,8},{8,12},{12,0},{1,5},{5,9},{9,13},{13,1},{2,6},{6,10},{... | collective-permute-start | bytes 786440 | tf_op jit(solution)/shard_map/ppermute | solution.py:57
  82.7 33.1 %collective-permute-start.5 = (bf16[96,4096]{1,0:T(8,128)(2,1)S(1)}, bf16[96,4096]{1,0:T(8,128)(2,1)S(1)}, u32[]{:S(2)}, u32[]{:S(2)}) collective-permute-start(bf16[96,4096]{1,0:T(8,128)(2,1)S(1)} %get-tuple-element.15), channel_id=1, source_target_pairs={{0,4},{4,8},{8,12},{12,0},{1,5},{5,9},{9,13},{13,1},{2,6},{6,10},{... | collective-permute-start | bytes 2359304 | tf_op jit(solution)/shard_map/ppermute | solution.py:59
  86.1 20.0 %all-to-all-start.1 = ((f32[64,1,64]{2,1,0:T(1,128)}), f32[64,1,64]{2,1,0:T(1,128)S(1)}, u32[]{:S(2)}, u32[]{:S(2)}) async-start(f32[64,1,64]{2,1,0:T(1,128)} %broadcast_in_dim.4), calls=%async_computation.1 | async-start | bytes 65536 | tf_op jit(solution)/shard_map/all_to_all | solution.py:65
  97.3 19.6 %collective-permute-start.6 = (bf16[32,4096]{1,0:T(8,128)(2,1)S(1)}, bf16[32,4096]{1,0:T(8,128)(2,1)S(1)}, u32[]{:S(2)}, u32[]{:S(2)}) collective-permute-start(bf16[32,4096]{1,0:T(8,128)(2,1)S(1)} %bitcast.55), channel_id=1, source_target_pairs={{0,8},{4,12},{8,0},{12,4},{1,9},{5,13},{9,1},{13,5},{2,10},{6,14},... | collective-permute-start | bytes 786440 | tf_op jit(solution)/shard_map/ppermute | solution.py:57
  101.3 31.4 %collective-permute-start.8 = (bf16[32,4096]{1,0:T(8,128)(2,1)S(1)}, bf16[32,4096]{1,0:T(8,128)(2,1)S(1)}, u32[]{:S(2)}, u32[]{:S(2)}) collective-permute-start(bf16[32,4096]{1,0:T(8,128)(2,1)S(1)} %bitcast.56), channel_id=1, source_target_pairs={{0,12},{4,0},{8,4},{12,8},{1,13},{5,1},{9,5},{13,9},{2,14},{6,2},{... | collective-permute-start | bytes 786440 | tf_op jit(solution)/shard_map/ppermute | solution.py:57
  106.3 25.4 %collective-permute-start.7 = (bf16[96,4096]{1,0:T(8,128)(2,1)S(1)}, bf16[96,4096]{1,0:T(8,128)(2,1)S(1)}, u32[]{:S(2)}, u32[]{:S(2)}) collective-permute-start(bf16[96,4096]{1,0:T(8,128)(2,1)S(1)} %get-tuple-element.15), channel_id=1, source_target_pairs={{0,8},{4,12},{8,0},{12,4},{1,9},{5,13},{9,1},{13,5},{2,10},{6,14},... | collective-permute-start | bytes 2359304 | tf_op jit(solution)/shard_map/ppermute | solution.py:59
  112.6 32.8 %collective-permute-start.9 = (bf16[96,4096]{1,0:T(8,128)(2,1)S(1)}, bf16[96,4096]{1,0:T(8,128)(2,1)S(1)}, u32[]{:S(2)}, u32[]{:S(2)}) collective-permute-start(bf16[96,4096]{1,0:T(8,128)(2,1)S(1)} %get-tuple-element.15), channel_id=1, source_target_pairs={{0,12},{4,0},{8,4},{12,8},{1,13},{5,1},{9,5},{13,9},{2,14},{6,2},{... | collective-permute-start | bytes 2359304 | tf_op jit(solution)/shard_map/ppermute | solution.py:59
  152.2 3.8 %collective-permute-start.10 = (f32[16,16,512]{2,1,0:T(8,128)S(1)}, f32[16,16,512]{2,1,0:T(8,128)S(1)}, u32[]{:S(2)}, u32[]{:S(2)}) collective-permute-start(f32[16,16,512]{2,1,0:T(8,128)S(1)} %select_bitcast_fusion), channel_id=1, source_target_pairs={{0,64},{64,0},{1,65},{65,1},{2,66},{66,2},{3,67},{67,3},{4,68},{68... | collective-permute-start | bytes 1572872 | tf_op jit(solution)/shard_map/ppermute | solution.py:72
Sparse Core Ops, SparseCore 0:
  58.3 54.6 all-gather.1

commit v3 on v1

v3 whole, which is shorter than its diff:
```python
import functools

import jax
import jax.numpy as jnp
from jax import lax
from jax.experimental import pallas as pl
from jax.experimental.pallas import tpu as pltpu
from jax.sharding import Mesh, PartitionSpec as P

BLK = 128
KB = 512
INTERPRET = False
BF16, F32 = jnp.bfloat16, jnp.float32
PARAMS = dict(vmem_limit_bytes=48 * 1024 * 1024)


def sizes():
    return tuple(lax.axis_size(a) for a in ("x", "core", "zlo", "y", "zhi"))


def col_index():
    return lax.axis_index("zlo") * lax.axis_size("y") + lax.axis_index("y")


def mask_kernel(mask_ref, adj_ref, out_ref):
    nx, nk, nz, ny, nl = sizes()
    nc = nz * ny
    row = col_index() * nx + lax.axis_index("x")
    for c in range(nc):
        for x in range(nx):
            keep = mask_ref[row, c * nx + x].astype(F32).astype(BF16)
            lo = (c * nx + x) * BLK
            out_ref[x * nc + c] = adj_ref[0, :, lo : lo + BLK] * keep


def halves_kernel(out_ref, kept_ref, given_ref):
    n = out_ref.shape[1]
    flip = lax.axis_index("core") == 1
    low = lax.broadcasted_iota(jnp.int32, (n, BLK), 1) < n
    for p in range(out_ref.shape[0] // 2):
        a = out_ref[2 * p].astype(F32)
        b = out_ref[2 * p + 1].astype(F32)
        first = jnp.where(low, a, pltpu.roll(b, n, 1)).astype(BF16)
        second = jnp.where(low, pltpu.roll(a, n, 1), b).astype(BF16)
        cols = slice(p * BLK, (p + 1) * BLK)
        kept_ref[:, cols] = jnp.where(flip, second, first)
        given_ref[:, cols] = jnp.where(flip, first, second)


def form_kernel(recv_ref, kept_ref, other_ref, block_ref, shard_ref, sum_ref, acc_ref):
    nx, nk, nz, ny, nl = sizes()
    nc = nz * ny
    n = kept_ref.shape[0]
    part = n // nl
    step = pl.program_id(0)
    core = lax.axis_index("core")
    c_id = col_index()

    def tile(p):
        flipped = recv_ref[pl.ds(2 * p, 2)].reshape(BLK, BLK).astype(F32).T
        cols = pl.ds(pl.multiple_of(p * BLK, BLK), BLK)
        kept = kept_ref[:, cols].astype(F32)
        other = other_ref[:, cols].astype(F32)
        direct = jnp.concatenate(
            [jnp.where(core == 0, kept, other), jnp.where(core == 0, other, kept)], axis=0
        )
        return direct + flipped, cols

    acc = jnp.zeros((BLK, BLK), F32)
    own_p = jnp.where(step == lax.axis_index("x"), c_id // 2, -1)
    r = lax.broadcasted_iota(jnp.int32, (BLK, BLK), 0)
    k = lax.broadcasted_iota(jnp.int32, (BLK, BLK), 1)
    shift = (c_id % 2 - core) * n
    diagonal = jnp.where((r // n == core) & (k == r + shift), 1.0, 0.0)
    for p in range(nc // 2):
        value, cols = tile(p)
        value = value + jnp.where(own_p == p, diagonal, 0.0)
        rounded = value.astype(BF16)
        block_ref[:, p * BLK : (p + 1) * BLK] = rounded
        acc = acc + rounded.astype(F32)

    @pl.when(step == 0)
    def _():
        acc_ref[...] = acc

    @pl.when(step > 0)
    def _():
        acc_ref[...] += acc

    z_id = lax.axis_index("zhi") * nz + lax.axis_index("zlo")
    for i, s in enumerate(z_steps(nz)):
        layer = (z_id + s + nz * nl) % (nz * nl) // nz
        for half in range(nk):
            rows = pl.ds(pl.multiple_of(half * n + layer * part, part), part)
            shard_ref[i, half * part : (half + 1) * part, :] = block_ref[rows, :]

    @pl.when(step == pl.num_programs(0) - 1)
    def _():
        sum_ref[...] = jnp.sum(acc_ref[...].T, axis=0, keepdims=True)


def z_steps(nz):
    return [s if s <= nz // 2 else s - nz for s in range(nz)]


def product_kernel(own_ref, near_ref, right_ref, degree_ref, mine_ref, theirs_ref, left, acc):
    nx, nk, nz, ny, nl = sizes()
    part = own_ref.shape[1] // nk
    rows = nk * part
    for y in range(ny):
        base = y * nz * rows
        left[base : base + rows, :] = own_ref[y]
        left[base + rows : base + nz * rows, :] = near_ref[y]
    right = (right_ref[...].astype(F32) * (1.0 / degree_ref[...])).astype(BF16)
    value = lax.dot_general(
        left[...], right, (((1,), (1,)), ((), ())), preferred_element_type=F32
    )
    value = value.reshape(acc.shape)

    @pl.when(pl.program_id(0) == 0)
    def _():
        acc[...] = value

    @pl.when(pl.program_id(0) > 0)
    def _():
        acc[...] += value

    @pl.when(pl.program_id(0) == pl.num_programs(0) - 1)
    def _():
        core = lax.axis_index("core")
        for z in range(nz):
            step = (lax.axis_index("zlo") - z + nz) % nz
            for y in range(ny):
                spot = (y * nz + step) * nk
                mine_ref[z * ny + y] = acc[spot + core]
                theirs_ref[z * ny + y] = acc[spot + 1 - core]


def on_device(adjacency, block_mask, prune_mask):
    rows_dev = adjacency.shape[1]
    node_count = adjacency.shape[2]
    nx, nk, nz, ny, nl = sizes()
    nc = nz * ny
    x_id, k_id = lax.axis_index("x"), lax.axis_index("core")
    c_id = col_index()
    part = rows_dev // nl
    half = node_count // nk
    shape = jax.ShapeDtypeStruct
    smem = pl.BlockSpec(memory_space=pltpu.SMEM)
    call = functools.partial(
        pl.pallas_call, compiler_params=pltpu.CompilerParams(**PARAMS), interpret=INTERPRET
    )
    outgoing = call(
        mask_kernel,
        out_shape=shape((nx * nc, rows_dev, BLK), BF16),
        in_specs=[smem, pl.BlockSpec(memory_space=pltpu.VMEM)],
    )(block_mask, adjacency)
    received = lax.all_to_all(outgoing, ("x", "zlo", "y"), split_axis=0, concat_axis=0, tiled=True)
    kept, given = call(halves_kernel, out_shape=[shape((rows_dev, half), BF16)] * 2)(outgoing)
    other = lax.ppermute(given, "core", [(0, 1), (1, 0)])
    width = half // nx
    block, shards, row_sum = call(
        form_kernel,
        grid=(nx,),
        in_specs=[
            pl.BlockSpec((nc, rows_dev, BLK), lambda i: (i, 0, 0)),
            pl.BlockSpec((rows_dev, width), lambda i: (0, i)),
            pl.BlockSpec((rows_dev, width), lambda i: (0, i)),
        ],
        out_specs=[
            pl.BlockSpec((BLK, width), lambda i: (0, i)),
            pl.BlockSpec((nz, nk * part, width), lambda i: (0, 0, i)),
            pl.BlockSpec((1, BLK), lambda i: (0, 0)),
        ],
        out_shape=[
            shape((BLK, half), BF16),
            shape((nz, nk * part, half), BF16),
            shape((1, BLK), F32),
        ],
        scratch_shapes=[pltpu.VMEM((BLK, BLK), F32)],
    )(received, kept, other)

    def z_pairs(step):
        spots = [(z, (z + step) % (nz * nl)) for z in range(nz * nl)]
        return [(a % nz * nl + a // nz, b % nz * nl + b // nz) for a, b in spots]

    def spread(piece, axes, count):
        wide = jnp.broadcast_to(piece[None], (count,) + piece.shape)
        return lax.all_to_all(wide, axes, split_axis=0, concat_axis=0, tiled=True)

    near = [
        lax.ppermute(shards[i], ("zlo", "zhi"), z_pairs(s))
        for i, s in enumerate(z_steps(nz))
        if i > 0
    ]
    own_y = spread(shards[0], "y", ny)
    near_y = spread(jnp.concatenate(near, axis=0), "y", ny)
    right = lax.all_gather(block, "x", axis=0, tiled=True)
    degree_chip = lax.psum(row_sum, "core").reshape(nk, rows_dev)
    degree_own = jnp.where(k_id == 0, degree_chip[0], degree_chip[1])
    degree = spread(degree_own, ("x", "zlo", "y"), nx * nc).reshape(1, half)
    tile_cols = nx * BLK
    mine, theirs = call(
        product_kernel,
        grid=(half // KB,),
        in_specs=[
            pl.BlockSpec((ny, nk * part, KB), lambda i: (0, 0, i)),
            pl.BlockSpec((ny, (nz - 1) * nk * part, KB), lambda i: (0, 0, i)),
            pl.BlockSpec((tile_cols, KB), lambda i: (0, i)),
            pl.BlockSpec((1, KB), lambda i: (0, i)),
        ],
        out_specs=[pl.BlockSpec((nc, part, tile_cols), lambda i: (0, 0, 0))] * 2,
        out_shape=[shape((nc, part, tile_cols), F32)] * 2,
        scratch_shapes=[
            pltpu.VMEM((nc * nk * part, KB), BF16),
            pltpu.VMEM((nc * nk, part, tile_cols), F32),
        ],
    )(own_y, near_y, right, degree)
    summed = mine + lax.ppermute(theirs, "core", [(0, 1), (1, 0)])
    prune = prune_mask.reshape(nc, nx, nc, nx)
    prune = lax.dynamic_index_in_dim(prune, x_id, 1, keepdims=False)
    prune = lax.dynamic_index_in_dim(prune, c_id, 1, keepdims=False)
    prune = jnp.repeat(prune.astype(F32), BLK, axis=1)
    pruned = summed * summed * prune[:, None, :]
    mass = lax.psum(jnp.sum(pruned, axis=(0, 1)), "core")
    mass = jnp.sum(spread(mass.reshape(-1, BLK), ("x", "zhi"), nx * nl), axis=0).reshape(-1)
    return pruned * (node_count / mass)[None, None, :]


def solution(mesh):
    rows, cols, layers = mesh.devices.shape
    devices = mesh.devices.reshape(rows // 2, 2, cols // 4, 4, layers)
    split = Mesh(devices, ("x", "core", "zlo", "y", "zhi"))
    in_specs = (P(("zlo", "y"), ("x", "core"), None), P(), P())
    out_specs = P(None, ("x", "core", "zhi"), ("zlo", "y"))
    return jax.shard_map(
        on_device, mesh=split, in_specs=in_specs, out_specs=out_specs, check_vma=False
    )
```

time: 198 us -> 195 us (0.985)
  the two profiles are of different devices: /device:TPU:8 before, /device:TPU:32 now
where the time goes in v3:
time: 195 us; the launch traced here: 194 us
  waiting for transfers between devices  77.8 us (40%)
  starting transfers between devices  45.4 us (23%)
  blocking collectives  30 us (15%)
  Pallas kernels  14.8 us (8%)
  between operations  13.6 us (7%)
  local copies, waits for them, and re-layouts  9.05 us (5%)
  other arithmetic  2.97 us (2%)
    all_to_all x3, waiting for transfers between devices, spread(): return lax.all_to_all(wide, axes, split_axis=0, concat_axis=0, tiled=True)  42.7 us
    all_to_all x1, blocking collectives, spread(): return lax.all_to_all(wide, axes, split_axis=0, concat_axis=0, tiled=True)  25.1 us
    all_to_all x1, waiting for transfers between devices, on_device(): lax.all_to_all(outgoing, ('x', 'zlo', 'y'), split_axis=0, concat_axis=0,...  20.6 us
    all_to_all x3, starting transfers between devices, spread(): return lax.all_to_all(wide, axes, split_axis=0, concat_axis=0, tiled=True)  16.1 us
    ppermute x3, starting transfers between devices, on_device(): lax.ppermute(shards[i], ('zlo', 'zhi'), z_pairs(s))  13.7 us
    all_to_all x1, starting transfers between devices, on_device(): lax.all_to_all(outgoing, ('x', 'zlo', 'y'), split_axis=0, concat_axis=0,...  11.7 us
    ppermute x3, waiting for transfers between devices, on_device(): lax.ppermute(shards[i], ('zlo', 'zhi'), z_pairs(s))  11.1 us
    pallas_call x1, Pallas kernels, on_device(): call(product_kernel, grid=(half // KB,), in_specs=[pl.BlockSpec((ny, nk *...  8.27 us
  transfers between devices with their start and end apart: 10, of which 6 were waited for; matrix products, arithmetic and copies ran while one was open for 3% of the time, Pallas kernels for 1%

profile of v3, /device:TPU:32, one launch (start us, length us, event | category | flops | bytes accessed | tf_op | source)
XLA Modules:
  0.0 193.6 jit_solution(17174515487547773102)
XLA Ops:
  6.5 1.2 copy-done.4
  7.8 0.8 copy-done.5
  8.5 2.3 %shard_map.37.out_ref = bf16[64,64,128]{2,1,0:T(8,128)(2,1)} custom-call(s32[64,64]{1,0:T(8,128)S(1)} %copy-done.5, bf16[1,64,8192]{2,1,0:T(8,128)(2,1)S(1)} %copy-done.4), custom_call_target="tpu_custom_call" | custom-call | tf_op jit(solution)/shard_map/pallas_call | solution.py:153
  10.8 11.7 %all-to-all-start = ((bf16[64,64,128]{2,1,0:T(8,128)(2,1)}), bf16[64,64,128]{2,1,0:T(8,128)(2,1)S(1)}, u32[]{:S(2)}, u32[]{:S(2)}) async-start(bf16[64,64,128]{2,1,0:T(8,128)(2,1)} %shard_map.37.out_ref), calls=%async_computation | async-start | bytes 2097152 | tf_op jit(solution)/shard_map/all_to_all | solution.py:158
  22.5 1.7 shard_map.38
  24.2 1.9 collective-permute-start
  26.2 1.9 collective-permute-done.other_ref
  28.0 20.6 %all-to-all-done.recv_ref = bf16[64,64,128]{2,1,0:T(8,128)(2,1)S(1)} async-done(((bf16[64,64,128]{2,1,0:T(8,128)(2,1)}), bf16[64,64,128]{2,1,0:T(8,128)(2,1)S(1)}, u32[]{:S(2)}, u32[]{:S(2)}) %all-to-all-start) | async-done | bytes 1048608 | tf_op jit(solution)/shard_map/all_to_all | solution.py:158
  48.7 2.5 %shard_map.39 = (bf16[128,4096]{1,0:T(8,128)(2,1)}, bf16[4,32,4096]{2,1,0:T(8,128)(2,1)S(1)}, f32[1,128]{1,0:T(1,128)S(1)}) custom-call(bf16[64,64,128]{2,1,0:T(8,128)(2,1)S(1)} %all-to-all-done.recv_ref, bf16[64,4096]{1,0:T(8,128)(2,1)S(1)} %get-tuple-element.12.kept_ref, bf16[64,4096]{1,0:T(8,128)(2,1)S(1)} %collective-permute-done.other_ref), custom_call_target="tpu_custom_call" | custom-call | tf_op jit(solution)/shard_map/pallas_call | solution.py:162
  51.2 2.5 %psum.14 = f32[1,128]{1,0:T(1,128)S(1)} all-reduce(f32[1,128]{1,0:T(1,128)S(1)} %get-tuple-element.16), channel_id=1, replica_groups=mesh['x'=4,'core'=2,'zlo'=4,'y'=4,'zhi'=4] {'core'}, use_global_device_ids=true, to_apply=%region_0.0 | all-reduce | flops 128 | bytes 1024 | tf_op jit(solution)/shard_map/psum | solution.py:199
  53.8 0.6 broadcast_in_dim.33
  54.4 8.1 %all-to-all-start.3 = ((f32[64,1,64]{2,1,0:T(1,128)}), f32[64,1,64]{2,1,0:T(1,128)S(1)}, u32[]{:S(2)}, u32[]{:S(2)}) async-start(f32[64,1,64]{2,1,0:T(1,128)} %broadcast_in_dim.33), calls=%async_computation.3 | async-start | bytes 65536 | tf_op jit(solution)/shard_map/all_to_all | solution.py:189
  62.6 8.7 %all-to-all-done.3 = f32[64,1,64]{2,1,0:T(1,128)S(1)} async-done(((f32[64,1,64]{2,1,0:T(1,128)}), f32[64,1,64]{2,1,0:T(1,128)S(1)}, u32[]{:S(2)}, u32[]{:S(2)}) %all-to-all-start.3) | async-done | bytes 16416 | tf_op jit(solution)/shard_map/all_to_all | solution.py:189
  71.3 1.1 broadcast_in_dim.15
  72.4 3.5 %all-to-all-start.1 = ((bf16[4,32,4096]{2,1,0:T(8,128)(2,1)}), bf16[4,32,4096]{2,1,0:T(8,128)(2,1)S(1)}, u32[]{:S(2)}, u32[]{:S(2)}) async-start(bf16[4,32,4096]{2,1,0:T(8,128)(2,1)} %broadcast_in_dim.15), calls=%async_computation.1 | async-start | bytes 2097152 | tf_op jit(solution)/shard_map/all_to_all | solution.py:189
  75.9 2.5 %collective-permute-start.1 = (bf16[32,4096]{1,0:T(8,128)(2,1)S(1)}, bf16[32,4096]{1,0:T(8,128)(2,1)S(1)}, u32[]{:S(2)}, u32[]{:S(2)}) collective-permute-start(bf16[32,4096]{1,0:T(8,128)(2,1)S(1)} %get-tuple-element.19), channel_id=1, source_target_pairs={{0,16},{16,32},{32,48},{48,1},{1,17},{17,33},{33,49},{49,2},{2,18}... | collective-permute-start | bytes 786440 | tf_op jit(solution)/shard_map/ppermute | solution.py:192
  78.4 9.3 %collective-permute-start.2 = (bf16[32,4096]{1,0:T(8,128)(2,1)S(1)}, bf16[32,4096]{1,0:T(8,128)(2,1)S(1)}, u32[]{:S(2)}, u32[]{:S(2)}) collective-permute-start(bf16[32,4096]{1,0:T(8,128)(2,1)S(1)} %get-tuple-element.21), channel_id=1, source_target_pairs={{0,32},{16,48},{32,1},{48,17},{1,33},{17,49},{33,2},{49,18},{2,34}... | collective-permute-start | bytes 786440 | tf_op jit(solution)/shard_map/ppermute | solution.py:192
  87.6 1.9 collective-permute-start.3
  89.6 11.1 %collective-permute-done.2 = bf16[32,4096]{1,0:T(8,128)(2,1)S(1)} collective-permute-done((bf16[32,4096]{1,0:T(8,128)(2,1)S(1)}, bf16[32,4096]{1,0:T(8,128)(2,1)S(1)}, u32[]{:S(2)}, u32[]{:S(2)}) %collective-permute-start.2) | collective-permute-done | bytes 262176 | tf_op jit(solution)/shard_map/ppermute | solution.py:192
  100.8 2.1 %broadcast_in_dim.32 = bf16[4,96,4096]{2,1,0:T(8,128)(2,1)} broadcast(bf16[96,4096]{1,0:T(8,128)(2,1)S(1)} %pad_maximum_fusion), dimensions={1,2} | broadcast | bytes 3932160 | tf_op jit(solution)/shard_map/broadcast_in_dim | solution.py:188
  102.9 4.5 %all-to-all-start.2 = ((bf16[4,96,4096]{2,1,0:T(8,128)(2,1)}), bf16[4,96,4096]{2,1,0:T(8,128)(2,1)S(1)}, u32[]{:S(2)}, u32[]{:S(2)}) async-start(bf16[4,96,4096]{2,1,0:T(8,128)(2,1)} %broadcast_in_dim.32), calls=%async_computation.2 | async-start | bytes 6291456 | tf_op jit(solution)/shard_map/all_to_all | solution.py:189
  107.8 0.7 reduce.3
  108.7 34.0 %all-to-all-done.2.near_ref = bf16[4,96,4096]{2,1,0:T(8,128)(2,1)S(1)} async-done(((bf16[4,96,4096]{2,1,0:T(8,128)(2,1)}), bf16[4,96,4096]{2,1,0:T(8,128)(2,1)S(1)}, u32[]{:S(2)}, u32[]{:S(2)}) %all-to-all-start.2) | async-done | bytes 3145760 | tf_op jit(solution)/shard_map/all_to_all | solution.py:189
  142.6 1.2 copy-done.1
  143.9 8.3 %shard_map.40 = (f32[16,16,512]{2,1,0:T(8,128)S(1)}, f32[16,16,512]{2,1,0:T(8,128)}) custom-call(bf16[4,32,4096]{2,1,0:T(8,128)(2,1)S(1)} %copy-done.1, bf16[4,96,4096]{2,1,0:T(8,128)(2,1)S(1)} %all-to-all-done.2.near_ref, bf16[512,4096]{1,0:T(8,128)(2,1)} %all-gather.2.cloned.1.call-done.right_ref, f32[1,4096]{1,0:T(1,128)S(1)} %reshape.32.degree_ref), custom_call_target="tpu_custom_call" | custom-call | tf_op jit(solution)/shard_map/pallas_call | solution.py:203
  152.1 0.8 copy-done.2
  152.9 2.0 %collective-permute-start.4 = (f32[16,16,512]{2,1,0:T(8,128)}, f32[16,16,512]{2,1,0:T(8,128)S(1)}, u32[]{:S(2)}, u32[]{:S(2)}) collective-permute-start(f32[16,16,512]{2,1,0:T(8,128)} %get-tuple-element.18), channel_id=1, source_target_pairs={{0,64},{64,0},{1,65},{65,1},{2,66},{66,2},{3,67},{67,3},{4,68},{68... | collective-permute-start | bytes 1572872 | tf_op jit(solution)/shard_map/ppermute | solution.py:219
  155.6 1.5 collective-permute-done.4
  157.1 1.1 fusion
  158.2 2.5 %psum.15 = f32[4,128]{1,0:T(4,128)S(1)} all-reduce(f32[4,128]{1,0:T(4,128)S(1)} %bitcast.22), channel_id=1, replica_groups=mesh['x'=4,'core'=2,'zlo'=4,'y'=4,'zhi'=4] {'core'}, use_global_device_ids=true, to_apply=%region_2.3 | all-reduce | flops 512 | bytes 4096 | tf_op jit(solution)/shard_map/psum | solution.py:225
  160.7 25.1 %all_to_all.26 = f32[16,4,128]{2,1,0:T(4,128)S(1)} all-to-all(f32[16,4,128]{2,1,0:T(4,128)S(1)} %broadcast_in_dim.36), channel_id=1, replica_groups=mesh['x'=4,'core'=2,'zlo'=4,'y'=4,'zhi'=4] {'x','zhi'}, dimensions={0} | all-to-all | bytes 65536 | tf_op jit(solution)/shard_map/all_to_all | solution.py:189
  185.8 0.9 broadcast_multiply_fusion
  (31 shorter events, 1.5 us)
Async XLA Ops:
  6.5 1.2 copy-start.4
  7.8 0.8 copy-start.5
  10.8 37.9 %all-to-all-start = ((bf16[64,64,128]{2,1,0:T(8,128)(2,1)}), bf16[64,64,128]{2,1,0:T(8,128)(2,1)S(1)}, u32[]{:S(2)}, u32[]{:S(2)}) async-start(bf16[64,64,128]{2,1,0:T(8,128)(2,1)} %shard_map.37.out_ref), calls=%async_computation | async-start | bytes 2097152 | tf_op jit(solution)/shard_map/all_to_all | solution.py:158
  22.5 120.2 %all-gather.2.cloned.1.call-start = ((), (), s32[]{:S(2)}) async-start(), calls=%async_computation.5 | async-start | bytes 5242880 | tf_op jit(solution)/shard_map/all_gather | solution.py:198
  24.2 3.8 %collective-permute-start = (bf16[64,4096]{1,0:T(8,128)(2,1)S(1)}, bf16[64,4096]{1,0:T(8,128)(2,1)S(1)}, u32[]{:S(2)}, u32[]{:S(2)}) collective-permute-start(bf16[64,4096]{1,0:T(8,128)(2,1)S(1)} %get-tuple-element.13), channel_id=1, source_target_pairs={{0,64},{64,0},{1,65},{65,1},{2,66},{66,2},{3,67},{67,3},{4,68},{68... | collective-permute-start | bytes 1572872 | tf_op jit(solution)/shard_map/ppermute | solution.py:160
  54.4 16.9 %all-to-all-start.3 = ((f32[64,1,64]{2,1,0:T(1,128)}), f32[64,1,64]{2,1,0:T(1,128)S(1)}, u32[]{:S(2)}, u32[]{:S(2)}) async-start(f32[64,1,64]{2,1,0:T(1,128)} %broadcast_in_dim.33), calls=%async_computation.3 | async-start | bytes 65536 | tf_op jit(solution)/shard_map/all_to_all | solution.py:189
  72.4 28.4 %all-to-all-start.1 = ((bf16[4,32,4096]{2,1,0:T(8,128)(2,1)}), bf16[4,32,4096]{2,1,0:T(8,128)(2,1)S(1)}, u32[]{:S(2)}, u32[]{:S(2)}) async-start(bf16[4,32,4096]{2,1,0:T(8,128)(2,1)} %broadcast_in_dim.15), calls=%async_computation.1 | async-start | bytes 2097152 | tf_op jit(solution)/shard_map/all_to_all | solution.py:189
  75.9 13.7 %collective-permute-start.1 = (bf16[32,4096]{1,0:T(8,128)(2,1)S(1)}, bf16[32,4096]{1,0:T(8,128)(2,1)S(1)}, u32[]{:S(2)}, u32[]{:S(2)}) collective-permute-start(bf16[32,4096]{1,0:T(8,128)(2,1)S(1)} %get-tuple-element.19), channel_id=1, source_target_pairs={{0,16},{16,32},{32,48},{48,1},{1,17},{17,33},{33,49},{49,2},{2,18}... | collective-permute-start | bytes 786440 | tf_op jit(solution)/shard_map/ppermute | solution.py:192
  78.4 22.3 %collective-permute-start.2 = (bf16[32,4096]{1,0:T(8,128)(2,1)S(1)}, bf16[32,4096]{1,0:T(8,128)(2,1)S(1)}, u32[]{:S(2)}, u32[]{:S(2)}) collective-permute-start(bf16[32,4096]{1,0:T(8,128)(2,1)S(1)} %get-tuple-element.21), channel_id=1, source_target_pairs={{0,32},{16,48},{32,1},{48,17},{1,33},{17,49},{33,2},{49,18},{2,34}... | collective-permute-start | bytes 786440 | tf_op jit(solution)/shard_map/ppermute | solution.py:192
  87.6 13.1 %collective-permute-start.3 = (bf16[32,4096]{1,0:T(8,128)(2,1)S(1)}, bf16[32,4096]{1,0:T(8,128)(2,1)S(1)}, u32[]{:S(2)}, u32[]{:S(2)}) collective-permute-start(bf16[32,4096]{1,0:T(8,128)(2,1)S(1)} %get-tuple-element.20), channel_id=1, source_target_pairs={{0,51},{16,0},{32,16},{48,32},{1,48},{17,1},{33,17},{49,33},{2,49}... | collective-permute-start | bytes 786440 | tf_op jit(solution)/shard_map/ppermute | solution.py:192
  100.8 2.1 %copy-start = (bf16[4,32,4096]{2,1,0:T(8,128)(2,1)}, bf16[4,32,4096]{2,1,0:T(8,128)(2,1)S(1)}, u32[]{:S(2)}) copy-start(bf16[4,32,4096]{2,1,0:T(8,128)(2,1)S(1)} %all-to-all-done.1.own_ref) | copy-start | bytes 3145732
  102.9 39.8 %all-to-all-start.2 = ((bf16[4,96,4096]{2,1,0:T(8,128)(2,1)}), bf16[4,96,4096]{2,1,0:T(8,128)(2,1)S(1)}, u32[]{:S(2)}, u32[]{:S(2)}) async-start(bf16[4,96,4096]{2,1,0:T(8,128)(2,1)} %broadcast_in_dim.32), calls=%async_computation.2 | async-start | bytes 6291456 | tf_op jit(solution)/shard_map/all_to_all | solution.py:189
  108.6 46.4 %copy-start.6 = (s32[64,64]{1,0:T(8,128)S(1)}, s32[64,64]{1,0:T(8,128)}, u32[]{:S(2)}) copy-start(s32[64,64]{1,0:T(8,128)} %param.5) | copy-start | bytes 49156
  142.6 1.2 copy-start.1
  152.1 0.8 copy-start.2
  152.9 32.9 %copy-start.3 = (f32[16,16,512]{2,1,0:T(8,128)S(1)}, f32[16,16,512]{2,1,0:T(8,128)}, u32[]{:S(2)}) copy-start(f32[16,16,512]{2,1,0:T(8,128)} %copy-done.2) | copy-start | bytes 1572868
  152.9 4.1 %collective-permute-start.4 = (f32[16,16,512]{2,1,0:T(8,128)}, f32[16,16,512]{2,1,0:T(8,128)S(1)}, u32[]{:S(2)}, u32[]{:S(2)}) collective-permute-start(f32[16,16,512]{2,1,0:T(8,128)} %get-tuple-element.18), channel_id=1, source_target_pairs={{0,64},{64,0},{1,65},{65,1},{2,66},{66,2},{3,67},{67,3},{4,68},{68... | collective-permute-start | bytes 1572872 | tf_op jit(solution)/shard_map/ppermute | solution.py:219
Sparse Core Ops, SparseCore 0:
  51.4 56.5 all-gather.1

commit v4 on v1

v4 whole, which is shorter than its diff:
```python
import functools

import jax
import jax.numpy as jnp
from jax import lax
from jax.experimental import pallas as pl
from jax.experimental.pallas import tpu as pltpu
from jax.sharding import Mesh, PartitionSpec as P

BLK = 128
KB = 512
INTERPRET = False
BF16, F32 = jnp.bfloat16, jnp.float32
PARAMS = dict(vmem_limit_bytes=48 * 1024 * 1024)
AXES = ("x", "core", "zlo", "y1", "y0", "zhi")
SWAP = [(0, 1), (1, 0)]


def where_am_i():
    return tuple(lax.axis_index(a) for a in AXES)


def z_steps(nz):
    return [s if s <= nz // 2 else s - nz for s in range(nz)]


def mask_kernel(mask_ref, adj_ref, out_ref):
    x_id, _, z_id, y1, y0, _ = where_am_i()
    nx, nz = lax.axis_size("x"), lax.axis_size("zlo")
    row = (z_id * 4 + y1 * 2 + y0) * nx + x_id
    for x in range(nx):
        for z in range(nz):
            base = (x * nz + z) * 2
            for y in range(4):
                block = (z * 4 + y) * nx + x
                keep = mask_ref[row, block].astype(F32).astype(BF16)
                low, high = (y, 0) if y < 2 else (3 - y, 1)
                spot = base + jnp.where(y1 == 0, low, 1 - low)
                out_ref[spot, :, high * BLK : (high + 1) * BLK] = (
                    adj_ref[0, :, block * BLK : (block + 1) * BLK] * keep
                )


def pieces_kernel(out_ref, piece_ref):
    _, core, _, y1, _, _ = where_am_i()
    n = out_ref.shape[1]
    low_lanes = lax.broadcasted_iota(jnp.int32, (n, BLK), 1) < n
    for p in range(out_ref.shape[0] // 2):
        cols = slice(p * BLK, (p + 1) * BLK)
        outer = out_ref[2 * p + y1].astype(F32)
        inner = out_ref[2 * p + 1 - y1].astype(F32)
        tiles = [outer[:, :BLK], inner[:, :BLK], inner[:, BLK:], outer[:, BLK:]]
        for half in range(2):
            a, b = tiles[2 * half], tiles[2 * half + 1]
            first = jnp.where(low_lanes, a, pltpu.roll(b, n, 1)).astype(BF16)
            second = jnp.where(low_lanes, pltpu.roll(a, n, 1), b).astype(BF16)
            i = jnp.where(y1 == half, 0, 1)
            piece_ref[2 * i + core, :, cols] = first
            piece_ref[2 * i + 1 - core, :, cols] = second


def form_kernel(recv_ref, d00, d01, d10, d11, block_ref, shard_ref, sum_ref, flip_ref, acc_ref):
    x_id, core, z_id, y1, y0, l_id = where_am_i()
    nz, nl = lax.axis_size("zlo"), lax.axis_size("zhi")
    n = d00.shape[0]
    part = n // nl
    step = pl.program_id(0)
    own_p = jnp.where(step == x_id, z_id, -1)
    r = lax.broadcasted_iota(jnp.int32, (n, BLK), 0)
    k = lax.broadcasted_iota(jnp.int32, (n, BLK), 1)
    diagonal = jnp.where(k == r + y0 * n, 1.0, 0.0)

    @pl.when(step == 0)
    def _():
        acc_ref[...] = jnp.zeros_like(acc_ref)

    for p in range(nz):
        cols = slice(p * BLK, (p + 1) * BLK)
        got = recv_ref[2 * p : 2 * p + 2].reshape(BLK, 2 * BLK).astype(F32)
        flip_ref[...] = got.T.reshape(flip_ref.shape)
        for i, direct in enumerate((d00, d01, d10, d11)):
            b, c = i // 2, i % 2
            spot = jnp.where(y1 == b, 0, 2) + jnp.where(core == c, 0, 1)
            value = direct[:, cols].astype(F32) + flip_ref[spot]
            if i == 0:
                value = value + jnp.where(own_p == p, diagonal, 0.0)
            rounded = value.astype(BF16)
            block_ref[spot, :, cols] = rounded
            acc_ref[spot] += rounded.astype(F32)

    z_pos = l_id * nz + z_id
    for i, s in enumerate(z_steps(nz)):
        layer = (z_pos + s + nz * nl) % (nz * nl) // nz
        rows = pl.ds(pl.multiple_of(layer * part, part), part)
        for group in range(4):
            shard_ref[i, group * part : (group + 1) * part, :] = block_ref[group, rows, :]

    @pl.when(step == pl.num_programs(0) - 1)
    def _():
        acc = acc_ref[...].reshape(4 * n, BLK)
        sum_ref[...] = jnp.sum(acc.T, axis=0, keepdims=True)


def product_kernel(
    own_ref, far_ref, right_ref, degree_ref, m_own, m_oth, t_own, t_oth, left, right, acc
):
    _, core, z_id, y1, y0, _ = where_am_i()
    nx, nz, nl = lax.axis_size("x"), lax.axis_size("zlo"), lax.axis_size("zhi")
    rows = own_ref.shape[0]
    left[:rows] = own_ref[...]
    left[rows:] = far_ref[...]
    inverse = 1.0 / degree_ref[...]
    for x in range(nx):
        for b in range(2):
            spot = jnp.where(y1 == b, 0, nx) + x
            scaled = right_ref[2 * x + b].astype(F32) * inverse
            right[spot] = scaled.astype(BF16)
    value = lax.dot_general(
        left[...],
        right[...].reshape(-1, right.shape[2]),
        (((1,), (1,)), ((), ())),
        preferred_element_type=F32,
    )
    value = value.reshape(acc.shape)

    @pl.when(pl.program_id(0) == 0)
    def _():
        acc[...] = value

    @pl.when(pl.program_id(0) > 0)
    def _():
        acc[...] += value

    @pl.when(pl.program_id(0) == pl.num_programs(0) - 1)
    def _():
        width = nx * BLK
        for z in range(nz):
            step = (z_id - z + nz) % nz
            for y in range(4):
                low, b = (y, 0) if y < 2 else (3 - y, 1)
                far = jnp.where((y0 + y1) % 2 == low, 0, 1)
                spot = ((far * nz + step) * 2 + b) * 2
                m_own[z * 4 + y] = acc[spot + core, :, :width]
                m_oth[z * 4 + y] = acc[spot + core, :, width:]
                t_own[z * 4 + y] = acc[spot + 1 - core, :, :width]
                t_oth[z * 4 + y] = acc[spot + 1 - core, :, width:]


def on_device(adjacency, block_mask, prune_mask):
    rows_dev = adjacency.shape[1]
    node_count = adjacency.shape[2]
    nx, nk, nz, _, _, nl = (lax.axis_size(a) for a in AXES)
    nc = nz * 4
    x_id, k_id, z_id, y1, y0, _ = where_am_i()
    c_id = z_id * 4 + y1 * 2 + y0
    part = rows_dev // nl
    inner = node_count // 4
    width = inner // nx
    shape = jax.ShapeDtypeStruct
    vmem = pl.BlockSpec(memory_space=pltpu.VMEM)
    call = functools.partial(
        pl.pallas_call, compiler_params=pltpu.CompilerParams(**PARAMS), interpret=INTERPRET
    )
    group = ("x", "zlo", "y0")
    members = nx * nz * 2

    def partner(value):
        return lax.ppermute(value, ("y1", "y0"), [(y, 3 - y) for y in range(4)])

    def other_core(value):
        return lax.ppermute(value, "core", SWAP)

    def spread(piece, axes, count):
        wide = jnp.broadcast_to(piece[None], (count,) + piece.shape)
        return lax.all_to_all(wide, axes, split_axis=0, concat_axis=0, tiled=True)

    outgoing = call(
        mask_kernel,
        out_shape=shape((members, rows_dev, 2 * BLK), BF16),
        in_specs=[pl.BlockSpec(memory_space=pltpu.SMEM), vmem],
        out_specs=vmem,
    )(block_mask, adjacency)
    received = lax.all_to_all(outgoing, group, split_axis=0, concat_axis=0, tiled=True)
    pieces = call(pieces_kernel, out_shape=shape((4, rows_dev, inner), BF16))(outgoing)
    across = [(c * 4 + y, (1 - c) * 4 + 3 - y) for c in range(2) for y in range(4)]
    direct = [
        pieces[0],
        other_core(pieces[1]),
        partner(pieces[2]),
        lax.ppermute(pieces[3], ("core", "y1", "y0"), across),
    ]
    block, shards, row_sum = call(
        form_kernel,
        grid=(nx,),
        in_specs=[pl.BlockSpec((2 * nz, rows_dev, 2 * BLK), lambda i: (i, 0, 0))]
        + [pl.BlockSpec((rows_dev, width), lambda i: (0, i))] * 4,
        out_specs=[
            pl.BlockSpec((4, rows_dev, width), lambda i: (0, 0, i)),
            pl.BlockSpec((nz, 4 * part, width), lambda i: (0, 0, i)),
            pl.BlockSpec((1, 4 * rows_dev), lambda i: (0, 0)),
        ],
        out_shape=[
            shape((4, rows_dev, inner), BF16),
            shape((nz, 4 * part, inner), BF16),
            shape((1, 4 * rows_dev), F32),
        ],
        scratch_shapes=[
            pltpu.VMEM((4, rows_dev, BLK), F32),
            pltpu.VMEM((4, rows_dev, BLK), F32),
        ],
    )(received, *direct)

    def z_pairs(step):
        spots = [(z, (z + step) % (nz * nl)) for z in range(nz * nl)]
        return [(a % nz * nl + a // nz, b % nz * nl + b // nz) for a, b in spots]

    near = [
        lax.ppermute(shards[i], ("zlo", "zhi"), z_pairs(s)) if i else shards[0]
        for i, s in enumerate(z_steps(nz))
    ]
    own_rows = jnp.concatenate(near, axis=0)
    far_rows = lax.ppermute(own_rows, "y0", SWAP)
    right = lax.all_gather(block.reshape(4 * rows_dev, inner), "x", axis=0, tiled=True)
    degree_pair = lax.psum(row_sum, "core")
    degree_pair = (degree_pair + partner(degree_pair)).reshape(4, rows_dev)
    degree_own = lax.dynamic_index_in_dim(degree_pair, y1 * 2 + k_id, 0, keepdims=False)
    degree = spread(degree_own, group, members).reshape(1, inner)
    tile_cols = nx * BLK
    tile = shape((nc, part, tile_cols), F32)
    m_own, m_oth, t_own, t_oth = call(
        product_kernel,
        grid=(inner // KB,),
        in_specs=[
            pl.BlockSpec((nz * 4 * part, KB), lambda i: (0, i)),
            pl.BlockSpec((nz * 4 * part, KB), lambda i: (0, i)),
            pl.BlockSpec((2 * nx, BLK, KB), lambda i: (0, 0, i)),
            pl.BlockSpec((1, KB), lambda i: (0, i)),
        ],
        out_specs=[pl.BlockSpec(tile.shape, lambda i: (0, 0, 0))] * 4,
        out_shape=[tile] * 4,
        scratch_shapes=[
            pltpu.VMEM((2 * nz * 4 * part, KB), BF16),
            pltpu.VMEM((2 * nx, BLK, KB), BF16),
            pltpu.VMEM((2 * nc, part, 2 * tile_cols), F32),
        ],
    )(own_rows, far_rows, right.reshape(2 * nx, BLK, inner), degree)
    sent = (m_oth + other_core(t_oth)).astype(BF16)
    summed = m_own + other_core(t_own) + partner(sent).astype(F32)
    prune = prune_mask.reshape(nc, nx, nc, nx)
    prune = lax.dynamic_index_in_dim(prune, x_id, 1, keepdims=False)
    prune = lax.dynamic_index_in_dim(prune, c_id, 1, keepdims=False)
    prune = jnp.repeat(prune.astype(F32), BLK, axis=1)
    pruned = summed * summed * prune[:, None, :]
    mass = lax.psum(jnp.sum(pruned, axis=(0, 1)), "core")
    mass = jnp.sum(spread(mass.reshape(-1, BLK), ("x", "zhi"), nx * nl), axis=0).reshape(-1)
    return pruned * (node_count / mass)[None, None, :]


def solution(mesh):
    rows, cols, layers = mesh.devices.shape
    devices = mesh.devices.reshape(rows // 2, 2, cols // 4, 2, 2, layers)
    split = Mesh(devices, AXES)
    in_specs = (P(("zlo", "y1", "y0"), ("x", "core"), None), P(), P())
    out_specs = P(None, ("x", "core", "zhi"), ("zlo", "y1", "y0"))
    return jax.shard_map(
        on_device, mesh=split, in_specs=in_specs, out_specs=out_specs, check_vma=False
    )
```

time: 198 us -> 171 us (0.86)
  the two profiles are of different devices: /device:TPU:8 before, /device:TPU:1 now
where the time goes in v4:
time: 171 us; the launch traced here: 170 us
  starting transfers between devices  47.1 us (28%)
  blocking collectives  46.7 us (27%)
  waiting for transfers between devices  42.4 us (25%)
  Pallas kernels  13.7 us (8%)
  between operations  13.6 us (8%)
  local copies, waits for them, and re-layouts  4.21 us (2%)
  other arithmetic  2.06 us (1%)
    all_to_all x2, blocking collectives, spread(): return lax.all_to_all(wide, axes, split_axis=0, concat_axis=0, tiled=True)  38.4 us
    ppermute x3, starting transfers between devices, partner(): return lax.ppermute(value, ('y1', 'y0'), [(y, 3 - y) for y in range(4)])  14.3 us
    ppermute x3, waiting for transfers between devices, on_device(): lax.ppermute(shards[i], ('zlo', 'zhi'), z_pairs(s))  13.1 us
    ppermute x3, waiting for transfers between devices, partner(): return lax.ppermute(value, ('y1', 'y0'), [(y, 3 - y) for y in range(4)])  11.8 us
    ppermute x3, starting transfers between devices, on_device(): lax.ppermute(shards[i], ('zlo', 'zhi'), z_pairs(s))  11.2 us
    all_to_all x1, starting transfers between devices, on_device(): lax.all_to_all(outgoing, group, split_axis=0, concat_axis=0, tiled=True)  10.3 us
    ppermute x3, starting transfers between devices, other_core(): return lax.ppermute(value, 'core', SWAP)  7.36 us
    pallas_call x1, Pallas kernels, on_device(): call(product_kernel, grid=(inner // KB,), in_specs=[pl.BlockSpec((nz * 4...  6.79 us
  transfers between devices with their start and end apart: 13, of which 8 were waited for; matrix products, arithmetic and copies ran while one was open for 1% of the time, Pallas kernels for 1%

profile of v4, /device:TPU:1, one launch (start us, length us, event | category | flops | bytes accessed | tf_op | source)
XLA Modules:
  0.0 169.8 jit_solution(3562571730941401244)
XLA Ops:
  6.5 1.2 copy-done
  7.8 0.8 copy-done.1
  8.5 2.3 %shard_map.37.out_ref = bf16[32,64,256]{2,1,0:T(8,128)(2,1)} custom-call(s32[64,64]{1,0:T(8,128)S(1)} %copy-done.1, bf16[1,64,8192]{2,1,0:T(8,128)(2,1)S(1)} %copy-done), custom_call_target="tpu_custom_call" | custom-call | tf_op jit(solution)/shard_map/pallas_call | solution.py:177
  10.8 10.3 %all-to-all-start = ((bf16[32,64,256]{2,1,0:T(8,128)(2,1)}), bf16[32,64,256]{2,1,0:T(8,128)(2,1)S(1)}, u32[]{:S(2)}, u32[]{:S(2)}) async-start(bf16[32,64,256]{2,1,0:T(8,128)(2,1)} %shard_map.37.out_ref), calls=%async_computation | async-start | bytes 2097152 | tf_op jit(solution)/shard_map/all_to_all | solution.py:183
  21.2 1.7 shard_map.38
  23.0 2.9 %collective-permute-start = (bf16[64,2048]{1,0:T(8,128)(2,1)S(1)}, bf16[64,2048]{1,0:T(8,128)(2,1)S(1)}, u32[]{:S(2)}, u32[]{:S(2)}) collective-permute-start(bf16[64,2048]{1,0:T(8,128)(2,1)S(1)} %get-tuple-element.25), channel_id=1, source_target_pairs={{0,64},{64,0},{1,65},{65,1},{2,66},{66,2},{3,67},{67,3},{4,68},{68... | collective-permute-start | bytes 786440 | tf_op jit(solution)/shard_map/ppermute | solution.py:171
  25.9 4.9 %collective-permute-start.1 = (bf16[64,2048]{1,0:T(8,128)(2,1)S(1)}, bf16[64,2048]{1,0:T(8,128)(2,1)S(1)}, u32[]{:S(2)}, u32[]{:S(2)}) collective-permute-start(bf16[64,2048]{1,0:T(8,128)(2,1)S(1)} %get-tuple-element.24), channel_id=1, source_target_pairs={{0,12},{4,8},{8,4},{12,0},{1,13},{5,9},{9,5},{13,1},{2,14},{6,10},... | collective-permute-start | bytes 786440 | tf_op jit(solution)/shard_map/ppermute | solution.py:168
  30.7 1.9 %collective-permute-start.2 = (bf16[64,2048]{1,0:T(8,128)(2,1)S(1)}, bf16[64,2048]{1,0:T(8,128)(2,1)S(1)}, u32[]{:S(2)}, u32[]{:S(2)}) collective-permute-start(bf16[64,2048]{1,0:T(8,128)(2,1)S(1)} %get-tuple-element.23), channel_id=1, source_target_pairs={{0,76},{4,72},{8,68},{12,64},{64,12},{68,8},{72,4},{76,0},{1,77},{... | collective-permute-start | bytes 786440 | tf_op jit(solution)/shard_map/ppermute | solution.py:190
  32.7 4.7 %collective-permute-done.1.d10 = bf16[64,2048]{1,0:T(8,128)(2,1)S(1)} collective-permute-done((bf16[64,2048]{1,0:T(8,128)(2,1)S(1)}, bf16[64,2048]{1,0:T(8,128)(2,1)S(1)}, u32[]{:S(2)}, u32[]{:S(2)}) %collective-permute-start.1) | collective-permute-done | bytes 262176 | tf_op jit(solution)/shard_map/ppermute | solution.py:168
  37.4 5.6 %collective-permute-done.2.d11 = bf16[64,2048]{1,0:T(8,128)(2,1)S(1)} collective-permute-done((bf16[64,2048]{1,0:T(8,128)(2,1)S(1)}, bf16[64,2048]{1,0:T(8,128)(2,1)S(1)}, u32[]{:S(2)}, u32[]{:S(2)}) %collective-permute-start.2) | collective-permute-done | bytes 262176 | tf_op jit(solution)/shard_map/ppermute | solution.py:190
  43.0 5.5 %all-to-all-done.recv_ref = bf16[32,64,256]{2,1,0:T(8,128)(2,1)S(1)} async-done(((bf16[32,64,256]{2,1,0:T(8,128)(2,1)}), bf16[32,64,256]{2,1,0:T(8,128)(2,1)S(1)}, u32[]{:S(2)}, u32[]{:S(2)}) %all-to-all-start) | async-done | bytes 1048608 | tf_op jit(solution)/shard_map/all_to_all | solution.py:183
  48.5 2.9 %shard_map.39 = (bf16[4,64,2048]{2,1,0:T(8,128)(2,1)}, bf16[4,64,2048]{2,1,0:T(8,128)(2,1)S(1)}, f32[1,256]{1,0:T(1,128)S(1)}) custom-call(bf16[32,64,256]{2,1,0:T(8,128)(2,1)S(1)} %all-to-all-done.recv_ref, bf16[64,2048]{1,0:T(8,128)(2,1)S(1)} %get-tuple-element.26.d00, bf16[64,2048]{1,0:T(8,128)(2,1)S(1)} %collective-permute-done.d01, ...), custom_call_target="tpu_custom_call" | custom-call | tf_op jit(solution)/shard_map/pallas_call | solution.py:192
  51.5 1.9 %collective-permute-start.3 = (bf16[64,2048]{1,0:T(8,128)(2,1)S(1)}, bf16[64,2048]{1,0:T(8,128)(2,1)S(1)}, u32[]{:S(2)}, u32[]{:S(2)}) collective-permute-start(bf16[64,2048]{1,0:T(8,128)(2,1)S(1)} %get-tuple-element.22), channel_id=1, source_target_pairs={{0,16},{16,32},{32,48},{48,1},{1,17},{17,33},{33,49},{49,2},{2,18}... | collective-permute-start | bytes 786440 | tf_op jit(solution)/shard_map/ppermute | solution.py:218
  53.4 2.8 %collective-permute-start.4 = (bf16[64,2048]{1,0:T(8,128)(2,1)S(1)}, bf16[64,2048]{1,0:T(8,128)(2,1)S(1)}, u32[]{:S(2)}, u32[]{:S(2)}) collective-permute-start(bf16[64,2048]{1,0:T(8,128)(2,1)S(1)} %get-tuple-element.21), channel_id=1, source_target_pairs={{0,32},{16,48},{32,1},{48,17},{1,33},{17,49},{33,2},{49,18},{2,34}... | collective-permute-start | bytes 786440 | tf_op jit(solution)/shard_map/ppermute | solution.py:218
  56.2 6.5 %collective-permute-start.5 = (bf16[64,2048]{1,0:T(8,128)(2,1)S(1)}, bf16[64,2048]{1,0:T(8,128)(2,1)S(1)}, u32[]{:S(2)}, u32[]{:S(2)}) collective-permute-start(bf16[64,2048]{1,0:T(8,128)(2,1)S(1)} %get-tuple-element.20), channel_id=1, source_target_pairs={{0,51},{16,0},{32,16},{48,32},{1,48},{17,1},{33,17},{49,33},{2,49}... | collective-permute-start | bytes 786440 | tf_op jit(solution)/shard_map/ppermute | solution.py:218
  62.7 2.4 %collective-permute-done.3 = bf16[64,2048]{1,0:T(8,128)(2,1)S(1)} collective-permute-done((bf16[64,2048]{1,0:T(8,128)(2,1)S(1)}, bf16[64,2048]{1,0:T(8,128)(2,1)S(1)}, u32[]{:S(2)}, u32[]{:S(2)}) %collective-permute-start.3) | collective-permute-done | bytes 262176 | tf_op jit(solution)/shard_map/ppermute | solution.py:218
  65.1 10.7 %collective-permute-done.4 = bf16[64,2048]{1,0:T(8,128)(2,1)S(1)} collective-permute-done((bf16[64,2048]{1,0:T(8,128)(2,1)S(1)}, bf16[64,2048]{1,0:T(8,128)(2,1)S(1)}, u32[]{:S(2)}, u32[]{:S(2)}) %collective-permute-start.4) | collective-permute-done | bytes 262176 | tf_op jit(solution)/shard_map/ppermute | solution.py:218
  75.9 1.9 %collective-permute-start.6 = (bf16[256,2048]{1,0:T(8,128)(2,1)S(1)}, bf16[256,2048]{1,0:T(8,128)(2,1)S(1)}, u32[]{:S(2)}, u32[]{:S(2)}) collective-permute-start(bf16[256,2048]{1,0:T(8,128)(2,1)S(1)} %pad_maximum_fusion.own_ref), channel_id=1, source_target_pairs={{0,4},{4,0},{1,5},{5,1},{2,6},{6,2},{3,7},{7,3},{8,12},{12,8},{9,1... | collective-permute-start | bytes 3145736 | tf_op jit(solution)/shard_map/ppermute | solution.py:222
  77.8 4.9 %psum.14 = f32[1,256]{1,0:T(1,128)S(1)} all-reduce(f32[1,256]{1,0:T(1,128)S(1)} %get-tuple-element.14), channel_id=1, replica_groups=mesh['x'=4,'core'=2,'zlo'=4,'y1'=2,'y0'=2,'zhi'=4] {'core'}, use_global_device_ids=true, to_apply=%region_0.0 | all-reduce | flops 256 | bytes 2048 | tf_op jit(solution)/shard_map/psum | solution.py:224
  82.7 5.1 %collective-permute-start.7 = (f32[1,256]{1,0:T(1,128)S(1)}, f32[1,256]{1,0:T(1,128)S(1)}, u32[]{:S(2)}, u32[]{:S(2)}) collective-permute-start(f32[1,256]{1,0:T(1,128)S(1)} %psum.14), channel_id=1, source_target_pairs={{0,12},{4,8},{8,4},{12,0},{1,13},{5,9},{9,5},{13,1},{2,14},{6,10},... | collective-permute-start | bytes 3080 | tf_op jit(solution)/shard_map/ppermute | solution.py:168
  87.8 1.3 collective-permute-done.7
  89.2 11.4 %all_to_all.16 = f32[32,1,64]{2,1,0:T(1,128)S(1)} all-to-all(f32[32,1,64]{2,1,0:T(1,128)S(1)} %broadcast_in_dim.8), channel_id=1, replica_groups=mesh['x'=4,'core'=2,'zlo'=4,'y1'=2,'y0'=2,'zhi'=4] {'x','zlo','y0'}, dimensions={0} | all-to-all | bytes 16384 | tf_op jit(solution)/shard_map/all_to_all | solution.py:175
  102.0 6.4 %all-gather.2.cloned.1.call-done = bf16[1024,2048]{1,0:T(8,128)(2,1)} async-done(((bf16[256,2048]{1,0:T(8,128)(2,1)}), bf16[1024,2048]{1,0:T(8,128)(2,1)}) %all-gather.2.cloned.1.call-update) | async-done | bytes 4194320 | tf_op jit(solution)/shard_map/all_gather | solution.py:223
  108.3 6.8 %shard_map.40 = (f32[16,16,512]{2,1,0:T(8,128)S(1)}, f32[16,16,512]{2,1,0:T(8,128)S(1)}, f32[16,16,512]{2,1,0:T(8,128)S(1)}, f32[16,16,512]{2,1,0:T(8,128)}) custom-call(bf16[256,2048]{1,0:T(8,128)(2,1)S(1)} %pad_maximum_fusion.own_ref, bf16[256,2048]{1,0:T(8,128)(2,1)S(1)} %collective-permute-done.6.far_ref, bf16[8,128,2048]{2,1,0:T(8,128)(2,1)} %bitcast.29, ...), custom_call_target="tpu_custom_call" | custom-call | tf_op jit(solution)/shard_map/pallas_call | solution.py:230
  115.1 0.8 copy-done.2
  115.9 2.6 %collective-permute-start.9 = (f32[16,16,512]{2,1,0:T(8,128)}, f32[16,16,512]{2,1,0:T(8,128)S(1)}, u32[]{:S(2)}, u32[]{:S(2)}) collective-permute-start(f32[16,16,512]{2,1,0:T(8,128)} %get-tuple-element.18), channel_id=1, source_target_pairs={{0,64},{64,0},{1,65},{65,1},{2,66},{66,2},{3,67},{67,3},{4,68},{68... | collective-permute-start | bytes 1572872 | tf_op jit(solution)/shard_map/ppermute | solution.py:171
  118.8 1.9 %collective-permute-start.8 = (f32[16,16,512]{2,1,0:T(8,128)}, f32[16,16,512]{2,1,0:T(8,128)S(1)}, u32[]{:S(2)}, u32[]{:S(2)}) collective-permute-start(f32[16,16,512]{2,1,0:T(8,128)} %copy-done.2), channel_id=1, source_target_pairs={{0,64},{64,0},{1,65},{65,1},{2,66},{66,2},{3,67},{67,3},{4,68},{68... | collective-permute-start | bytes 1572872 | tf_op jit(solution)/shard_map/ppermute | solution.py:171
  120.9 4.4 %collective-permute-start.10 = (bf16[16,16,512]{2,1,0:T(8,128)(2,1)S(1)}, bf16[16,16,512]{2,1,0:T(8,128)(2,1)S(1)}, u32[]{:S(2)}, u32[]{:S(2)}) collective-permute-start(bf16[16,16,512]{2,1,0:T(8,128)(2,1)S(1)} %add_convert_fusion), channel_id=1, source_target_pairs={{0,12},{4,8},{8,4},{12,0},{1,13},{5,9},{9,5},{13,1},{2,14},{6,10},... | collective-permute-start | bytes 786440 | tf_op jit(solution)/shard_map/ppermute | solution.py:168
  125.5 5.8 %collective-permute-done.10 = bf16[16,16,512]{2,1,0:T(8,128)(2,1)S(1)} collective-permute-done((bf16[16,16,512]{2,1,0:T(8,128)(2,1)S(1)}, bf16[16,16,512]{2,1,0:T(8,128)(2,1)S(1)}, u32[]{:S(2)}, u32[]{:S(2)}) %collective-permute-start.10) | collective-permute-done | bytes 262176 | tf_op jit(solution)/shard_map/ppermute | solution.py:168
  131.5 3.5 %psum.15 = f32[4,128]{1,0:T(4,128)S(1)} all-reduce(f32[4,128]{1,0:T(4,128)S(1)} %bitcast.33), channel_id=1, replica_groups=mesh['x'=4,'core'=2,'zlo'=4,'y1'=2,'y0'=2,'zhi'=4] {'core'}, use_global_device_ids=true, to_apply=%region_2.3 | all-reduce | flops 512 | bytes 4096 | tf_op jit(solution)/shard_map/psum | solution.py:254
  135.0 27.0 %all_to_all.17 = f32[16,4,128]{2,1,0:T(4,128)S(1)} all-to-all(f32[16,4,128]{2,1,0:T(4,128)S(1)} %broadcast_in_dim.20), channel_id=1, replica_groups=mesh['x'=4,'core'=2,'zlo'=4,'y1'=2,'y0'=2,'zhi'=4] {'x','zhi'}, dimensions={0} | all-to-all | bytes 65536 | tf_op jit(solution)/shard_map/all_to_all | solution.py:175
  162.0 1.0 broadcast_multiply_fusion
  (34 shorter events, 2.6 us)
Async XLA Ops:
  6.5 1.2 copy-start
  7.8 0.8 copy-start.1
  10.8 37.6 %all-to-all-start = ((bf16[32,64,256]{2,1,0:T(8,128)(2,1)}), bf16[32,64,256]{2,1,0:T(8,128)(2,1)S(1)}, u32[]{:S(2)}, u32[]{:S(2)}) async-start(bf16[32,64,256]{2,1,0:T(8,128)(2,1)} %shard_map.37.out_ref), calls=%async_computation | async-start | bytes 2097152 | tf_op jit(solution)/shard_map/all_to_all | solution.py:183
  21.2 87.2 %all-gather.2.cloned.1.call-start = ((), (), s32[]{:S(2)}) async-start(), calls=%async_computation.3 | async-start | bytes 5242880 | tf_op jit(solution)/shard_map/all_gather | solution.py:223
  23.0 9.7 %collective-permute-start = (bf16[64,2048]{1,0:T(8,128)(2,1)S(1)}, bf16[64,2048]{1,0:T(8,128)(2,1)S(1)}, u32[]{:S(2)}, u32[]{:S(2)}) collective-permute-start(bf16[64,2048]{1,0:T(8,128)(2,1)S(1)} %get-tuple-element.25), channel_id=1, source_target_pairs={{0,64},{64,0},{1,65},{65,1},{2,66},{66,2},{3,67},{67,3},{4,68},{68... | collective-permute-start | bytes 786440 | tf_op jit(solution)/shard_map/ppermute | solution.py:171
  25.9 11.5 %collective-permute-start.1 = (bf16[64,2048]{1,0:T(8,128)(2,1)S(1)}, bf16[64,2048]{1,0:T(8,128)(2,1)S(1)}, u32[]{:S(2)}, u32[]{:S(2)}) collective-permute-start(bf16[64,2048]{1,0:T(8,128)(2,1)S(1)} %get-tuple-element.24), channel_id=1, source_target_pairs={{0,12},{4,8},{8,4},{12,0},{1,13},{5,9},{9,5},{13,1},{2,14},{6,10},... | collective-permute-start | bytes 786440 | tf_op jit(solution)/shard_map/ppermute | solution.py:168
  30.7 12.3 %collective-permute-start.2 = (bf16[64,2048]{1,0:T(8,128)(2,1)S(1)}, bf16[64,2048]{1,0:T(8,128)(2,1)S(1)}, u32[]{:S(2)}, u32[]{:S(2)}) collective-permute-start(bf16[64,2048]{1,0:T(8,128)(2,1)S(1)} %get-tuple-element.23), channel_id=1, source_target_pairs={{0,76},{4,72},{8,68},{12,64},{64,12},{68,8},{72,4},{76,0},{1,77},{... | collective-permute-start | bytes 786440 | tf_op jit(solution)/shard_map/ppermute | solution.py:190
  51.5 13.6 %collective-permute-start.3 = (bf16[64,2048]{1,0:T(8,128)(2,1)S(1)}, bf16[64,2048]{1,0:T(8,128)(2,1)S(1)}, u32[]{:S(2)}, u32[]{:S(2)}) collective-permute-start(bf16[64,2048]{1,0:T(8,128)(2,1)S(1)} %get-tuple-element.22), channel_id=1, source_target_pairs={{0,16},{16,32},{32,48},{48,1},{1,17},{17,33},{33,49},{49,2},{2,18}... | collective-permute-start | bytes 786440 | tf_op jit(solution)/shard_map/ppermute | solution.py:218
  53.4 22.4 %collective-permute-start.4 = (bf16[64,2048]{1,0:T(8,128)(2,1)S(1)}, bf16[64,2048]{1,0:T(8,128)(2,1)S(1)}, u32[]{:S(2)}, u32[]{:S(2)}) collective-permute-start(bf16[64,2048]{1,0:T(8,128)(2,1)S(1)} %get-tuple-element.21), channel_id=1, source_target_pairs={{0,32},{16,48},{32,1},{48,17},{1,33},{17,49},{33,2},{49,18},{2,34}... | collective-permute-start | bytes 786440 | tf_op jit(solution)/shard_map/ppermute | solution.py:218
  56.2 19.6 %collective-permute-start.5 = (bf16[64,2048]{1,0:T(8,128)(2,1)S(1)}, bf16[64,2048]{1,0:T(8,128)(2,1)S(1)}, u32[]{:S(2)}, u32[]{:S(2)}) collective-permute-start(bf16[64,2048]{1,0:T(8,128)(2,1)S(1)} %get-tuple-element.20), channel_id=1, source_target_pairs={{0,51},{16,0},{32,16},{48,32},{1,48},{17,1},{33,17},{49,33},{2,49}... | collective-permute-start | bytes 786440 | tf_op jit(solution)/shard_map/ppermute | solution.py:218
  75.9 26.0 %collective-permute-start.6 = (bf16[256,2048]{1,0:T(8,128)(2,1)S(1)}, bf16[256,2048]{1,0:T(8,128)(2,1)S(1)}, u32[]{:S(2)}, u32[]{:S(2)}) collective-permute-start(bf16[256,2048]{1,0:T(8,128)(2,1)S(1)} %pad_maximum_fusion.own_ref), channel_id=1, source_target_pairs={{0,4},{4,0},{1,5},{5,1},{2,6},{6,2},{3,7},{7,3},{8,12},{12,8},{9,1... | collective-permute-start | bytes 3145736 | tf_op jit(solution)/shard_map/ppermute | solution.py:222
  82.7 6.4 %collective-permute-start.7 = (f32[1,256]{1,0:T(1,128)S(1)}, f32[1,256]{1,0:T(1,128)S(1)}, u32[]{:S(2)}, u32[]{:S(2)}) collective-permute-start(f32[1,256]{1,0:T(1,128)S(1)} %psum.14), channel_id=1, source_target_pairs={{0,12},{4,8},{8,4},{12,0},{1,13},{5,9},{9,5},{13,1},{2,14},{6,10},... | collective-permute-start | bytes 3080 | tf_op jit(solution)/shard_map/ppermute | solution.py:168
  108.3 10.2 %copy-start.3 = (s32[64,64]{1,0:T(8,128)S(1)}, s32[64,64]{1,0:T(8,128)}, u32[]{:S(2)}) copy-start(s32[64,64]{1,0:T(8,128)} %param.5) | copy-start | bytes 49156
  115.1 0.8 copy-start.2
  115.9 4.8 %collective-permute-start.9 = (f32[16,16,512]{2,1,0:T(8,128)}, f32[16,16,512]{2,1,0:T(8,128)S(1)}, u32[]{:S(2)}, u32[]{:S(2)}) collective-permute-start(f32[16,16,512]{2,1,0:T(8,128)} %get-tuple-element.18), channel_id=1, source_target_pairs={{0,64},{64,0},{1,65},{65,1},{2,66},{66,2},{3,67},{67,3},{4,68},{68... | collective-permute-start | bytes 1572872 | tf_op jit(solution)/shard_map/ppermute | solution.py:171
  118.8 6.7 %collective-permute-start.8 = (f32[16,16,512]{2,1,0:T(8,128)}, f32[16,16,512]{2,1,0:T(8,128)S(1)}, u32[]{:S(2)}, u32[]{:S(2)}) collective-permute-start(f32[16,16,512]{2,1,0:T(8,128)} %copy-done.2), channel_id=1, source_target_pairs={{0,64},{64,0},{1,65},{65,1},{2,66},{66,2},{3,67},{67,3},{4,68},{68... | collective-permute-start | bytes 1572872 | tf_op jit(solution)/shard_map/ppermute | solution.py:171
  120.9 10.5 %collective-permute-start.10 = (bf16[16,16,512]{2,1,0:T(8,128)(2,1)S(1)}, bf16[16,16,512]{2,1,0:T(8,128)(2,1)S(1)}, u32[]{:S(2)}, u32[]{:S(2)}) collective-permute-start(bf16[16,16,512]{2,1,0:T(8,128)(2,1)S(1)} %add_convert_fusion), channel_id=1, source_target_pairs={{0,12},{4,8},{8,4},{12,0},{1,13},{5,9},{9,5},{13,1},{2,14},{6,10},... | collective-permute-start | bytes 786440 | tf_op jit(solution)/shard_map/ppermute | solution.py:168
Sparse Core Ops, SparseCore 0:
  51.5 56.7 all-gather.1

commit v5 on v4

v5 whole, which is shorter than its diff:
```python
import functools

import jax
import jax.numpy as jnp
from jax import lax
from jax.experimental import pallas as pl
from jax.experimental.pallas import tpu as pltpu
from jax.sharding import Mesh, PartitionSpec as P

BLK = 128
INTERPRET = False
BF16, F32 = jnp.bfloat16, jnp.float32
PARAMS = dict(vmem_limit_bytes=48 * 1024 * 1024)
AXES = ("x", "core", "z1", "z0", "y", "zhi")
SWAP = [(0, 1), (1, 0)]


def where_am_i():
    return tuple(lax.axis_index(a) for a in AXES)


def mask_kernel(mask_ref, adj_ref, out_ref):
    x_id, _, z1, z0, y_id, _ = where_am_i()
    nx, ny = lax.axis_size("x"), lax.axis_size("y")
    row = ((z1 * 2 + z0) * ny + y_id) * nx + x_id
    for x in range(nx):
        for z in range(4):
            low, high = (z, 0) if z < 2 else (3 - z, 1)
            base = (x * 2 + jnp.where(z1 == 0, low, 1 - low)) * ny
            for y in range(ny):
                block = (z * ny + y) * nx + x
                keep = mask_ref[row, block].astype(F32).astype(BF16)
                out_ref[base + y, :, high * BLK : (high + 1) * BLK] = (
                    adj_ref[0, :, block * BLK : (block + 1) * BLK] * keep
                )


def pieces_kernel(out_ref, piece_ref):
    _, core, z1, _, _, _ = where_am_i()
    nx, ny = lax.axis_size("x"), lax.axis_size("y")
    n = out_ref.shape[1]
    low_lanes = lax.broadcasted_iota(jnp.int32, (n, BLK), 1) < n
    for p in range(nx * ny):
        x, z0, q = p // ny, p % ny // (ny // 2), p % (ny // 2)
        cols = slice(p * BLK, (p + 1) * BLK)
        for half in range(2):
            low = z0 ^ half
            spot = (x * 2 + jnp.where(z1 == 0, low, 1 - low)) * ny + 2 * q
            lanes = slice(half * BLK, (half + 1) * BLK)
            a = out_ref[spot, :, lanes].astype(F32)
            b = out_ref[spot + 1, :, lanes].astype(F32)
            first = jnp.where(low_lanes, a, pltpu.roll(b, n, 1)).astype(BF16)
            second = jnp.where(low_lanes, pltpu.roll(a, n, 1), b).astype(BF16)
            i = jnp.where(z1 == half, 0, 1)
            piece_ref[2 * i + core, :, cols] = first
            piece_ref[2 * i + 1 - core, :, cols] = second


def form_kernel(
    recv_ref, d00, d01, d10, d11, block_ref, shard_ref, sum_ref, flip_ref, acc_ref
):
    x_id, core, z1, z0, y_id, l_id = where_am_i()
    ny, nl = lax.axis_size("y"), lax.axis_size("zhi")
    n = d00.shape[0]
    part = n // nl
    step = pl.program_id(0)
    own_source = z0 * ny + y_id
    own_p = jnp.where(step == x_id, own_source // 2, -1)
    r = lax.broadcasted_iota(jnp.int32, (n, BLK), 0)
    k = lax.broadcasted_iota(jnp.int32, (n, BLK), 1)
    diagonal = jnp.where(k == r + own_source % 2 * n, 1.0, 0.0)

    @pl.when(step == 0)
    def _():
        acc_ref[...] = jnp.zeros_like(acc_ref)

    for p in range(ny):
        cols = slice(p * BLK, (p + 1) * BLK)
        got = recv_ref[2 * p : 2 * p + 2].reshape(BLK, 2 * BLK).astype(F32)
        flip_ref[...] = got.T.reshape(flip_ref.shape)
        for i, direct in enumerate((d00, d01, d10, d11)):
            b, c = i // 2, i % 2
            spot = jnp.where(z1 == b, 0, 2) + jnp.where(core == c, 0, 1)
            value = direct[:, cols].astype(F32) + flip_ref[spot]
            if i == 0:
                value = value + jnp.where(own_p == p, diagonal, 0.0)
            rounded = value.astype(BF16)
            block_ref[2 * jnp.where(core == c, 0, 1) + b, :, cols] = rounded
            acc_ref[spot] += rounded.astype(F32)

    rows = pl.ds(pl.multiple_of(l_id * part, part), part)
    for group in range(4):
        spot = group % 2 * 2 + (group // 2 ^ z1)
        shard_ref[group * part : (group + 1) * part, :] = block_ref[spot, rows, :]

    @pl.when(step == pl.num_programs(0) - 1)
    def _():
        acc = acc_ref[...].reshape(4 * n, BLK)
        sum_ref[...] = jnp.sum(acc.T, axis=0, keepdims=True)


def product_kernel(group, left_ref, *refs):
    *right_refs, degree_ref, mine_ref, theirs_ref, right = refs
    if len(right_refs) == 5:
        own_ref, before_ref, far0_ref, far1_ref, after_ref = right_refs
        right_refs = [(own_ref,) * 2, (before_ref,) * 2, (far0_ref, far1_ref), (after_ref,) * 2]
    else:
        right_refs = [(ref,) * 2 for ref in right_refs]
    x_id, core, z1, _, _, _ = where_am_i()
    nx, ny = lax.axis_size("x"), lax.axis_size("y")
    part = left_ref.shape[0] // (8 * ny)
    inverse = 1.0 / degree_ref[...]
    n = BLK // 2
    for d, pair in enumerate(right_refs):
        for core_rows, ref in enumerate(pair):
            low = (2 * core_rows if ref.shape[0] > BLK else 0) * n + group * n
            block = ref[low : low + n, :].astype(F32)
            rows = slice(d * BLK + core_rows * n, d * BLK + (core_rows + 1) * n)
            right[rows, :] = (block * inverse).astype(BF16)
    value = lax.dot_general(
        left_ref[...], right[...], (((1,), (1,)), ((), ())), preferred_element_type=F32
    )
    value = value.reshape(8 * ny, part, right.shape[0])
    for sel in range(2):
        low = jnp.where(z1 == sel, 0, 1)
        for y in range(ny):
            for b in range(2):
                c = jnp.where(b == 0, low, 3 - low) * ny + y
                spot = ((sel * ny + y) * 2 + b) * 2
                first, second = value[spot], value[spot + 1]
                mine = jnp.where(core == 0, first, second)
                theirs = jnp.where(core == 0, second, first).astype(BF16)
                for e in range(nx):
                    x = (x_id - e + nx) % nx
                    lanes = pl.ds(pl.multiple_of(x * BLK, BLK), BLK)
                    mine_ref[c, :, lanes] = mine[:, e * BLK : (e + 1) * BLK]
                    theirs_ref[c, :, lanes] = theirs[:, e * BLK : (e + 1) * BLK]


def on_device(adjacency, block_mask, prune_mask):
    rows_dev = adjacency.shape[1]
    node_count = adjacency.shape[2]
    nx, nk, _, _, ny, nl = (lax.axis_size(a) for a in AXES)
    nc = 4 * ny
    x_id, k_id, z1, z0, y_id, _ = where_am_i()
    c_id = (z1 * 2 + z0) * ny + y_id
    part = rows_dev // nl
    inner = node_count // 4
    width = inner // nx
    shape = jax.ShapeDtypeStruct
    vmem = pl.BlockSpec(memory_space=pltpu.VMEM)
    params = pltpu.CompilerParams(**PARAMS)
    call = functools.partial(pl.pallas_call, compiler_params=params, interpret=INTERPRET)
    group = ("x", "z0", "y")
    members = nx * 2 * ny

    def other_core(value):
        return lax.ppermute(value, "core", SWAP)

    def spread(piece, axes, count):
        wide = jnp.broadcast_to(piece[None], (count,) + piece.shape)
        return lax.all_to_all(wide, axes, split_axis=0, concat_axis=0, tiled=True)

    ring = []
    for l in range(nl):
        ring += [(0 * nl + l, 3 * nl + (l - 1) % nl), (3 * nl + l, 0 * nl + (l + 1) % nl)]
        ring += [(1 * nl + l, 2 * nl + l), (2 * nl + l, 1 * nl + l)]
    spots = 4 * nl
    ring_across = [(c * spots + a, (1 - c) * spots + b) for c in range(2) for a, b in ring]

    outgoing = call(
        mask_kernel,
        out_shape=shape((members, rows_dev, 2 * BLK), BF16),
        in_specs=[pl.BlockSpec(memory_space=pltpu.SMEM), vmem],
        out_specs=vmem,
    )(block_mask, adjacency)
    received = lax.all_to_all(outgoing, group, split_axis=0, concat_axis=0, tiled=True)
    pieces = call(pieces_kernel, out_shape=shape((4, rows_dev, inner), BF16))(outgoing)
    by_ring = lax.ppermute(pieces[2], ("z1", "z0", "zhi"), ring)
    across = lax.ppermute(pieces[3], ("core", "z1", "z0", "zhi"), ring_across)
    by_ring, swapped = lax.optimization_barrier((by_ring, pieces[1]))
    direct = [pieces[0], other_core(swapped), by_ring, across]
    block, shard, row_sum = call(
        form_kernel,
        grid=(nx,),
        in_specs=[pl.BlockSpec((2 * ny, rows_dev, 2 * BLK), lambda i: (i, 0, 0))]
        + [pl.BlockSpec((rows_dev, width), lambda i: (0, i))] * 4,
        out_specs=[
            pl.BlockSpec((4, rows_dev, width), lambda i: (0, 0, i)),
            pl.BlockSpec((4 * part, width), lambda i: (0, i)),
            pl.BlockSpec((1, 4 * rows_dev), lambda i: (0, 0)),
        ],
        out_shape=[
            shape((4, rows_dev, inner), BF16),
            shape((4 * part, inner), BF16),
            shape((1, 4 * rows_dev), F32),
        ],
        scratch_shapes=[
            pltpu.VMEM((4, rows_dev, BLK), F32),
            pltpu.VMEM((4, rows_dev, BLK), F32),
        ],
    )(received, *direct)
    rows = lax.all_gather(shard, ("z0", "y"), axis=0, tiled=True)
    def step_x(piece, d):
        return lax.ppermute(piece, "x", [(i, (i + d) % nx) for i in range(nx)])

    partial = row_sum.reshape(2, 2, rows_dev).transpose(1, 0, 2)
    partial = jnp.broadcast_to(partial[:, :, None, None], (2, 2, 2, ny, rows_dev))
    partial = lax.all_to_all(
        partial.reshape(8 * ny, rows_dev),
        ("core", "z1", "z0", "y"),
        split_axis=0,
        concat_axis=0,
        tiled=True,
    )
    own_block = block.reshape(2 * BLK, inner)
    blocks = [own_block, step_x(own_block, 1)]
    if nx == 4:
        after = step_x(own_block, -1)
        before, after, partial = lax.optimization_barrier((blocks[1], after, partial))
        blocks = [own_block, before, step_x(before[:BLK], 1), step_x(after[BLK:], -1), after]
    partial = jnp.sum(partial.reshape(2, 2, 2, ny, rows_dev), axis=0)
    degree = jnp.where(
        z1 == 0, partial[0] + partial[1, ::-1], partial[1] + partial[0, ::-1]
    )
    degree = spread(degree.reshape(-1, BLK), "x", nx).reshape(1, inner)
    tile_cols = nx * BLK

    def product(group):
        return call(
            functools.partial(product_kernel, group),
            in_specs=[vmem] * (len(blocks) + 2),
            out_specs=[vmem] * 2,
            out_shape=[shape((nc, part, tile_cols), t) for t in (F32, BF16)],
            scratch_shapes=[pltpu.VMEM((tile_cols, inner), BF16)],
        )(rows, *blocks, degree)

    mine, theirs = product(1)
    sent = (mine + other_core(theirs).astype(F32)).astype(BF16)
    got = lax.all_to_all(
        jnp.stack([sent, sent]),
        ("z1", "z0"),
        split_axis=0,
        concat_axis=0,
        tiled=True,
        axis_index_groups=[[0, 3], [1, 2]],
    )
    got = lax.dynamic_index_in_dim(got, 1 - z1, 0, keepdims=False)
    mine, theirs = product(0)
    summed = mine + other_core(theirs).astype(F32) + got.astype(F32)
    prune = prune_mask.reshape(nc, nx, nc, nx)
    prune = lax.dynamic_index_in_dim(prune, x_id, 1, keepdims=False)
    prune = lax.dynamic_index_in_dim(prune, c_id, 1, keepdims=False)
    prune = jnp.repeat(prune.astype(F32), BLK, axis=1)
    pruned = summed * summed * prune[:, None, :]
    mass = lax.psum(jnp.sum(pruned, axis=(0, 1)), "core")
    mass = jnp.sum(spread(mass.reshape(-1, BLK), ("x", "zhi"), nx * nl), axis=0).reshape(-1)
    return pruned * (node_count / mass)[None, None, :]


def solution(mesh):
    rows, cols, layers = mesh.devices.shape
    devices = mesh.devices.reshape(rows // 2, 2, 2, 2, cols // 4, layers)
    split = Mesh(devices, AXES)
    in_specs = (P(("z1", "z0", "y"), ("x", "core"), None), P(), P())
    out_specs = P(None, ("x", "core", "zhi"), ("z1", "z0", "y"))
    return jax.shard_map(
        on_device, mesh=split, in_specs=in_specs, out_specs=out_specs, check_vma=False
    )
```

time: 171 us -> 160 us (0.936)
  the two profiles are of different devices: /device:TPU:1 before, /device:TPU:32 now
where the time goes in v5:
time: 160 us; the launch traced here: 159 us
  blocking collectives  60.5 us (38%)
  starting transfers between devices  38.6 us (24%)
  waiting for transfers between devices  21.2 us (13%)
  between operations  13.6 us (8%)
  Pallas kernels  13 us (8%)
  local copies, waits for them, and re-layouts  7.45 us (5%)
  other arithmetic  4.94 us (3%)
    all_to_all x2, blocking collectives, spread(): return lax.all_to_all(wide, axes, split_axis=0, concat_axis=0, tiled=True)  39.3 us
    all_to_all x1, blocking collectives, on_device(): lax.all_to_all(partial.reshape(8 * ny, rows_dev), ('core', 'z1', 'z0', 'y...  18.8 us
    ppermute x4, starting transfers between devices, step_x(): return lax.ppermute(piece, 'x', [(i, (i + d) % nx) for i in range(nx)])  14.1 us
    all_to_all x1, starting transfers between devices, on_device(): lax.all_to_all(outgoing, group, split_axis=0, concat_axis=0, tiled=True)  9.08 us
    all_to_all x1, waiting for transfers between devices, on_device(): lax.all_to_all(jnp.stack([sent, sent]), ('z1', 'z0'), split_axis=0, conca...  6.79 us
    pallas_call x2, Pallas kernels, product(): call(functools.partial(product_kernel, group), in_specs=[vmem] * (len(blo...  6.25 us
    ppermute x3, starting transfers between devices, other_core(): return lax.ppermute(value, 'core', SWAP)  5.86 us
    ppermute x1, waiting for transfers between devices, on_device(): by_ring = lax.ppermute(pieces[2], ('z1', 'z0', 'zhi'), ring)  5.14 us
  transfers between devices with their start and end apart: 12, of which 8 were waited for; matrix products, arithmetic and copies ran while one was open for 3% of the time, Pallas kernels for 3%

profile of v5, /device:TPU:32, one launch (start us, length us, event | category | flops | bytes accessed | tf_op | source)
XLA Modules:
  0.0 159.2 jit_solution(3432353801212987264)
XLA Ops:
  6.5 1.2 copy-done.1
  8.5 2.3 %shard_map.37.out_ref = bf16[32,64,256]{2,1,0:T(8,128)(2,1)} custom-call(s32[64,64]{1,0:T(8,128)S(1)} %copy-done.2, bf16[1,64,8192]{2,1,0:T(8,128)(2,1)S(1)} %copy-done.1), custom_call_target="tpu_custom_call" | custom-call | tf_op jit(solution)/shard_map/pallas_call | solution.py:171
  10.8 9.1 %all-to-all-start = ((bf16[32,64,256]{2,1,0:T(8,128)(2,1)}), bf16[32,64,256]{2,1,0:T(8,128)(2,1)S(1)}, u32[]{:S(2)}, u32[]{:S(2)}) async-start(bf16[32,64,256]{2,1,0:T(8,128)(2,1)} %shard_map.37.out_ref), calls=%async_computation | async-start | bytes 2097152 | tf_op jit(solution)/shard_map/all_to_all | solution.py:177
  20.0 1.7 %shard_map.38 = bf16[4,64,2048]{2,1,0:T(8,128)(2,1)S(1)} custom-call(bf16[32,64,256]{2,1,0:T(8,128)(2,1)} %shard_map.37.out_ref), custom_call_target="tpu_custom_call" | custom-call | tf_op jit(solution)/shard_map/pallas_call | solution.py:178
  21.8 3.4 %collective-permute-start = (bf16[64,2048]{1,0:T(8,128)(2,1)S(1)}, bf16[64,2048]{1,0:T(8,128)(2,1)S(1)}, u32[]{:S(2)}, u32[]{:S(2)}) collective-permute-start(bf16[64,2048]{1,0:T(8,128)(2,1)S(1)} %get-tuple-element.31), channel_id=1, source_target_pairs={{0,51},{48,1},{16,32},{32,16},{1,48},{49,2},{17,33},{33,17},{2,49}... | collective-permute-start | bytes 786440 | tf_op jit(solution)/shard_map/ppermute | solution.py:179
  25.2 1.9 %collective-permute-start.2 = (bf16[64,2048]{1,0:T(8,128)(2,1)S(1)}, bf16[64,2048]{1,0:T(8,128)(2,1)S(1)}, u32[]{:S(2)}, u32[]{:S(2)}) collective-permute-start(bf16[64,2048]{1,0:T(8,128)(2,1)S(1)} %get-tuple-element.29), channel_id=1, source_target_pairs={{0,115},{48,65},{16,96},{32,80},{1,112},{49,66},{17,97},{33,81},{2... | collective-permute-start | bytes 786440 | tf_op jit(solution)/shard_map/ppermute | solution.py:180
  27.1 5.1 %collective-permute-done.d10 = bf16[64,2048]{1,0:T(8,128)(2,1)S(1)} collective-permute-done((bf16[64,2048]{1,0:T(8,128)(2,1)S(1)}, bf16[64,2048]{1,0:T(8,128)(2,1)S(1)}, u32[]{:S(2)}, u32[]{:S(2)}) %collective-permute-start) | collective-permute-done | bytes 262176 | tf_op jit(solution)/shard_map/ppermute | solution.py:179
  32.3 1.9 %collective-permute-start.1 = (bf16[64,2048]{1,0:T(8,128)(2,1)S(1)}, bf16[64,2048]{1,0:T(8,128)(2,1)S(1)}, u32[]{:S(2)}, u32[]{:S(2)}) collective-permute-start(bf16[64,2048]{1,0:T(8,128)(2,1)S(1)} %get-tuple-element.17), channel_id=1, source_target_pairs={{0,64},{64,0},{1,65},{65,1},{2,66},{66,2},{3,67},{67,3},{4,68},{68... | collective-permute-start | bytes 786440 | tf_op jit(solution)/shard_map/ppermute | solution.py:158
  34.2 1.9 %collective-permute-done.2.d11 = bf16[64,2048]{1,0:T(8,128)(2,1)S(1)} collective-permute-done((bf16[64,2048]{1,0:T(8,128)(2,1)S(1)}, bf16[64,2048]{1,0:T(8,128)(2,1)S(1)}, u32[]{:S(2)}, u32[]{:S(2)}) %collective-permute-start.2) | collective-permute-done | bytes 262176 | tf_op jit(solution)/shard_map/ppermute | solution.py:180
  36.1 2.7 %shard_map.39 = (bf16[4,64,2048]{2,1,0:T(8,128)(2,1)S(1)}, bf16[64,2048]{1,0:T(8,128)(2,1)}, f32[1,256]{1,0:T(1,128)S(1)}) custom-call(bf16[32,64,256]{2,1,0:T(8,128)(2,1)S(1)} %all-to-all-done.recv_ref, bf16[64,2048]{1,0:T(8,128)(2,1)S(1)} %get-tuple-element.32.d00, bf16[64,2048]{1,0:T(8,128)(2,1)S(1)} %collective-permute-done.1.d01, ...), custom_call_target="tpu_custom_call" | custom-call | tf_op jit(solution)/shard_map/pallas_call | solution.py:183
  38.8 3.4 %collective-permute-start.3 = (bf16[256,2048]{1,0:T(8,128)(2,1)S(1)}, bf16[256,2048]{1,0:T(8,128)(2,1)S(1)}, u32[]{:S(2)}, u32[]{:S(2)}) collective-permute-start(bf16[256,2048]{1,0:T(8,128)(2,1)S(1)} %bitcast.32), channel_id=1, source_target_pairs={{0,128},{128,256},{256,384},{384,0},{1,129},{129,257},{257,385},{3... | collective-permute-start | bytes 3145736 | tf_op jit(solution)/shard_map/ppermute | solution.py:205
  42.2 3.6 %collective-permute-start.4 = (bf16[256,2048]{1,0:T(8,128)(2,1)S(1)}, bf16[256,2048]{1,0:T(8,128)(2,1)S(1)}, u32[]{:S(2)}, u32[]{:S(2)}) collective-permute-start(bf16[256,2048]{1,0:T(8,128)(2,1)S(1)} %bitcast.33), channel_id=1, source_target_pairs={{0,384},{128,0},{256,128},{384,256},{1,385},{129,1},{257,129},{385... | collective-permute-start | bytes 3145736 | tf_op jit(solution)/shard_map/ppermute | solution.py:205
  47.2 18.8 %all_to_all.32 = f32[32,1,64]{2,1,0:T(1,128)S(1)} all-to-all(f32[32,1,64]{2,1,0:T(1,128)S(1)} %bitcast.42), channel_id=1, replica_groups=mesh['x'=4,'core'=2,'z1'=2,'z0'=2,'y'=4,'zhi'=4] {'core','z1','z0','y'}, dimensions={0} | all-to-all | bytes 16384 | tf_op jit(solution)/shard_map/all_to_all | solution.py:209
  65.9 1.7 %collective-permute-done.3.refs_1_ = bf16[256,2048]{1,0:T(8,128)(2,1)S(1)} collective-permute-done((bf16[256,2048]{1,0:T(8,128)(2,1)S(1)}, bf16[256,2048]{1,0:T(8,128)(2,1)S(1)}, u32[]{:S(2)}, u32[]{:S(2)}) %collective-permute-start.3) | collective-permute-done | bytes 1048608 | tf_op jit(solution)/shard_map/ppermute | solution.py:205
  67.6 1.9 %collective-permute-done.4.refs_4_ = bf16[256,2048]{1,0:T(8,128)(2,1)S(1)} collective-permute-done((bf16[256,2048]{1,0:T(8,128)(2,1)S(1)}, bf16[256,2048]{1,0:T(8,128)(2,1)S(1)}, u32[]{:S(2)}, u32[]{:S(2)}) %collective-permute-start.4) | collective-permute-done | bytes 1048608 | tf_op jit(solution)/shard_map/ppermute | solution.py:205
  70.3 3.4 %collective-permute-start.5 = (bf16[128,2048]{1,0:T(8,128)(2,1)}, bf16[128,2048]{1,0:T(8,128)(2,1)}, u32[]{:S(2)}, u32[]{:S(2)}) collective-permute-start(bf16[128,2048]{1,0:T(8,128)(2,1)} %slice.30), channel_id=1, source_target_pairs={{0,128},{128,256},{256,384},{384,0},{1,129},{129,257},{257,385},{3... | collective-permute-start | bytes 1572872 | tf_op jit(solution)/shard_map/ppermute | solution.py:205
  74.5 3.7 %collective-permute-start.6 = (bf16[128,2048]{1,0:T(8,128)(2,1)}, bf16[128,2048]{1,0:T(8,128)(2,1)}, u32[]{:S(2)}, u32[]{:S(2)}) collective-permute-start(bf16[128,2048]{1,0:T(8,128)(2,1)} %slice.31), channel_id=1, source_target_pairs={{0,384},{128,0},{256,128},{384,256},{1,385},{129,1},{257,129},{385... | collective-permute-start | bytes 1572872 | tf_op jit(solution)/shard_map/ppermute | solution.py:205
  78.4 11.6 %all_to_all.33 = f32[4,4,128]{2,1,0:T(4,128)S(1)} all-to-all(f32[4,4,128]{2,1,0:T(4,128)S(1)} %broadcast_in_dim.11), channel_id=1, replica_groups=mesh['x'=4,'core'=2,'z1'=2,'z0'=2,'y'=4,'zhi'=4] {'x'}, dimensions={0} | all-to-all | bytes 16384 | tf_op jit(solution)/shard_map/all_to_all | solution.py:162
  89.9 2.0 %all-gather.2.cloned.1.call-done.left_ref = bf16[512,2048]{1,0:T(8,128)(2,1)} async-done(((bf16[64,2048]{1,0:T(8,128)(2,1)}), bf16[512,2048]{1,0:T(8,128)(2,1)}) %all-gather.2.cloned.1.call-update) | async-done | bytes 2097168 | tf_op jit(solution)/shard_map/all_gather | solution.py:203
  91.9 3.1 %shard_map.41 = (f32[16,16,512]{2,1,0:T(8,128)S(1)}, bf16[16,16,512]{2,1,0:T(8,128)(2,1)S(1)}) custom-call(bf16[512,2048]{1,0:T(8,128)(2,1)} %all-gather.2.cloned.1.call-done.left_ref, bf16[256,2048]{1,0:T(8,128)(2,1)S(1)} %bitcast.34, bf16[256,2048]{1,0:T(8,128)(2,1)S(1)} %collective-permute-done.3.refs_1_, ...), custom_call_target="tpu_custom_call" | custom-call | tf_op jit(solution)/shard_map/pallas_call | solution.py:230
  95.1 1.9 %collective-permute-start.8 = (bf16[16,16,512]{2,1,0:T(8,128)(2,1)S(1)}, bf16[16,16,512]{2,1,0:T(8,128)(2,1)S(1)}, u32[]{:S(2)}, u32[]{:S(2)}) collective-permute-start(bf16[16,16,512]{2,1,0:T(8,128)(2,1)S(1)} %get-tuple-element.28), channel_id=1, source_target_pairs={{0,64},{64,0},{1,65},{65,1},{2,66},{66,2},{3,67},{67,3},{4,68},{68... | collective-permute-start | bytes 786440 | tf_op jit(solution)/shard_map/ppermute | solution.py:158
  97.0 1.5 collective-permute-done.8
  99.4 4.2 %all-to-all-start.3 = ((bf16[2,16,16,512]{3,2,1,0:T(8,128)(2,1)}), bf16[2,16,16,512]{3,2,1,0:T(8,128)(2,1)}, u32[]{:S(2)}, u32[]{:S(2)}) async-start(bf16[2,16,16,512]{3,2,1,0:T(8,128)(2,1)} %pad_maximum_fusion), calls=%async_computation.3 | async-start | bytes 1048576 | tf_op jit(solution)/shard_map/all_to_all | solution.py:240
  103.6 1.1 reshape.62
  104.7 3.1 %shard_map.40 = (f32[16,16,512]{2,1,0:T(8,128)S(1)}, bf16[16,16,512]{2,1,0:T(8,128)(2,1)S(1)}) custom-call(bf16[512,2048]{1,0:T(8,128)(2,1)} %all-gather.2.cloned.1.call-done.left_ref, bf16[256,2048]{1,0:T(8,128)(2,1)S(1)} %bitcast.35, bf16[256,2048]{1,0:T(8,128)(2,1)S(1)} %collective-permute-done.3.refs_1_, ...), custom_call_target="tpu_custom_call" | custom-call | tf_op jit(solution)/shard_map/pallas_call | solution.py:230
  108.6 2.0 %collective-permute-start.7 = (bf16[16,16,512]{2,1,0:T(8,128)(2,1)S(1)}, bf16[16,16,512]{2,1,0:T(8,128)(2,1)S(1)}, u32[]{:S(2)}, u32[]{:S(2)}) collective-permute-start(bf16[16,16,512]{2,1,0:T(8,128)(2,1)S(1)} %get-tuple-element.26), channel_id=1, source_target_pairs={{0,64},{64,0},{1,65},{65,1},{2,66},{66,2},{3,67},{67,3},{4,68},{68... | collective-permute-start | bytes 786440 | tf_op jit(solution)/shard_map/ppermute | solution.py:158
  110.7 0.9 constant_dynamic-slice_fusion
  112.1 6.8 %all-to-all-done.3 = bf16[2,16,16,512]{3,2,1,0:T(8,128)(2,1)} async-done(((bf16[2,16,16,512]{3,2,1,0:T(8,128)(2,1)}), bf16[2,16,16,512]{3,2,1,0:T(8,128)(2,1)}, u32[]{:S(2)}, u32[]{:S(2)}) %all-to-all-start.3) | async-done | bytes 524320 | tf_op jit(solution)/shard_map/all_to_all | solution.py:240
  118.8 1.3 fusion.3
  120.1 2.5 %psum.7 = f32[4,128]{1,0:T(4,128)S(1)} all-reduce(f32[4,128]{1,0:T(4,128)S(1)} %bitcast.43), channel_id=1, replica_groups=mesh['x'=4,'core'=2,'z1'=2,'z0'=2,'y'=4,'zhi'=4] {'core'}, use_global_device_ids=true, to_apply=%region_2.3 | all-reduce | flops 512 | bytes 4096 | tf_op jit(solution)/shard_map/psum | solution.py:256
  122.6 27.7 %all_to_all.34 = f32[16,4,128]{2,1,0:T(4,128)S(1)} all-to-all(f32[16,4,128]{2,1,0:T(4,128)S(1)} %broadcast_in_dim.26), channel_id=1, replica_groups=mesh['x'=4,'core'=2,'z1'=2,'z0'=2,'y'=4,'zhi'=4] {'x','zhi'}, dimensions={0} | all-to-all | bytes 65536 | tf_op jit(solution)/shard_map/all_to_all | solution.py:162
  150.3 2.1 %broadcast_multiply_fusion = f32[16,16,512]{2,1,0:T(8,128)} fusion(f32[512]{0:T(512)S(1)} %divide_bitcast_fusion, f32[16,512]{1,0:T(8,128)S(1)} %bitcast.39, bf16[2,16,16,512]{3,2,1,0:T(8,128)(2,1)} %all-to-all-done.3, s32[]{:T(128)S(6)} %select_n.34, f32[16,16,512]{2,1,0:T(8,128)} %copy-done, bf16[16,16,512]{2,1,0:T(8,128)(2,1)S(1)} %collective-permute-done.7), kind=kLoop, calls=%fused_computation.10 | loop fusion | flops 917504 | bytes 1607684 | tf_op jit(solution)/shard_map/mul | solution.py:258
  (37 shorter events, 6.2 us)
Async XLA Ops:
  6.5 1.2 copy-start.1
  7.8 0.8 copy-start.2
  10.8 25.2 %all-to-all-start = ((bf16[32,64,256]{2,1,0:T(8,128)(2,1)}), bf16[32,64,256]{2,1,0:T(8,128)(2,1)S(1)}, u32[]{:S(2)}, u32[]{:S(2)}) async-start(bf16[32,64,256]{2,1,0:T(8,128)(2,1)} %shard_map.37.out_ref), calls=%async_computation | async-start | bytes 2097152 | tf_op jit(solution)/shard_map/all_to_all | solution.py:177
  19.9 72.0 %all-gather.2.cloned.1.call-start = ((), (), s32[]{:S(2)}) async-start(), calls=%async_computation.5 | async-start | bytes 2359296 | tf_op jit(solution)/shard_map/all_gather | solution.py:203
  21.8 10.5 %collective-permute-start = (bf16[64,2048]{1,0:T(8,128)(2,1)S(1)}, bf16[64,2048]{1,0:T(8,128)(2,1)S(1)}, u32[]{:S(2)}, u32[]{:S(2)}) collective-permute-start(bf16[64,2048]{1,0:T(8,128)(2,1)S(1)} %get-tuple-element.31), channel_id=1, source_target_pairs={{0,51},{48,1},{16,32},{32,16},{1,48},{49,2},{17,33},{33,17},{2,49}... | collective-permute-start | bytes 786440 | tf_op jit(solution)/shard_map/ppermute | solution.py:179
  25.2 10.9 %collective-permute-start.2 = (bf16[64,2048]{1,0:T(8,128)(2,1)S(1)}, bf16[64,2048]{1,0:T(8,128)(2,1)S(1)}, u32[]{:S(2)}, u32[]{:S(2)}) collective-permute-start(bf16[64,2048]{1,0:T(8,128)(2,1)S(1)} %get-tuple-element.29), channel_id=1, source_target_pairs={{0,115},{48,65},{16,96},{32,80},{1,112},{49,66},{17,97},{33,81},{2... | collective-permute-start | bytes 786440 | tf_op jit(solution)/shard_map/ppermute | solution.py:180
  32.3 3.8 %collective-permute-start.1 = (bf16[64,2048]{1,0:T(8,128)(2,1)S(1)}, bf16[64,2048]{1,0:T(8,128)(2,1)S(1)}, u32[]{:S(2)}, u32[]{:S(2)}) collective-permute-start(bf16[64,2048]{1,0:T(8,128)(2,1)S(1)} %get-tuple-element.17), channel_id=1, source_target_pairs={{0,64},{64,0},{1,65},{65,1},{2,66},{66,2},{3,67},{67,3},{4,68},{68... | collective-permute-start | bytes 786440 | tf_op jit(solution)/shard_map/ppermute | solution.py:158
  38.8 28.8 %collective-permute-start.3 = (bf16[256,2048]{1,0:T(8,128)(2,1)S(1)}, bf16[256,2048]{1,0:T(8,128)(2,1)S(1)}, u32[]{:S(2)}, u32[]{:S(2)}) collective-permute-start(bf16[256,2048]{1,0:T(8,128)(2,1)S(1)} %bitcast.32), channel_id=1, source_target_pairs={{0,128},{128,256},{256,384},{384,0},{1,129},{129,257},{257,385},{3... | collective-permute-start | bytes 3145736 | tf_op jit(solution)/shard_map/ppermute | solution.py:205
  42.2 27.3 %collective-permute-start.4 = (bf16[256,2048]{1,0:T(8,128)(2,1)S(1)}, bf16[256,2048]{1,0:T(8,128)(2,1)S(1)}, u32[]{:S(2)}, u32[]{:S(2)}) collective-permute-start(bf16[256,2048]{1,0:T(8,128)(2,1)S(1)} %bitcast.33), channel_id=1, source_target_pairs={{0,384},{128,0},{256,128},{384,256},{1,385},{129,1},{257,129},{385... | collective-permute-start | bytes 3145736 | tf_op jit(solution)/shard_map/ppermute | solution.py:205
  70.3 19.6 %collective-permute-start.5 = (bf16[128,2048]{1,0:T(8,128)(2,1)}, bf16[128,2048]{1,0:T(8,128)(2,1)}, u32[]{:S(2)}, u32[]{:S(2)}) collective-permute-start(bf16[128,2048]{1,0:T(8,128)(2,1)} %slice.30), channel_id=1, source_target_pairs={{0,128},{128,256},{256,384},{384,0},{1,129},{129,257},{257,385},{3... | collective-permute-start | bytes 1572872 | tf_op jit(solution)/shard_map/ppermute | solution.py:205
  74.5 15.4 %collective-permute-start.6 = (bf16[128,2048]{1,0:T(8,128)(2,1)}, bf16[128,2048]{1,0:T(8,128)(2,1)}, u32[]{:S(2)}, u32[]{:S(2)}) collective-permute-start(bf16[128,2048]{1,0:T(8,128)(2,1)} %slice.31), channel_id=1, source_target_pairs={{0,384},{128,0},{256,128},{384,256},{1,385},{129,1},{257,129},{385... | collective-permute-start | bytes 1572872 | tf_op jit(solution)/shard_map/ppermute | solution.py:205
  95.0 8.6 %copy-start.3 = (s32[64,64]{1,0:T(8,128)S(1)}, s32[64,64]{1,0:T(8,128)}, u32[]{:S(2)}) copy-start(s32[64,64]{1,0:T(8,128)} %param.5) | copy-start | bytes 49156
  95.1 3.4 %collective-permute-start.8 = (bf16[16,16,512]{2,1,0:T(8,128)(2,1)S(1)}, bf16[16,16,512]{2,1,0:T(8,128)(2,1)S(1)}, u32[]{:S(2)}, u32[]{:S(2)}) collective-permute-start(bf16[16,16,512]{2,1,0:T(8,128)(2,1)S(1)} %get-tuple-element.28), channel_id=1, source_target_pairs={{0,64},{64,0},{1,65},{65,1},{2,66},{66,2},{3,67},{67,3},{4,68},{68... | collective-permute-start | bytes 786440 | tf_op jit(solution)/shard_map/ppermute | solution.py:158
  99.4 19.5 %all-to-all-start.3 = ((bf16[2,16,16,512]{3,2,1,0:T(8,128)(2,1)}), bf16[2,16,16,512]{3,2,1,0:T(8,128)(2,1)}, u32[]{:S(2)}, u32[]{:S(2)}) async-start(bf16[2,16,16,512]{3,2,1,0:T(8,128)(2,1)} %pad_maximum_fusion), calls=%async_computation.3 | async-start | bytes 1048576 | tf_op jit(solution)/shard_map/all_to_all | solution.py:240
  107.8 0.8 copy-start
  108.6 3.4 %collective-permute-start.7 = (bf16[16,16,512]{2,1,0:T(8,128)(2,1)S(1)}, bf16[16,16,512]{2,1,0:T(8,128)(2,1)S(1)}, u32[]{:S(2)}, u32[]{:S(2)}) collective-permute-start(bf16[16,16,512]{2,1,0:T(8,128)(2,1)S(1)} %get-tuple-element.26), channel_id=1, source_target_pairs={{0,64},{64,0},{1,65},{65,1},{2,66},{66,2},{3,67},{67,3},{4,68},{68... | collective-permute-start | bytes 786440 | tf_op jit(solution)/shard_map/ppermute | solution.py:158
Sparse Core Ops, SparseCore 0:
  38.9 52.9 all-gather.1

commit v6 on v5

--- a/solution.py
+++ b/solution.py
@@ -99,16 +99,20 @@
         sum_ref[...] = jnp.sum(acc.T, axis=0, keepdims=True)
 
 
-def product_kernel(group, left_ref, *refs):
-    *right_refs, degree_ref, mine_ref, theirs_ref, right = refs
+def product_kernel(group, ny, *refs):
+    left_refs, refs = refs[:ny], refs[ny:]
+    *right_refs, degree_ref, mine_ref, theirs_ref, left, right = refs
     if len(right_refs) == 5:
         own_ref, before_ref, far0_ref, far1_ref, after_ref = right_refs
         right_refs = [(own_ref,) * 2, (before_ref,) * 2, (far0_ref, far1_ref), (after_ref,) * 2]
     else:
         right_refs = [(ref,) * 2 for ref in right_refs]
-    x_id, core, z1, _, _, _ = where_am_i()
-    nx, ny = lax.axis_size("x"), lax.axis_size("y")
-    part = left_ref.shape[0] // (8 * ny)
+    x_id, core, z1, z0, y_id, _ = where_am_i()
+    nx = lax.axis_size("x")
+    lines = left_refs[0].shape[0]
+    part = lines // 8
+    for i, ref in enumerate(left_refs):
+        left[i * lines : (i + 1) * lines, :] = ref[...]
     inverse = 1.0 / degree_ref[...]
     n = BLK // 2
     for d, pair in enumerate(right_refs):
@@ -118,15 +122,15 @@
             rows = slice(d * BLK + core_rows * n, d * BLK + (core_rows + 1) * n)
             right[rows, :] = (block * inverse).astype(BF16)
     value = lax.dot_general(
-        left_ref[...], right[...], (((1,), (1,)), ((), ())), preferred_element_type=F32
+        left[...], right[...], (((1,), (1,)), ((), ())), preferred_element_type=F32
     )
     value = value.reshape(8 * ny, part, right.shape[0])
     for sel in range(2):
-        low = jnp.where(z1 == sel, 0, 1)
+        low = jnp.where((z0 + z1) % 2 == sel, 0, 1)
         for y in range(ny):
             for b in range(2):
-                c = jnp.where(b == 0, low, 3 - low) * ny + y
-                spot = ((sel * ny + y) * 2 + b) * 2
+                c = jnp.where(b == 0, low, 3 - low) * ny + (y_id - y + ny) % ny
+                spot = ((y * 2 + sel) * 2 + b) * 2
                 first, second = value[spot], value[spot + 1]
                 mine = jnp.where(core == 0, first, second)
                 theirs = jnp.where(core == 0, second, first).astype(BF16)
@@ -200,40 +204,45 @@
             pltpu.VMEM((4, rows_dev, BLK), F32),
         ],
     )(received, *direct)
-    rows = lax.all_gather(shard, ("z0", "y"), axis=0, tiled=True)
+    near = jnp.concatenate([shard, lax.ppermute(shard, "z0", SWAP)], axis=0)
     def step_x(piece, d):
         return lax.ppermute(piece, "x", [(i, (i + d) % nx) for i in range(nx)])
 
-    partial = row_sum.reshape(2, 2, rows_dev).transpose(1, 0, 2)
-    partial = jnp.broadcast_to(partial[:, :, None, None], (2, 2, 2, ny, rows_dev))
+    partial = row_sum.reshape(1, 2, 2, 1, 1, rows_dev).transpose(0, 2, 1, 3, 4, 5)
+    partial = jnp.broadcast_to(partial, (nx, 2, 2, 2, ny, rows_dev))
     partial = lax.all_to_all(
-        partial.reshape(8 * ny, rows_dev),
-        ("core", "z1", "z0", "y"),
+        partial.reshape(2 * members * 2, rows_dev),
+        ("x", "core", "z1", "z0", "y"),
         split_axis=0,
         concat_axis=0,
         tiled=True,
     )
+    partial = jnp.sum(partial.reshape(nx, 2, 2, 2, ny, rows_dev), axis=1)
+    degree = jnp.where(
+        z1 == 0,
+        partial[:, 0] + partial[:, 1, ::-1],
+        partial[:, 1] + partial[:, 0, ::-1],
+    ).reshape(1, inner)
+    rows = [near] + [
+        lax.ppermute(near, "y", [(i, (i + d) % ny) for i in range(ny)]) for d in range(1, ny)
+    ]
+
     own_block = block.reshape(2 * BLK, inner)
     blocks = [own_block, step_x(own_block, 1)]
     if nx == 4:
         after = step_x(own_block, -1)
-        before, after, partial = lax.optimization_barrier((blocks[1], after, partial))
+        before = blocks[1]
         blocks = [own_block, before, step_x(before[:BLK], 1), step_x(after[BLK:], -1), after]
-    partial = jnp.sum(partial.reshape(2, 2, 2, ny, rows_dev), axis=0)
-    degree = jnp.where(
-        z1 == 0, partial[0] + partial[1, ::-1], partial[1] + partial[0, ::-1]
-    )
-    degree = spread(degree.reshape(-1, BLK), "x", nx).reshape(1, inner)
     tile_cols = nx * BLK
 
     def product(group):
         return call(
-            functools.partial(product_kernel, group),
-            in_specs=[vmem] * (len(blocks) + 2),
+            functools.partial(product_kernel, group, ny),
+            in_specs=[vmem] * (ny + len(blocks) + 1),
             out_specs=[vmem] * 2,
             out_shape=[shape((nc, part, tile_cols), t) for t in (F32, BF16)],
-            scratch_shapes=[pltpu.VMEM((tile_cols, inner), BF16)],
-        )(rows, *blocks, degree)
+            scratch_shapes=[pltpu.VMEM((ny * near.shape[0], inner), BF16), pltpu.VMEM((tile_cols, inner), BF16)],
+        )(*rows, *blocks, degree)
 
     mine, theirs = product(1)
     sent = (mine + other_core(theirs).astype(F32)).astype(BF16)

time: 160 us -> 150 us (0.938)
  blocking collectives: 60.5 us -> 28.3 us
  starting transfers between devices: 38.6 us -> 68.3 us
  between operations: 13.6 us -> 0.3 us
  waiting for transfers between devices: 21.2 us -> 25.9 us
  local copies, waits for them, and re-layouts: 7.45 us -> 9.19 us
    ppermute x0 -> x4, starting transfers between devices: none -> 21.3 us  [the longest x3 11.3 us: on_device(): lax.ppermute(near, 'y', [(i, (i + d) % ny) for i in range(ny)])]
    all_to_all x1 -> x0, blocking collectives: 18.8 us -> none  [on_device(): lax.all_to_all(partial.reshape(8 * ny, rows_dev), ('core', 'z1', 'z0', 'y...]
    all_to_all x2 -> x1, blocking collectives: 39.3 us -> 25.9 us  [spread(): return lax.all_to_all(wide, axes, split_axis=0, concat_axis=0, tiled=True)]
    ppermute x0 -> x4, waiting for transfers between devices: none -> 9.62 us  [the longest x3 9.61 us: on_device(): lax.ppermute(near, 'y', [(i, (i + d) % ny) for i in range(ny)])]
    all_to_all x0 -> x1, starting transfers between devices: none -> 8.27 us  [on_device(): lax.all_to_all(partial.reshape(2 * members * 2, rows_dev), ('x', 'core',...]
    all_gather x1 -> x0, waiting for transfers between devices: 1.97 us -> none  [on_device(): rows = lax.all_gather(shard, ('z0', 'y'), axis=0, tiled=True)]
    ppermute x4, waiting for transfers between devices: 3.6 us -> 1.79 us  [step_x(): return lax.ppermute(piece, 'x', [(i, (i + d) % nx) for i in range(nx)])]
  transfers between devices with their start and end apart: 12 -> 16, of which waited for: 8 -> 8; matrix products, arithmetic and copies ran while one was open for 3% -> 5% of each run, Pallas kernels for 3% -> 3%
where the time goes in v6:
time: 150 us; the launch traced here: 149 us
  starting transfers between devices  68.3 us (46%)
  blocking collectives  28.3 us (19%)
  waiting for transfers between devices  25.9 us (17%)
  Pallas kernels  12.3 us (8%)
  local copies, waits for them, and re-layouts  9.19 us (6%)
  other arithmetic  4.84 us (3%)
    all_to_all x1, blocking collectives, spread(): return lax.all_to_all(wide, axes, split_axis=0, concat_axis=0, tiled=True)  25.9 us
    ppermute x4, starting transfers between devices, step_x(): return lax.ppermute(piece, 'x', [(i, (i + d) % nx) for i in range(nx)])  14.1 us
    ppermute x3, starting transfers between devices, on_device(): lax.ppermute(near, 'y', [(i, (i + d) % ny) for i in range(ny)])  11.3 us
    ppermute x1, starting transfers between devices, on_device(): near = jnp.concatenate([shard, lax.ppermute(shard, 'z0', SWAP)], axis=0)  9.94 us
    ppermute x3, waiting for transfers between devices, on_device(): lax.ppermute(near, 'y', [(i, (i + d) % ny) for i in range(ny)])  9.61 us
    all_to_all x1, starting transfers between devices, on_device(): lax.all_to_all(outgoing, group, split_axis=0, concat_axis=0, tiled=True)  9.08 us
    all_to_all x1, starting transfers between devices, on_device(): lax.all_to_all(partial.reshape(2 * members * 2, rows_dev), ('x', 'core',...  8.27 us
    pallas_call x2, Pallas kernels, product(): call(functools.partial(product_kernel, group, ny), in_specs=[vmem] * (ny...  6.39 us
  transfers between devices with their start and end apart: 16, of which 8 were waited for; matrix products, arithmetic and copies ran while one was open for 5% of the time, Pallas kernels for 3%

profile of v6, /device:TPU:32, one launch (start us, length us, event | category | flops | bytes accessed | tf_op | source)
XLA Modules:
  0.0 149.2 jit_solution(14653402533320758980)
XLA Ops:
  2.0 2.3 %shard_map.37.out_ref = bf16[32,64,256]{2,1,0:T(8,128)(2,1)} custom-call(s32[64,64]{1,0:T(8,128)S(1)} %copy-done.3, bf16[1,64,8192]{2,1,0:T(8,128)(2,1)S(1)} %copy-done.2), custom_call_target="tpu_custom_call" | custom-call | tf_op jit(solution)/shard_map/pallas_call | solution.py:175
  4.3 9.1 %all-to-all-start = ((bf16[32,64,256]{2,1,0:T(8,128)(2,1)}), bf16[32,64,256]{2,1,0:T(8,128)(2,1)S(1)}, u32[]{:S(2)}, u32[]{:S(2)}) async-start(bf16[32,64,256]{2,1,0:T(8,128)(2,1)} %shard_map.37.out_ref), calls=%async_computation | async-start | bytes 2097152 | tf_op jit(solution)/shard_map/all_to_all | solution.py:181
  13.4 1.7 %shard_map.38 = bf16[4,64,2048]{2,1,0:T(8,128)(2,1)S(1)} custom-call(bf16[32,64,256]{2,1,0:T(8,128)(2,1)} %shard_map.37.out_ref), custom_call_target="tpu_custom_call" | custom-call | tf_op jit(solution)/shard_map/pallas_call | solution.py:182
  15.2 3.4 %collective-permute-start = (bf16[64,2048]{1,0:T(8,128)(2,1)S(1)}, bf16[64,2048]{1,0:T(8,128)(2,1)S(1)}, u32[]{:S(2)}, u32[]{:S(2)}) collective-permute-start(bf16[64,2048]{1,0:T(8,128)(2,1)S(1)} %get-tuple-element.25), channel_id=1, source_target_pairs={{0,51},{48,1},{16,32},{32,16},{1,48},{49,2},{17,33},{33,17},{2,49}... | collective-permute-start | bytes 786440 | tf_op jit(solution)/shard_map/ppermute | solution.py:183
  18.6 1.9 %collective-permute-start.2 = (bf16[64,2048]{1,0:T(8,128)(2,1)S(1)}, bf16[64,2048]{1,0:T(8,128)(2,1)S(1)}, u32[]{:S(2)}, u32[]{:S(2)}) collective-permute-start(bf16[64,2048]{1,0:T(8,128)(2,1)S(1)} %get-tuple-element.23), channel_id=1, source_target_pairs={{0,115},{48,65},{16,96},{32,80},{1,112},{49,66},{17,97},{33,81},{2... | collective-permute-start | bytes 786440 | tf_op jit(solution)/shard_map/ppermute | solution.py:184
  20.5 5.1 %collective-permute-done.d10 = bf16[64,2048]{1,0:T(8,128)(2,1)S(1)} collective-permute-done((bf16[64,2048]{1,0:T(8,128)(2,1)S(1)}, bf16[64,2048]{1,0:T(8,128)(2,1)S(1)}, u32[]{:S(2)}, u32[]{:S(2)}) %collective-permute-start) | collective-permute-done | bytes 262176 | tf_op jit(solution)/shard_map/ppermute | solution.py:183
  25.7 1.9 %collective-permute-start.1 = (bf16[64,2048]{1,0:T(8,128)(2,1)S(1)}, bf16[64,2048]{1,0:T(8,128)(2,1)S(1)}, u32[]{:S(2)}, u32[]{:S(2)}) collective-permute-start(bf16[64,2048]{1,0:T(8,128)(2,1)S(1)} %get-tuple-element.14), channel_id=1, source_target_pairs={{0,64},{64,0},{1,65},{65,1},{2,66},{66,2},{3,67},{67,3},{4,68},{68... | collective-permute-start | bytes 786440 | tf_op jit(solution)/shard_map/ppermute | solution.py:162
  27.6 1.9 %collective-permute-done.2.d11 = bf16[64,2048]{1,0:T(8,128)(2,1)S(1)} collective-permute-done((bf16[64,2048]{1,0:T(8,128)(2,1)S(1)}, bf16[64,2048]{1,0:T(8,128)(2,1)S(1)}, u32[]{:S(2)}, u32[]{:S(2)}) %collective-permute-start.2) | collective-permute-done | bytes 262176 | tf_op jit(solution)/shard_map/ppermute | solution.py:184
  29.5 1.9 %shard_map.39 = (bf16[4,64,2048]{2,1,0:T(8,128)(2,1)S(1)}, bf16[64,2048]{1,0:T(8,128)(2,1)S(1)}, f32[1,256]{1,0:T(1,128)S(1)}) custom-call(bf16[32,64,256]{2,1,0:T(8,128)(2,1)S(1)} %all-to-all-done.recv_ref, bf16[64,2048]{1,0:T(8,128)(2,1)S(1)} %get-tuple-element.26.d00, bf16[64,2048]{1,0:T(8,128)(2,1)S(1)} %collective-permute-done.1.d01, ...), custom_call_target="tpu_custom_call" | custom-call | tf_op jit(solution)/shard_map/pallas_call | solution.py:187
  31.4 3.4 %collective-permute-start.7 = (bf16[256,2048]{1,0:T(8,128)(2,1)S(1)}, bf16[256,2048]{1,0:T(8,128)(2,1)S(1)}, u32[]{:S(2)}, u32[]{:S(2)}) collective-permute-start(bf16[256,2048]{1,0:T(8,128)(2,1)S(1)} %bitcast.32), channel_id=1, source_target_pairs={{0,128},{128,256},{256,384},{384,0},{1,129},{129,257},{257,385},{3... | collective-permute-start | bytes 3145736 | tf_op jit(solution)/shard_map/ppermute | solution.py:209
  34.9 3.6 %collective-permute-start.9 = (bf16[256,2048]{1,0:T(8,128)(2,1)S(1)}, bf16[256,2048]{1,0:T(8,128)(2,1)}, u32[]{:S(2)}, u32[]{:S(2)}) collective-permute-start(bf16[256,2048]{1,0:T(8,128)(2,1)S(1)} %bitcast.33), channel_id=1, source_target_pairs={{0,384},{128,0},{256,128},{384,256},{1,385},{129,1},{257,129},{385... | collective-permute-start | bytes 3145736 | tf_op jit(solution)/shard_map/ppermute | solution.py:209
  38.5 9.9 %collective-permute-start.3 = (bf16[64,2048]{1,0:T(8,128)(2,1)S(1)}, bf16[64,2048]{1,0:T(8,128)(2,1)S(1)}, u32[]{:S(2)}, u32[]{:S(2)}) collective-permute-start(bf16[64,2048]{1,0:T(8,128)(2,1)S(1)} %get-tuple-element.16), channel_id=1, source_target_pairs={{0,16},{16,0},{1,17},{17,1},{2,18},{18,2},{3,19},{19,3},{4,20},{20... | collective-permute-start | bytes 786440 | tf_op jit(solution)/shard_map/ppermute | solution.py:207
  50.4 8.3 %all-to-all-start.1 = ((f32[128,1,64]{2,1,0:T(1,128)}), f32[128,1,64]{2,1,0:T(1,128)S(1)}, u32[]{:S(2)}, u32[]{:S(2)}) async-start(f32[128,1,64]{2,1,0:T(1,128)} %bitcast.7), calls=%async_computation.1 | async-start | bytes 131072 | tf_op jit(solution)/shard_map/all_to_all | solution.py:213
  58.7 3.4 %collective-permute-start.4 = (bf16[128,2048]{1,0:T(8,128)(2,1)S(1)}, bf16[128,2048]{1,0:T(8,128)(2,1)S(1)}, u32[]{:S(2)}, u32[]{:S(2)}) collective-permute-start(bf16[128,2048]{1,0:T(8,128)(2,1)S(1)} %constant_dynamic-update-slice_fusion.refs_0_), channel_id=1, source_target_pairs={{0,4},{4,8},{8,12},{12,0},{1,5},{5,9},{9,13},{13,1},{2,6},{6,10},{... | collective-permute-start | bytes 1572872 | tf_op jit(solution)/shard_map/ppermute | solution.py:227
  62.1 4.6 %collective-permute-start.5 = (bf16[128,2048]{1,0:T(8,128)(2,1)S(1)}, bf16[128,2048]{1,0:T(8,128)(2,1)}, u32[]{:S(2)}, u32[]{:S(2)}) collective-permute-start(bf16[128,2048]{1,0:T(8,128)(2,1)S(1)} %constant_dynamic-update-slice_fusion.refs_0_), channel_id=1, source_target_pairs={{0,8},{4,12},{8,0},{12,4},{1,9},{5,13},{9,1},{13,5},{2,10},{6,14},... | collective-permute-start | bytes 1572872 | tf_op jit(solution)/shard_map/ppermute | solution.py:227
  66.7 3.4 %collective-permute-start.6 = (bf16[128,2048]{1,0:T(8,128)(2,1)S(1)}, bf16[128,2048]{1,0:T(8,128)(2,1)}, u32[]{:S(2)}, u32[]{:S(2)}) collective-permute-start(bf16[128,2048]{1,0:T(8,128)(2,1)S(1)} %constant_dynamic-update-slice_fusion.refs_0_), channel_id=1, source_target_pairs={{0,12},{4,0},{8,4},{12,8},{1,13},{5,1},{9,5},{13,9},{2,14},{6,2},{... | collective-permute-start | bytes 1572872 | tf_op jit(solution)/shard_map/ppermute | solution.py:227
  70.9 3.5 %collective-permute-start.8 = (bf16[128,2048]{1,0:T(8,128)(2,1)}, bf16[128,2048]{1,0:T(8,128)(2,1)}, u32[]{:S(2)}, u32[]{:S(2)}) collective-permute-start(bf16[128,2048]{1,0:T(8,128)(2,1)} %slice.38), channel_id=1, source_target_pairs={{0,128},{128,256},{256,384},{384,0},{1,129},{129,257},{257,385},{3... | collective-permute-start | bytes 1572872 | tf_op jit(solution)/shard_map/ppermute | solution.py:209
  74.4 1.9 %slice.39 = bf16[128,2048]{1,0:T(8,128)(2,1)} slice(bf16[256,2048]{1,0:T(8,128)(2,1)} %collective-permute-done.9.refs_8_), slice={[128:256], [0:2048]} | slice | bytes 1048576 | tf_op jit(solution)/shard_map/slice | solution.py:235
  76.3 3.6 %collective-permute-start.10 = (bf16[128,2048]{1,0:T(8,128)(2,1)}, bf16[128,2048]{1,0:T(8,128)(2,1)}, u32[]{:S(2)}, u32[]{:S(2)}) collective-permute-start(bf16[128,2048]{1,0:T(8,128)(2,1)} %slice.39), channel_id=1, source_target_pairs={{0,384},{128,0},{256,128},{384,256},{1,385},{129,1},{257,129},{385... | collective-permute-start | bytes 1572872 | tf_op jit(solution)/shard_map/ppermute | solution.py:209
  80.0 8.3 %collective-permute-done.5.refs_2_ = bf16[128,2048]{1,0:T(8,128)(2,1)} collective-permute-done((bf16[128,2048]{1,0:T(8,128)(2,1)S(1)}, bf16[128,2048]{1,0:T(8,128)(2,1)}, u32[]{:S(2)}, u32[]{:S(2)}) %collective-permute-start.5) | collective-permute-done | bytes 524320 | tf_op jit(solution)/shard_map/ppermute | solution.py:227
  88.3 1.4 collective-permute-done.6.refs_3_
  89.7 1.8 %collective-permute-done.10.refs_7_ = bf16[128,2048]{1,0:T(8,128)(2,1)} collective-permute-done((bf16[128,2048]{1,0:T(8,128)(2,1)}, bf16[128,2048]{1,0:T(8,128)(2,1)}, u32[]{:S(2)}, u32[]{:S(2)}) %collective-permute-start.10) | collective-permute-done | bytes 524320 | tf_op jit(solution)/shard_map/ppermute | solution.py:209
  91.4 3.2 %shard_map.41 = (f32[16,16,512]{2,1,0:T(8,128)S(1)}, bf16[16,16,512]{2,1,0:T(8,128)(2,1)S(1)}) custom-call(bf16[128,2048]{1,0:T(8,128)(2,1)S(1)} %constant_dynamic-update-slice_fusion.refs_0_, bf16[128,2048]{1,0:T(8,128)(2,1)S(1)} %collective-permute-done.4.refs_1_, bf16[128,2048]{1,0:T(8,128)(2,1)} %collective-permute-done.5.refs_2_, ...), custom_call_target="tpu_custom_call" | custom-call | tf_op jit(solution)/shard_map/pallas_call | solution.py:239
  94.6 1.9 %collective-permute-start.12 = (bf16[16,16,512]{2,1,0:T(8,128)(2,1)S(1)}, bf16[16,16,512]{2,1,0:T(8,128)(2,1)S(1)}, u32[]{:S(2)}, u32[]{:S(2)}) collective-permute-start(bf16[16,16,512]{2,1,0:T(8,128)(2,1)S(1)} %get-tuple-element.22), channel_id=1, source_target_pairs={{0,64},{64,0},{1,65},{65,1},{2,66},{66,2},{3,67},{67,3},{4,68},{68... | collective-permute-start | bytes 786440 | tf_op jit(solution)/shard_map/ppermute | solution.py:162
  96.6 1.5 %collective-permute-done.12 = bf16[16,16,512]{2,1,0:T(8,128)(2,1)S(1)} collective-permute-done((bf16[16,16,512]{2,1,0:T(8,128)(2,1)S(1)}, bf16[16,16,512]{2,1,0:T(8,128)(2,1)S(1)}, u32[]{:S(2)}, u32[]{:S(2)}) %collective-permute-start.12) | collective-permute-done | bytes 262176 | tf_op jit(solution)/shard_map/ppermute | solution.py:162
  99.0 4.3 %all-to-all-start.2 = ((bf16[2,16,16,512]{3,2,1,0:T(8,128)(2,1)}), bf16[2,16,16,512]{3,2,1,0:T(8,128)(2,1)}, u32[]{:S(2)}, u32[]{:S(2)}) async-start(bf16[2,16,16,512]{3,2,1,0:T(8,128)(2,1)} %pad_maximum_fusion), calls=%async_computation.2 | async-start | bytes 1048576 | tf_op jit(solution)/shard_map/all_to_all | solution.py:249
  104.4 3.2 %shard_map.40 = (f32[16,16,512]{2,1,0:T(8,128)S(1)}, bf16[16,16,512]{2,1,0:T(8,128)(2,1)S(1)}) custom-call(bf16[128,2048]{1,0:T(8,128)(2,1)S(1)} %constant_dynamic-update-slice_fusion.refs_0_, bf16[128,2048]{1,0:T(8,128)(2,1)S(1)} %collective-permute-done.4.refs_1_, bf16[128,2048]{1,0:T(8,128)(2,1)} %collective-permute-done.5.refs_2_, ...), custom_call_target="tpu_custom_call" | custom-call | tf_op jit(solution)/shard_map/pallas_call | solution.py:239
  108.4 2.0 %collective-permute-start.11 = (bf16[16,16,512]{2,1,0:T(8,128)(2,1)S(1)}, bf16[16,16,512]{2,1,0:T(8,128)(2,1)S(1)}, u32[]{:S(2)}, u32[]{:S(2)}) collective-permute-start(bf16[16,16,512]{2,1,0:T(8,128)(2,1)S(1)} %get-tuple-element.20), channel_id=1, source_target_pairs={{0,64},{64,0},{1,65},{65,1},{2,66},{66,2},{3,67},{67,3},{4,68},{68... | collective-permute-start | bytes 786440 | tf_op jit(solution)/shard_map/ppermute | solution.py:162
  111.9 5.7 %all-to-all-done.2 = bf16[2,16,16,512]{3,2,1,0:T(8,128)(2,1)} async-done(((bf16[2,16,16,512]{3,2,1,0:T(8,128)(2,1)}), bf16[2,16,16,512]{3,2,1,0:T(8,128)(2,1)}, u32[]{:S(2)}, u32[]{:S(2)}) %all-to-all-start.2) | async-done | bytes 524320 | tf_op jit(solution)/shard_map/all_to_all | solution.py:249
  118.9 2.5 %psum.7 = f32[4,128]{1,0:T(4,128)S(1)} all-reduce(f32[4,128]{1,0:T(4,128)S(1)} %bitcast.40), channel_id=1, replica_groups=mesh['x'=4,'core'=2,'z1'=2,'z0'=2,'y'=4,'zhi'=4] {'core'}, use_global_device_ids=true, to_apply=%region_2.3 | all-reduce | flops 512 | bytes 4096 | tf_op jit(solution)/shard_map/psum | solution.py:265
  121.4 25.9 %all_to_all.24 = f32[16,4,128]{2,1,0:T(4,128)S(1)} all-to-all(f32[16,4,128]{2,1,0:T(4,128)S(1)} %broadcast_in_dim.22), channel_id=1, replica_groups=mesh['x'=4,'core'=2,'z1'=2,'z0'=2,'y'=4,'zhi'=4] {'x','zhi'}, dimensions={0} | all-to-all | bytes 65536 | tf_op jit(solution)/shard_map/all_to_all | solution.py:166
  147.3 1.9 %broadcast_multiply_fusion = f32[16,16,512]{2,1,0:T(8,128)} fusion(f32[512]{0:T(512)S(1)} %divide_bitcast_fusion, f32[16,512]{1,0:T(8,128)S(1)} %bitcast.37, bf16[2,16,16,512]{3,2,1,0:T(8,128)(2,1)} %all-to-all-done.2, s32[]{:T(128)S(6)} %select_n.37, f32[16,16,512]{2,1,0:T(8,128)S(1)} %copy-done.1, bf16[16,16,512]{2,1,0:T(8,128)(2,1)S(1)} %collective-permute-done.11), kind=kLoop, calls=%fused_computation.10 | loop fusion | flops 917504 | bytes 1607684 | tf_op jit(solution)/shard_map/mul | solution.py:267
  (45 shorter events, 10.5 us)
Async XLA Ops:
  0.0 1.2 copy-start.2
  1.2 0.8 copy-start.3
  4.3 25.2 %all-to-all-start = ((bf16[32,64,256]{2,1,0:T(8,128)(2,1)}), bf16[32,64,256]{2,1,0:T(8,128)(2,1)S(1)}, u32[]{:S(2)}, u32[]{:S(2)}) async-start(bf16[32,64,256]{2,1,0:T(8,128)(2,1)} %shard_map.37.out_ref), calls=%async_computation | async-start | bytes 2097152 | tf_op jit(solution)/shard_map/all_to_all | solution.py:181
  15.2 10.5 %collective-permute-start = (bf16[64,2048]{1,0:T(8,128)(2,1)S(1)}, bf16[64,2048]{1,0:T(8,128)(2,1)S(1)}, u32[]{:S(2)}, u32[]{:S(2)}) collective-permute-start(bf16[64,2048]{1,0:T(8,128)(2,1)S(1)} %get-tuple-element.25), channel_id=1, source_target_pairs={{0,51},{48,1},{16,32},{32,16},{1,48},{49,2},{17,33},{33,17},{2,49}... | collective-permute-start | bytes 786440 | tf_op jit(solution)/shard_map/ppermute | solution.py:183
  18.6 10.9 %collective-permute-start.2 = (bf16[64,2048]{1,0:T(8,128)(2,1)S(1)}, bf16[64,2048]{1,0:T(8,128)(2,1)S(1)}, u32[]{:S(2)}, u32[]{:S(2)}) collective-permute-start(bf16[64,2048]{1,0:T(8,128)(2,1)S(1)} %get-tuple-element.23), channel_id=1, source_target_pairs={{0,115},{48,65},{16,96},{32,80},{1,112},{49,66},{17,97},{33,81},{2... | collective-permute-start | bytes 786440 | tf_op jit(solution)/shard_map/ppermute | solution.py:184
  25.7 3.8 %collective-permute-start.1 = (bf16[64,2048]{1,0:T(8,128)(2,1)S(1)}, bf16[64,2048]{1,0:T(8,128)(2,1)S(1)}, u32[]{:S(2)}, u32[]{:S(2)}) collective-permute-start(bf16[64,2048]{1,0:T(8,128)(2,1)S(1)} %get-tuple-element.14), channel_id=1, source_target_pairs={{0,64},{64,0},{1,65},{65,1},{2,66},{66,2},{3,67},{67,3},{4,68},{68... | collective-permute-start | bytes 786440 | tf_op jit(solution)/shard_map/ppermute | solution.py:162
  31.4 38.6 %collective-permute-start.7 = (bf16[256,2048]{1,0:T(8,128)(2,1)S(1)}, bf16[256,2048]{1,0:T(8,128)(2,1)S(1)}, u32[]{:S(2)}, u32[]{:S(2)}) collective-permute-start(bf16[256,2048]{1,0:T(8,128)(2,1)S(1)} %bitcast.32), channel_id=1, source_target_pairs={{0,128},{128,256},{256,384},{384,0},{1,129},{129,257},{257,385},{3... | collective-permute-start | bytes 3145736 | tf_op jit(solution)/shard_map/ppermute | solution.py:209
  34.9 39.5 %collective-permute-start.9 = (bf16[256,2048]{1,0:T(8,128)(2,1)S(1)}, bf16[256,2048]{1,0:T(8,128)(2,1)}, u32[]{:S(2)}, u32[]{:S(2)}) collective-permute-start(bf16[256,2048]{1,0:T(8,128)(2,1)S(1)} %bitcast.33), channel_id=1, source_target_pairs={{0,384},{128,0},{256,128},{384,256},{1,385},{129,1},{257,129},{385... | collective-permute-start | bytes 3145736 | tf_op jit(solution)/shard_map/ppermute | solution.py:209
  38.5 20.2 %collective-permute-start.3 = (bf16[64,2048]{1,0:T(8,128)(2,1)S(1)}, bf16[64,2048]{1,0:T(8,128)(2,1)S(1)}, u32[]{:S(2)}, u32[]{:S(2)}) collective-permute-start(bf16[64,2048]{1,0:T(8,128)(2,1)S(1)} %get-tuple-element.16), channel_id=1, source_target_pairs={{0,16},{16,0},{1,17},{17,1},{2,18},{18,2},{3,19},{19,3},{4,20},{20... | collective-permute-start | bytes 786440 | tf_op jit(solution)/shard_map/ppermute | solution.py:207
  50.4 29.5 %all-to-all-start.1 = ((f32[128,1,64]{2,1,0:T(1,128)}), f32[128,1,64]{2,1,0:T(1,128)S(1)}, u32[]{:S(2)}, u32[]{:S(2)}) async-start(f32[128,1,64]{2,1,0:T(1,128)} %bitcast.7), calls=%async_computation.1 | async-start | bytes 131072 | tf_op jit(solution)/shard_map/all_to_all | solution.py:213
  58.7 21.3 %collective-permute-start.4 = (bf16[128,2048]{1,0:T(8,128)(2,1)S(1)}, bf16[128,2048]{1,0:T(8,128)(2,1)S(1)}, u32[]{:S(2)}, u32[]{:S(2)}) collective-permute-start(bf16[128,2048]{1,0:T(8,128)(2,1)S(1)} %constant_dynamic-update-slice_fusion.refs_0_), channel_id=1, source_target_pairs={{0,4},{4,8},{8,12},{12,0},{1,5},{5,9},{9,13},{13,1},{2,6},{6,10},{... | collective-permute-start | bytes 1572872 | tf_op jit(solution)/shard_map/ppermute | solution.py:227
  62.1 26.2 %collective-permute-start.5 = (bf16[128,2048]{1,0:T(8,128)(2,1)S(1)}, bf16[128,2048]{1,0:T(8,128)(2,1)}, u32[]{:S(2)}, u32[]{:S(2)}) collective-permute-start(bf16[128,2048]{1,0:T(8,128)(2,1)S(1)} %constant_dynamic-update-slice_fusion.refs_0_), channel_id=1, source_target_pairs={{0,8},{4,12},{8,0},{12,4},{1,9},{5,13},{9,1},{13,5},{2,10},{6,14},... | collective-permute-start | bytes 1572872 | tf_op jit(solution)/shard_map/ppermute | solution.py:227
  66.7 23.0 %collective-permute-start.6 = (bf16[128,2048]{1,0:T(8,128)(2,1)S(1)}, bf16[128,2048]{1,0:T(8,128)(2,1)}, u32[]{:S(2)}, u32[]{:S(2)}) collective-permute-start(bf16[128,2048]{1,0:T(8,128)(2,1)S(1)} %constant_dynamic-update-slice_fusion.refs_0_), channel_id=1, source_target_pairs={{0,12},{4,0},{8,4},{12,8},{1,13},{5,1},{9,5},{13,9},{2,14},{6,2},{... | collective-permute-start | bytes 1572872 | tf_op jit(solution)/shard_map/ppermute | solution.py:227
  70.9 18.8 %collective-permute-start.8 = (bf16[128,2048]{1,0:T(8,128)(2,1)}, bf16[128,2048]{1,0:T(8,128)(2,1)}, u32[]{:S(2)}, u32[]{:S(2)}) collective-permute-start(bf16[128,2048]{1,0:T(8,128)(2,1)} %slice.38), channel_id=1, source_target_pairs={{0,128},{128,256},{256,384},{384,0},{1,129},{129,257},{257,385},{3... | collective-permute-start | bytes 1572872 | tf_op jit(solution)/shard_map/ppermute | solution.py:209
  76.3 15.1 %collective-permute-start.10 = (bf16[128,2048]{1,0:T(8,128)(2,1)}, bf16[128,2048]{1,0:T(8,128)(2,1)}, u32[]{:S(2)}, u32[]{:S(2)}) collective-permute-start(bf16[128,2048]{1,0:T(8,128)(2,1)} %slice.39), channel_id=1, source_target_pairs={{0,384},{128,0},{256,128},{384,256},{1,385},{129,1},{257,129},{385... | collective-permute-start | bytes 1572872 | tf_op jit(solution)/shard_map/ppermute | solution.py:209
  94.6 3.4 %collective-permute-start.12 = (bf16[16,16,512]{2,1,0:T(8,128)(2,1)S(1)}, bf16[16,16,512]{2,1,0:T(8,128)(2,1)S(1)}, u32[]{:S(2)}, u32[]{:S(2)}) collective-permute-start(bf16[16,16,512]{2,1,0:T(8,128)(2,1)S(1)} %get-tuple-element.22), channel_id=1, source_target_pairs={{0,64},{64,0},{1,65},{65,1},{2,66},{66,2},{3,67},{67,3},{4,68},{68... | collective-permute-start | bytes 786440 | tf_op jit(solution)/shard_map/ppermute | solution.py:162
  99.0 4.4 %copy-start.4 = (s32[64,64]{1,0:T(8,128)S(1)}, s32[64,64]{1,0:T(8,128)}, u32[]{:S(2)}) copy-start(s32[64,64]{1,0:T(8,128)} %param.5) | copy-start | bytes 49156
  99.0 18.6 %all-to-all-start.2 = ((bf16[2,16,16,512]{3,2,1,0:T(8,128)(2,1)}), bf16[2,16,16,512]{3,2,1,0:T(8,128)(2,1)}, u32[]{:S(2)}, u32[]{:S(2)}) async-start(bf16[2,16,16,512]{3,2,1,0:T(8,128)(2,1)} %pad_maximum_fusion), calls=%async_computation.2 | async-start | bytes 1048576 | tf_op jit(solution)/shard_map/all_to_all | solution.py:249
  107.6 0.8 copy-start
  108.4 3.4 %collective-permute-start.11 = (bf16[16,16,512]{2,1,0:T(8,128)(2,1)S(1)}, bf16[16,16,512]{2,1,0:T(8,128)(2,1)S(1)}, u32[]{:S(2)}, u32[]{:S(2)}) collective-permute-start(bf16[16,16,512]{2,1,0:T(8,128)(2,1)S(1)} %get-tuple-element.20), channel_id=1, source_target_pairs={{0,64},{64,0},{1,65},{65,1},{2,66},{66,2},{3,67},{67,3},{4,68},{68... | collective-permute-start | bytes 786440 | tf_op jit(solution)/shard_map/ppermute | solution.py:162
  117.6 29.7 %copy-start.1 = (f32[16,16,512]{2,1,0:T(8,128)S(1)}, f32[16,16,512]{2,1,0:T(8,128)}, u32[]{:S(2)}) copy-start(f32[16,16,512]{2,1,0:T(8,128)} %copy-done) | copy-start | bytes 1572868

commit v7 on v6

--- a/solution.py
+++ b/solution.py
@@ -35,25 +35,22 @@
                 )
 
 
-def pieces_kernel(out_ref, piece_ref):
-    _, core, z1, _, _, _ = where_am_i()
+def pieces_kernel(flip, out_ref, piece_ref):
+    core, z1 = lax.axis_index("core"), lax.axis_index("z1")
     nx, ny = lax.axis_size("x"), lax.axis_size("y")
     n = out_ref.shape[1]
     low_lanes = lax.broadcasted_iota(jnp.int32, (n, BLK), 1) < n
+    lanes = pl.ds(pl.multiple_of((z1 + flip) % 2 * BLK, BLK), BLK)
     for p in range(nx * ny):
         x, z0, q = p // ny, p % ny // (ny // 2), p % (ny // 2)
+        spot = (x * 2 + (z0 ^ flip)) * ny + 2 * q
+        a = out_ref[spot, :, lanes].astype(F32)
+        b = out_ref[spot + 1, :, lanes].astype(F32)
         cols = slice(p * BLK, (p + 1) * BLK)
-        for half in range(2):
-            low = z0 ^ half
-            spot = (x * 2 + jnp.where(z1 == 0, low, 1 - low)) * ny + 2 * q
-            lanes = slice(half * BLK, (half + 1) * BLK)
-            a = out_ref[spot, :, lanes].astype(F32)
-            b = out_ref[spot + 1, :, lanes].astype(F32)
-            first = jnp.where(low_lanes, a, pltpu.roll(b, n, 1)).astype(BF16)
-            second = jnp.where(low_lanes, pltpu.roll(a, n, 1), b).astype(BF16)
-            i = jnp.where(z1 == half, 0, 1)
-            piece_ref[2 * i + core, :, cols] = first
-            piece_ref[2 * i + 1 - core, :, cols] = second
+        first = jnp.where(low_lanes, a, pltpu.roll(b, n, 1))
+        second = jnp.where(low_lanes, pltpu.roll(a, n, 1), b)
+        piece_ref[core, :, cols] = first.astype(BF16)
+        piece_ref[1 - core, :, cols] = second.astype(BF16)
 
 
 def form_kernel(
@@ -95,8 +92,10 @@
 
     @pl.when(step == pl.num_programs(0) - 1)
     def _():
-        acc = acc_ref[...].reshape(4 * n, BLK)
-        sum_ref[...] = jnp.sum(acc.T, axis=0, keepdims=True)
+        sums = jnp.sum(acc_ref[...].reshape(4 * n, BLK).T, axis=0, keepdims=True)
+        for group in range(4):
+            spot = group % 2 * 2 + group // 2
+            sum_ref[spot : spot + 1, :] = sums[:, group * n : (group + 1) * n]
 
 
 def product_kernel(group, ny, *refs):
@@ -179,11 +178,16 @@
         out_specs=vmem,
     )(block_mask, adjacency)
     received = lax.all_to_all(outgoing, group, split_axis=0, concat_axis=0, tiled=True)
-    pieces = call(pieces_kernel, out_shape=shape((4, rows_dev, inner), BF16))(outgoing)
-    by_ring = lax.ppermute(pieces[2], ("z1", "z0", "zhi"), ring)
-    across = lax.ppermute(pieces[3], ("core", "z1", "z0", "zhi"), ring_across)
-    by_ring, swapped = lax.optimization_barrier((by_ring, pieces[1]))
-    direct = [pieces[0], other_core(swapped), by_ring, across]
+    ring_pieces, core_pieces = (
+        call(
+            functools.partial(pieces_kernel, flip), out_shape=shape((2, rows_dev, inner), BF16)
+        )(outgoing)
+        for flip in (1, 0)
+    )
+    by_ring = lax.ppermute(ring_pieces[0], ("z1", "z0", "zhi"), ring)
+    across = lax.ppermute(ring_pieces[1], ("core", "z1", "z0", "zhi"), ring_across)
+    by_ring, swapped = lax.optimization_barrier((by_ring, core_pieces[1]))
+    direct = [core_pieces[0], other_core(swapped), by_ring, across]
     block, shard, row_sum = call(
         form_kernel,
         grid=(nx,),
@@ -192,12 +196,12 @@
         out_specs=[
             pl.BlockSpec((4, rows_dev, width), lambda i: (0, 0, i)),
             pl.BlockSpec((4 * part, width), lambda i: (0, i)),
-            pl.BlockSpec((1, 4 * rows_dev), lambda i: (0, 0)),
+            pl.BlockSpec((4, rows_dev), lambda i: (0, 0)),
         ],
         out_shape=[
             shape((4, rows_dev, inner), BF16),
             shape((4 * part, inner), BF16),
-            shape((1, 4 * rows_dev), F32),
+            shape((4, rows_dev), F32),
         ],
         scratch_shapes=[
             pltpu.VMEM((4, rows_dev, BLK), F32),
@@ -208,7 +212,7 @@
     def step_x(piece, d):
         return lax.ppermute(piece, "x", [(i, (i + d) % nx) for i in range(nx)])
 
-    partial = row_sum.reshape(1, 2, 2, 1, 1, rows_dev).transpose(0, 2, 1, 3, 4, 5)
+    partial = row_sum.reshape(1, 2, 2, 1, 1, rows_dev)
     partial = jnp.broadcast_to(partial, (nx, 2, 2, 2, ny, rows_dev))
     partial = lax.all_to_all(
         partial.reshape(2 * members * 2, rows_dev),
@@ -261,7 +265,7 @@
     prune = lax.dynamic_index_in_dim(prune, x_id, 1, keepdims=False)
     prune = lax.dynamic_index_in_dim(prune, c_id, 1, keepdims=False)
     prune = jnp.repeat(prune.astype(F32), BLK, axis=1)
-    pruned = summed * summed * prune[:, None, :]
+    pruned = lax.optimization_barrier(summed * summed * prune[:, None, :])
     mass = lax.psum(jnp.sum(pruned, axis=(0, 1)), "core")
     mass = jnp.sum(spread(mass.reshape(-1, BLK), ("x", "zhi"), nx * nl), axis=0).reshape(-1)
     return pruned * (node_count / mass)[None, None, :]

time: 150 us -> 149 us (level)
  blocking collectives: 28.3 us -> 25.7 us
  other arithmetic: 4.84 us -> 3.15 us
    ppermute x4, waiting for transfers between devices: 1.79 us -> 4.64 us  [step_x(): return lax.ppermute(piece, 'x', [(i, (i + d) % nx) for i in range(nx)])]
    all_to_all x1, blocking collectives: 25.9 us -> 23.3 us  [spread(): return lax.all_to_all(wide, axes, split_axis=0, concat_axis=0, tiled=True)]
    ppermute x2, waiting for transfers between devices: 7.03 us -> 5.52 us  [the longest x1 3.62 us: on_device(): by_ring = lax.ppermute(ring_pieces[0], ('z1', 'z0', 'zhi'), ring)]
    unnamed x13 -> x11, local copies, waits for them, and re-layouts: 2.9 us -> 3.62 us
  transfers between devices with their start and end apart: 16 -> 16, of which waited for: 8 -> 8; matrix products, arithmetic and copies ran while one was open for 5% -> 4% of each run, Pallas kernels for 3% -> 4%
where the time goes in v7:
time: 149 us; the launch traced here: 148 us
  starting transfers between devices  69.1 us (46%)
  waiting for transfers between devices  26.5 us (18%)
  blocking collectives  25.7 us (17%)
  Pallas kernels  13.6 us (9%)
  local copies, waits for them, and re-layouts  9.28 us (6%)
  other arithmetic  3.15 us (2%)
    all_to_all x1, blocking collectives, spread(): return lax.all_to_all(wide, axes, split_axis=0, concat_axis=0, tiled=True)  23.3 us
    ppermute x4, starting transfers between devices, step_x(): return lax.ppermute(piece, 'x', [(i, (i + d) % nx) for i in range(nx)])  13.7 us
    ppermute x3, starting transfers between devices, on_device(): lax.ppermute(near, 'y', [(i, (i + d) % ny) for i in range(ny)])  11.3 us
    ppermute x1, starting transfers between devices, on_device(): near = jnp.concatenate([shard, lax.ppermute(shard, 'z0', SWAP)], axis=0)  9.91 us
    all_to_all x1, starting transfers between devices, on_device(): lax.all_to_all(partial.reshape(2 * members * 2, rows_dev), ('x', 'core',...  9.72 us
    ppermute x3, waiting for transfers between devices, on_device(): lax.ppermute(near, 'y', [(i, (i + d) % ny) for i in range(ny)])  9.62 us
    all_to_all x1, starting transfers between devices, on_device(): lax.all_to_all(outgoing, group, split_axis=0, concat_axis=0, tiled=True)  9.08 us
    pallas_call x2, Pallas kernels, product(): call(functools.partial(product_kernel, group, ny), in_specs=[vmem] * (ny...  6.39 us
  transfers between devices with their start and end apart: 16, of which 8 were waited for; matrix products, arithmetic and copies ran while one was open for 4% of the time, Pallas kernels for 4%

profile of v7, /device:TPU:32, one launch (start us, length us, event | category | flops | bytes accessed | tf_op | source)
XLA Modules:
  0.0 147.7 jit_solution(12851555193772384212)
XLA Ops:
  2.0 2.3 %shard_map.37.out_ref = bf16[32,64,256]{2,1,0:T(8,128)(2,1)} custom-call(s32[64,64]{1,0:T(8,128)S(1)} %copy-done.2, bf16[1,64,8192]{2,1,0:T(8,128)(2,1)S(1)} %copy-done), custom_call_target="tpu_custom_call" | custom-call | tf_op jit(solution)/shard_map/pallas_call | solution.py:174
  4.3 9.1 %all-to-all-start = ((bf16[32,64,256]{2,1,0:T(8,128)(2,1)}), bf16[32,64,256]{2,1,0:T(8,128)(2,1)S(1)}, u32[]{:S(2)}, u32[]{:S(2)}) async-start(bf16[32,64,256]{2,1,0:T(8,128)(2,1)} %shard_map.37.out_ref), calls=%async_computation | async-start | bytes 2097152 | tf_op jit(solution)/shard_map/all_to_all | solution.py:180
  13.4 1.5 %shard_map.39 = bf16[2,64,2048]{2,1,0:T(8,128)(2,1)S(1)} custom-call(bf16[32,64,256]{2,1,0:T(8,128)(2,1)} %shard_map.37.out_ref), custom_call_target="tpu_custom_call" | custom-call | tf_op jit(solution)/shard_map/pallas_call | solution.py:182
  14.9 3.4 %collective-permute-start = (bf16[64,2048]{1,0:T(8,128)(2,1)S(1)}, bf16[64,2048]{1,0:T(8,128)(2,1)S(1)}, u32[]{:S(2)}, u32[]{:S(2)}) collective-permute-start(bf16[64,2048]{1,0:T(8,128)(2,1)S(1)} %get-tuple-element.24), channel_id=1, source_target_pairs={{0,51},{48,1},{16,32},{32,16},{1,48},{49,2},{17,33},{33,17},{2,49}... | collective-permute-start | bytes 786440 | tf_op jit(solution)/shard_map/ppermute | solution.py:187
  18.4 1.9 %collective-permute-start.2 = (bf16[64,2048]{1,0:T(8,128)(2,1)S(1)}, bf16[64,2048]{1,0:T(8,128)(2,1)S(1)}, u32[]{:S(2)}, u32[]{:S(2)}) collective-permute-start(bf16[64,2048]{1,0:T(8,128)(2,1)S(1)} %get-tuple-element.23), channel_id=1, source_target_pairs={{0,115},{48,65},{16,96},{32,80},{1,112},{49,66},{17,97},{33,81},{2... | collective-permute-start | bytes 786440 | tf_op jit(solution)/shard_map/ppermute | solution.py:188
  20.3 1.5 shard_map.38
  21.8 3.6 %collective-permute-done.d10 = bf16[64,2048]{1,0:T(8,128)(2,1)S(1)} collective-permute-done((bf16[64,2048]{1,0:T(8,128)(2,1)S(1)}, bf16[64,2048]{1,0:T(8,128)(2,1)S(1)}, u32[]{:S(2)}, u32[]{:S(2)}) %collective-permute-start) | collective-permute-done | bytes 262176 | tf_op jit(solution)/shard_map/ppermute | solution.py:187
  25.4 1.9 %collective-permute-start.1 = (bf16[64,2048]{1,0:T(8,128)(2,1)S(1)}, bf16[64,2048]{1,0:T(8,128)(2,1)S(1)}, u32[]{:S(2)}, u32[]{:S(2)}) collective-permute-start(bf16[64,2048]{1,0:T(8,128)(2,1)S(1)} %get-tuple-element.14), channel_id=1, source_target_pairs={{0,64},{64,0},{1,65},{65,1},{2,66},{66,2},{3,67},{67,3},{4,68},{68... | collective-permute-start | bytes 786440 | tf_op jit(solution)/shard_map/ppermute | solution.py:161
  27.4 1.9 %collective-permute-done.2.d11 = bf16[64,2048]{1,0:T(8,128)(2,1)S(1)} collective-permute-done((bf16[64,2048]{1,0:T(8,128)(2,1)S(1)}, bf16[64,2048]{1,0:T(8,128)(2,1)S(1)}, u32[]{:S(2)}, u32[]{:S(2)}) %collective-permute-start.2) | collective-permute-done | bytes 262176 | tf_op jit(solution)/shard_map/ppermute | solution.py:188
  29.3 2.0 %shard_map.40 = (bf16[4,64,2048]{2,1,0:T(8,128)(2,1)S(1)}, bf16[64,2048]{1,0:T(8,128)(2,1)S(1)}, f32[4,64]{1,0:T(4,128)S(1)}) custom-call(bf16[32,64,256]{2,1,0:T(8,128)(2,1)S(1)} %all-to-all-done.recv_ref, bf16[64,2048]{1,0:T(8,128)(2,1)S(1)} %get-tuple-element.26.d00, bf16[64,2048]{1,0:T(8,128)(2,1)S(1)} %collective-permute-done.1.d01, ...), custom_call_target="tpu_custom_call" | custom-call | tf_op jit(solution)/shard_map/pallas_call | solution.py:191
  31.2 4.7 %collective-permute-start.9 = (bf16[256,2048]{1,0:T(8,128)(2,1)S(1)}, bf16[256,2048]{1,0:T(8,128)(2,1)}, u32[]{:S(2)}, u32[]{:S(2)}) collective-permute-start(bf16[256,2048]{1,0:T(8,128)(2,1)S(1)} %bitcast.26), channel_id=1, source_target_pairs={{0,384},{128,0},{256,128},{384,256},{1,385},{129,1},{257,129},{385... | collective-permute-start | bytes 3145736 | tf_op jit(solution)/shard_map/ppermute | solution.py:213
  35.9 1.9 %collective-permute-start.7 = (bf16[256,2048]{1,0:T(8,128)(2,1)S(1)}, bf16[256,2048]{1,0:T(8,128)(2,1)S(1)}, u32[]{:S(2)}, u32[]{:S(2)}) collective-permute-start(bf16[256,2048]{1,0:T(8,128)(2,1)S(1)} %bitcast.27), channel_id=1, source_target_pairs={{0,128},{128,256},{256,384},{384,0},{1,129},{129,257},{257,385},{3... | collective-permute-start | bytes 3145736 | tf_op jit(solution)/shard_map/ppermute | solution.py:213
  37.9 9.9 %collective-permute-start.3 = (bf16[64,2048]{1,0:T(8,128)(2,1)S(1)}, bf16[64,2048]{1,0:T(8,128)(2,1)S(1)}, u32[]{:S(2)}, u32[]{:S(2)}) collective-permute-start(bf16[64,2048]{1,0:T(8,128)(2,1)S(1)} %get-tuple-element.16), channel_id=1, source_target_pairs={{0,16},{16,0},{1,17},{17,1},{2,18},{18,2},{3,19},{19,3},{4,20},{20... | collective-permute-start | bytes 786440 | tf_op jit(solution)/shard_map/ppermute | solution.py:211
  48.4 9.7 %all-to-all-start.1 = ((f32[128,1,64]{2,1,0:T(1,128)}), f32[128,1,64]{2,1,0:T(1,128)S(1)}, u32[]{:S(2)}, u32[]{:S(2)}) async-start(f32[128,1,64]{2,1,0:T(1,128)} %bitcast.6), calls=%async_computation.1 | async-start | bytes 131072 | tf_op jit(solution)/shard_map/all_to_all | solution.py:217
  58.2 3.4 %collective-permute-start.4 = (bf16[128,2048]{1,0:T(8,128)(2,1)S(1)}, bf16[128,2048]{1,0:T(8,128)(2,1)S(1)}, u32[]{:S(2)}, u32[]{:S(2)}) collective-permute-start(bf16[128,2048]{1,0:T(8,128)(2,1)S(1)} %constant_dynamic-update-slice_fusion.refs_0_), channel_id=1, source_target_pairs={{0,4},{4,8},{8,12},{12,0},{1,5},{5,9},{9,13},{13,1},{2,6},{6,10},{... | collective-permute-start | bytes 1572872 | tf_op jit(solution)/shard_map/ppermute | solution.py:231
  61.6 4.6 %collective-permute-start.5 = (bf16[128,2048]{1,0:T(8,128)(2,1)S(1)}, bf16[128,2048]{1,0:T(8,128)(2,1)}, u32[]{:S(2)}, u32[]{:S(2)}) collective-permute-start(bf16[128,2048]{1,0:T(8,128)(2,1)S(1)} %constant_dynamic-update-slice_fusion.refs_0_), channel_id=1, source_target_pairs={{0,8},{4,12},{8,0},{12,4},{1,9},{5,13},{9,1},{13,5},{2,10},{6,14},... | collective-permute-start | bytes 1572872 | tf_op jit(solution)/shard_map/ppermute | solution.py:231
  66.2 3.4 %collective-permute-start.6 = (bf16[128,2048]{1,0:T(8,128)(2,1)S(1)}, bf16[128,2048]{1,0:T(8,128)(2,1)}, u32[]{:S(2)}, u32[]{:S(2)}) collective-permute-start(bf16[128,2048]{1,0:T(8,128)(2,1)S(1)} %constant_dynamic-update-slice_fusion.refs_0_), channel_id=1, source_target_pairs={{0,12},{4,0},{8,4},{12,8},{1,13},{5,1},{9,5},{13,9},{2,14},{6,2},{... | collective-permute-start | bytes 1572872 | tf_op jit(solution)/shard_map/ppermute | solution.py:231
  69.6 1.9 %slice.39 = bf16[128,2048]{1,0:T(8,128)(2,1)} slice(bf16[256,2048]{1,0:T(8,128)(2,1)} %collective-permute-done.9.refs_8_), slice={[128:256], [0:2048]} | slice | bytes 1048576 | tf_op jit(solution)/shard_map/slice | solution.py:239
  71.4 5.1 %collective-permute-start.10 = (bf16[128,2048]{1,0:T(8,128)(2,1)}, bf16[128,2048]{1,0:T(8,128)(2,1)}, u32[]{:S(2)}, u32[]{:S(2)}) collective-permute-start(bf16[128,2048]{1,0:T(8,128)(2,1)} %slice.39), channel_id=1, source_target_pairs={{0,384},{128,0},{256,128},{384,256},{1,385},{129,1},{257,129},{385... | collective-permute-start | bytes 1572872 | tf_op jit(solution)/shard_map/ppermute | solution.py:213
  77.4 1.9 %collective-permute-start.8 = (bf16[128,2048]{1,0:T(8,128)(2,1)}, bf16[128,2048]{1,0:T(8,128)(2,1)}, u32[]{:S(2)}, u32[]{:S(2)}) collective-permute-start(bf16[128,2048]{1,0:T(8,128)(2,1)} %slice.38), channel_id=1, source_target_pairs={{0,128},{128,256},{256,384},{384,0},{1,129},{129,257},{257,385},{3... | collective-permute-start | bytes 1572872 | tf_op jit(solution)/shard_map/ppermute | solution.py:213
  79.5 8.3 %collective-permute-done.5.refs_2_ = bf16[128,2048]{1,0:T(8,128)(2,1)} collective-permute-done((bf16[128,2048]{1,0:T(8,128)(2,1)S(1)}, bf16[128,2048]{1,0:T(8,128)(2,1)}, u32[]{:S(2)}, u32[]{:S(2)}) %collective-permute-start.5) | collective-permute-done | bytes 524320 | tf_op jit(solution)/shard_map/ppermute | solution.py:231
  87.9 1.3 collective-permute-done.6.refs_3_
  89.2 4.6 %collective-permute-done.8.refs_6_ = bf16[128,2048]{1,0:T(8,128)(2,1)} collective-permute-done((bf16[128,2048]{1,0:T(8,128)(2,1)}, bf16[128,2048]{1,0:T(8,128)(2,1)}, u32[]{:S(2)}, u32[]{:S(2)}) %collective-permute-start.8) | collective-permute-done | bytes 524320 | tf_op jit(solution)/shard_map/ppermute | solution.py:213
  93.8 3.2 %shard_map.42 = (f32[16,16,512]{2,1,0:T(8,128)S(1)}, bf16[16,16,512]{2,1,0:T(8,128)(2,1)S(1)}) custom-call(bf16[128,2048]{1,0:T(8,128)(2,1)S(1)} %constant_dynamic-update-slice_fusion.refs_0_, bf16[128,2048]{1,0:T(8,128)(2,1)S(1)} %collective-permute-done.4.refs_1_, bf16[128,2048]{1,0:T(8,128)(2,1)} %collective-permute-done.5.refs_2_, ...), custom_call_target="tpu_custom_call" | custom-call | tf_op jit(solution)/shard_map/pallas_call | solution.py:243
  97.0 1.9 %collective-permute-start.12 = (bf16[16,16,512]{2,1,0:T(8,128)(2,1)S(1)}, bf16[16,16,512]{2,1,0:T(8,128)(2,1)S(1)}, u32[]{:S(2)}, u32[]{:S(2)}) collective-permute-start(bf16[16,16,512]{2,1,0:T(8,128)(2,1)S(1)} %get-tuple-element.22), channel_id=1, source_target_pairs={{0,64},{64,0},{1,65},{65,1},{2,66},{66,2},{3,67},{67,3},{4,68},{68... | collective-permute-start | bytes 786440 | tf_op jit(solution)/shard_map/ppermute | solution.py:161
  98.9 1.5 %collective-permute-done.12 = bf16[16,16,512]{2,1,0:T(8,128)(2,1)S(1)} collective-permute-done((bf16[16,16,512]{2,1,0:T(8,128)(2,1)S(1)}, bf16[16,16,512]{2,1,0:T(8,128)(2,1)S(1)}, u32[]{:S(2)}, u32[]{:S(2)}) %collective-permute-start.12) | collective-permute-done | bytes 262176 | tf_op jit(solution)/shard_map/ppermute | solution.py:161
  101.3 4.2 %all-to-all-start.2 = ((bf16[2,16,16,512]{3,2,1,0:T(8,128)(2,1)}), bf16[2,16,16,512]{3,2,1,0:T(8,128)(2,1)}, u32[]{:S(2)}, u32[]{:S(2)}) async-start(bf16[2,16,16,512]{3,2,1,0:T(8,128)(2,1)} %pad_maximum_fusion), calls=%async_computation.2 | async-start | bytes 1048576 | tf_op jit(solution)/shard_map/all_to_all | solution.py:253
  107.4 3.2 %shard_map.41 = (f32[16,16,512]{2,1,0:T(8,128)S(1)}, bf16[16,16,512]{2,1,0:T(8,128)(2,1)S(1)}) custom-call(bf16[128,2048]{1,0:T(8,128)(2,1)S(1)} %constant_dynamic-update-slice_fusion.refs_0_, bf16[128,2048]{1,0:T(8,128)(2,1)S(1)} %collective-permute-done.4.refs_1_, bf16[128,2048]{1,0:T(8,128)(2,1)} %collective-permute-done.5.refs_2_, ...), custom_call_target="tpu_custom_call" | custom-call | tf_op jit(solution)/shard_map/pallas_call | solution.py:243
  111.4 2.0 %collective-permute-start.11 = (bf16[16,16,512]{2,1,0:T(8,128)(2,1)S(1)}, bf16[16,16,512]{2,1,0:T(8,128)(2,1)S(1)}, u32[]{:S(2)}, u32[]{:S(2)}) collective-permute-start(bf16[16,16,512]{2,1,0:T(8,128)(2,1)S(1)} %get-tuple-element.20), channel_id=1, source_target_pairs={{0,64},{64,0},{1,65},{65,1},{2,66},{66,2},{3,67},{67,3},{4,68},{68... | collective-permute-start | bytes 786440 | tf_op jit(solution)/shard_map/ppermute | solution.py:161
  114.8 5.0 %all-to-all-done.2 = bf16[2,16,16,512]{3,2,1,0:T(8,128)(2,1)} async-done(((bf16[2,16,16,512]{3,2,1,0:T(8,128)(2,1)}), bf16[2,16,16,512]{3,2,1,0:T(8,128)(2,1)}, u32[]{:S(2)}, u32[]{:S(2)}) %all-to-all-start.2) | async-done | bytes 524320 | tf_op jit(solution)/shard_map/all_to_all | solution.py:253
  121.1 2.5 %psum.7 = f32[4,128]{1,0:T(4,128)S(1)} all-reduce(f32[4,128]{1,0:T(4,128)S(1)} %bitcast.34), channel_id=1, replica_groups=mesh['x'=4,'core'=2,'z1'=2,'z0'=2,'y'=4,'zhi'=4] {'core'}, use_global_device_ids=true, to_apply=%region_2.3 | all-reduce | flops 512 | bytes 4096 | tf_op jit(solution)/shard_map/psum | solution.py:269
  123.6 23.3 %all_to_all.24 = f32[16,4,128]{2,1,0:T(4,128)S(1)} all-to-all(f32[16,4,128]{2,1,0:T(4,128)S(1)} %broadcast_in_dim.22), channel_id=1, replica_groups=mesh['x'=4,'core'=2,'z1'=2,'z0'=2,'y'=4,'zhi'=4] {'x','zhi'}, dimensions={0} | all-to-all | bytes 65536 | tf_op jit(solution)/shard_map/all_to_all | solution.py:165
  (42 shorter events, 10.8 us)
Async XLA Ops:
  0.0 1.2 copy-start
  1.2 0.8 copy-start.2
  4.3 24.9 %all-to-all-start = ((bf16[32,64,256]{2,1,0:T(8,128)(2,1)}), bf16[32,64,256]{2,1,0:T(8,128)(2,1)S(1)}, u32[]{:S(2)}, u32[]{:S(2)}) async-start(bf16[32,64,256]{2,1,0:T(8,128)(2,1)} %shard_map.37.out_ref), calls=%async_computation | async-start | bytes 2097152 | tf_op jit(solution)/shard_map/all_to_all | solution.py:180
  14.9 10.5 %collective-permute-start = (bf16[64,2048]{1,0:T(8,128)(2,1)S(1)}, bf16[64,2048]{1,0:T(8,128)(2,1)S(1)}, u32[]{:S(2)}, u32[]{:S(2)}) collective-permute-start(bf16[64,2048]{1,0:T(8,128)(2,1)S(1)} %get-tuple-element.24), channel_id=1, source_target_pairs={{0,51},{48,1},{16,32},{32,16},{1,48},{49,2},{17,33},{33,17},{2,49}... | collective-permute-start | bytes 786440 | tf_op jit(solution)/shard_map/ppermute | solution.py:187
  18.4 10.9 %collective-permute-start.2 = (bf16[64,2048]{1,0:T(8,128)(2,1)S(1)}, bf16[64,2048]{1,0:T(8,128)(2,1)S(1)}, u32[]{:S(2)}, u32[]{:S(2)}) collective-permute-start(bf16[64,2048]{1,0:T(8,128)(2,1)S(1)} %get-tuple-element.23), channel_id=1, source_target_pairs={{0,115},{48,65},{16,96},{32,80},{1,112},{49,66},{17,97},{33,81},{2... | collective-permute-start | bytes 786440 | tf_op jit(solution)/shard_map/ppermute | solution.py:188
  25.4 3.8 %collective-permute-start.1 = (bf16[64,2048]{1,0:T(8,128)(2,1)S(1)}, bf16[64,2048]{1,0:T(8,128)(2,1)S(1)}, u32[]{:S(2)}, u32[]{:S(2)}) collective-permute-start(bf16[64,2048]{1,0:T(8,128)(2,1)S(1)} %get-tuple-element.14), channel_id=1, source_target_pairs={{0,64},{64,0},{1,65},{65,1},{2,66},{66,2},{3,67},{67,3},{4,68},{68... | collective-permute-start | bytes 786440 | tf_op jit(solution)/shard_map/ppermute | solution.py:161
  31.2 38.3 %collective-permute-start.9 = (bf16[256,2048]{1,0:T(8,128)(2,1)S(1)}, bf16[256,2048]{1,0:T(8,128)(2,1)}, u32[]{:S(2)}, u32[]{:S(2)}) collective-permute-start(bf16[256,2048]{1,0:T(8,128)(2,1)S(1)} %bitcast.26), channel_id=1, source_target_pairs={{0,384},{128,0},{256,128},{384,256},{1,385},{129,1},{257,129},{385... | collective-permute-start | bytes 3145736 | tf_op jit(solution)/shard_map/ppermute | solution.py:213
  35.9 40.7 %collective-permute-start.7 = (bf16[256,2048]{1,0:T(8,128)(2,1)S(1)}, bf16[256,2048]{1,0:T(8,128)(2,1)S(1)}, u32[]{:S(2)}, u32[]{:S(2)}) collective-permute-start(bf16[256,2048]{1,0:T(8,128)(2,1)S(1)} %bitcast.27), channel_id=1, source_target_pairs={{0,128},{128,256},{256,384},{384,0},{1,129},{129,257},{257,385},{3... | collective-permute-start | bytes 3145736 | tf_op jit(solution)/shard_map/ppermute | solution.py:213
  37.9 20.3 %collective-permute-start.3 = (bf16[64,2048]{1,0:T(8,128)(2,1)S(1)}, bf16[64,2048]{1,0:T(8,128)(2,1)S(1)}, u32[]{:S(2)}, u32[]{:S(2)}) collective-permute-start(bf16[64,2048]{1,0:T(8,128)(2,1)S(1)} %get-tuple-element.16), channel_id=1, source_target_pairs={{0,16},{16,0},{1,17},{17,1},{2,18},{18,2},{3,19},{19,3},{4,20},{20... | collective-permute-start | bytes 786440 | tf_op jit(solution)/shard_map/ppermute | solution.py:211
  48.4 31.0 %all-to-all-start.1 = ((f32[128,1,64]{2,1,0:T(1,128)}), f32[128,1,64]{2,1,0:T(1,128)S(1)}, u32[]{:S(2)}, u32[]{:S(2)}) async-start(f32[128,1,64]{2,1,0:T(1,128)} %bitcast.6), calls=%async_computation.1 | async-start | bytes 131072 | tf_op jit(solution)/shard_map/all_to_all | solution.py:217
  58.2 21.3 %collective-permute-start.4 = (bf16[128,2048]{1,0:T(8,128)(2,1)S(1)}, bf16[128,2048]{1,0:T(8,128)(2,1)S(1)}, u32[]{:S(2)}, u32[]{:S(2)}) collective-permute-start(bf16[128,2048]{1,0:T(8,128)(2,1)S(1)} %constant_dynamic-update-slice_fusion.refs_0_), channel_id=1, source_target_pairs={{0,4},{4,8},{8,12},{12,0},{1,5},{5,9},{9,13},{13,1},{2,6},{6,10},{... | collective-permute-start | bytes 1572872 | tf_op jit(solution)/shard_map/ppermute | solution.py:231
  61.6 26.3 %collective-permute-start.5 = (bf16[128,2048]{1,0:T(8,128)(2,1)S(1)}, bf16[128,2048]{1,0:T(8,128)(2,1)}, u32[]{:S(2)}, u32[]{:S(2)}) collective-permute-start(bf16[128,2048]{1,0:T(8,128)(2,1)S(1)} %constant_dynamic-update-slice_fusion.refs_0_), channel_id=1, source_target_pairs={{0,8},{4,12},{8,0},{12,4},{1,9},{5,13},{9,1},{13,5},{2,10},{6,14},... | collective-permute-start | bytes 1572872 | tf_op jit(solution)/shard_map/ppermute | solution.py:231
  66.2 23.0 %collective-permute-start.6 = (bf16[128,2048]{1,0:T(8,128)(2,1)S(1)}, bf16[128,2048]{1,0:T(8,128)(2,1)}, u32[]{:S(2)}, u32[]{:S(2)}) collective-permute-start(bf16[128,2048]{1,0:T(8,128)(2,1)S(1)} %constant_dynamic-update-slice_fusion.refs_0_), channel_id=1, source_target_pairs={{0,12},{4,0},{8,4},{12,8},{1,13},{5,1},{9,5},{13,9},{2,14},{6,2},{... | collective-permute-start | bytes 1572872 | tf_op jit(solution)/shard_map/ppermute | solution.py:231
  71.4 17.7 %collective-permute-start.10 = (bf16[128,2048]{1,0:T(8,128)(2,1)}, bf16[128,2048]{1,0:T(8,128)(2,1)}, u32[]{:S(2)}, u32[]{:S(2)}) collective-permute-start(bf16[128,2048]{1,0:T(8,128)(2,1)} %slice.39), channel_id=1, source_target_pairs={{0,384},{128,0},{256,128},{384,256},{1,385},{129,1},{257,129},{385... | collective-permute-start | bytes 1572872 | tf_op jit(solution)/shard_map/ppermute | solution.py:213
  77.4 16.3 %collective-permute-start.8 = (bf16[128,2048]{1,0:T(8,128)(2,1)}, bf16[128,2048]{1,0:T(8,128)(2,1)}, u32[]{:S(2)}, u32[]{:S(2)}) collective-permute-start(bf16[128,2048]{1,0:T(8,128)(2,1)} %slice.38), channel_id=1, source_target_pairs={{0,128},{128,256},{256,384},{384,0},{1,129},{129,257},{257,385},{3... | collective-permute-start | bytes 1572872 | tf_op jit(solution)/shard_map/ppermute | solution.py:213
  97.0 3.4 %collective-permute-start.12 = (bf16[16,16,512]{2,1,0:T(8,128)(2,1)S(1)}, bf16[16,16,512]{2,1,0:T(8,128)(2,1)S(1)}, u32[]{:S(2)}, u32[]{:S(2)}) collective-permute-start(bf16[16,16,512]{2,1,0:T(8,128)(2,1)S(1)} %get-tuple-element.22), channel_id=1, source_target_pairs={{0,64},{64,0},{1,65},{65,1},{2,66},{66,2},{3,67},{67,3},{4,68},{68... | collective-permute-start | bytes 786440 | tf_op jit(solution)/shard_map/ppermute | solution.py:161
  101.3 18.5 %all-to-all-start.2 = ((bf16[2,16,16,512]{3,2,1,0:T(8,128)(2,1)}), bf16[2,16,16,512]{3,2,1,0:T(8,128)(2,1)}, u32[]{:S(2)}, u32[]{:S(2)}) async-start(bf16[2,16,16,512]{3,2,1,0:T(8,128)(2,1)} %pad_maximum_fusion), calls=%async_computation.2 | async-start | bytes 1048576 | tf_op jit(solution)/shard_map/all_to_all | solution.py:253
  105.6 0.8 copy-start.3
  110.6 0.8 copy-start.1
  111.4 3.4 %collective-permute-start.11 = (bf16[16,16,512]{2,1,0:T(8,128)(2,1)S(1)}, bf16[16,16,512]{2,1,0:T(8,128)(2,1)S(1)}, u32[]{:S(2)}, u32[]{:S(2)}) collective-permute-start(bf16[16,16,512]{2,1,0:T(8,128)(2,1)S(1)} %get-tuple-element.20), channel_id=1, source_target_pairs={{0,64},{64,0},{1,65},{65,1},{2,66},{66,2},{3,67},{67,3},{4,68},{68... | collective-permute-start | bytes 786440 | tf_op jit(solution)/shard_map/ppermute | solution.py:161

commit v8 on v7

--- a/solution.py
+++ b/solution.py
@@ -266,8 +266,8 @@
     prune = lax.dynamic_index_in_dim(prune, c_id, 1, keepdims=False)
     prune = jnp.repeat(prune.astype(F32), BLK, axis=1)
     pruned = lax.optimization_barrier(summed * summed * prune[:, None, :])
-    mass = lax.psum(jnp.sum(pruned, axis=(0, 1)), "core")
-    mass = jnp.sum(spread(mass.reshape(-1, BLK), ("x", "zhi"), nx * nl), axis=0).reshape(-1)
+    mass = jnp.sum(pruned, axis=(0, 1)).reshape(-1, BLK)
+    mass = jnp.sum(spread(mass, ("x", "core", "zhi"), nx * nk * nl), axis=0).reshape(-1)
     return pruned * (node_count / mass)[None, None, :]
 
 

time: 149 us -> 147 us (0.987)
  blocking collectives: 25.7 us -> 23.6 us
    psum x1 -> x0, blocking collectives: 2.46 us -> none  [on_device(): mass = lax.psum(jnp.sum(pruned, axis=(0, 1)), 'core')]
where the time goes in v8:
time: 147 us; the launch traced here: 146 us
  starting transfers between devices  69.1 us (47%)
  waiting for transfers between devices  26.5 us (18%)
  blocking collectives  23.6 us (16%)
  Pallas kernels  13.7 us (9%)
  local copies, waits for them, and re-layouts  9.29 us (6%)
  other arithmetic  3.15 us (2%)
    all_to_all x1, blocking collectives, spread(): return lax.all_to_all(wide, axes, split_axis=0, concat_axis=0, tiled=True)  23.6 us
    ppermute x4, starting transfers between devices, step_x(): return lax.ppermute(piece, 'x', [(i, (i + d) % nx) for i in range(nx)])  13.7 us
    ppermute x3, starting transfers between devices, on_device(): lax.ppermute(near, 'y', [(i, (i + d) % ny) for i in range(ny)])  11.3 us
    ppermute x1, starting transfers between devices, on_device(): near = jnp.concatenate([shard, lax.ppermute(shard, 'z0', SWAP)], axis=0)  9.91 us
    all_to_all x1, starting transfers between devices, on_device(): lax.all_to_all(partial.reshape(2 * members * 2, rows_dev), ('x', 'core',...  9.72 us
    ppermute x3, waiting for transfers between devices, on_device(): lax.ppermute(near, 'y', [(i, (i + d) % ny) for i in range(ny)])  9.62 us
    all_to_all x1, starting transfers between devices, on_device(): lax.all_to_all(outgoing, group, split_axis=0, concat_axis=0, tiled=True)  9.08 us
    pallas_call x2, Pallas kernels, product(): call(functools.partial(product_kernel, group, ny), in_specs=[vmem] * (ny...  6.39 us
  transfers between devices with their start and end apart: 16, of which 8 were waited for; matrix products, arithmetic and copies ran while one was open for 4% of the time, Pallas kernels for 4%

profile of v8, /device:TPU:32, one launch (start us, length us, event | category | flops | bytes accessed | tf_op | source)
XLA Modules:
  0.0 145.6 jit_solution(14576717972105345933)
XLA Ops:
  2.0 2.3 %shard_map.37.out_ref = bf16[32,64,256]{2,1,0:T(8,128)(2,1)} custom-call(s32[64,64]{1,0:T(8,128)S(1)} %copy-done.2, bf16[1,64,8192]{2,1,0:T(8,128)(2,1)S(1)} %copy-done), custom_call_target="tpu_custom_call" | custom-call | tf_op jit(solution)/shard_map/pallas_call | solution.py:174
  4.3 9.1 %all-to-all-start = ((bf16[32,64,256]{2,1,0:T(8,128)(2,1)}), bf16[32,64,256]{2,1,0:T(8,128)(2,1)S(1)}, u32[]{:S(2)}, u32[]{:S(2)}) async-start(bf16[32,64,256]{2,1,0:T(8,128)(2,1)} %shard_map.37.out_ref), calls=%async_computation | async-start | bytes 2097152 | tf_op jit(solution)/shard_map/all_to_all | solution.py:180
  13.4 1.5 %shard_map.39 = bf16[2,64,2048]{2,1,0:T(8,128)(2,1)S(1)} custom-call(bf16[32,64,256]{2,1,0:T(8,128)(2,1)} %shard_map.37.out_ref), custom_call_target="tpu_custom_call" | custom-call | tf_op jit(solution)/shard_map/pallas_call | solution.py:182
  15.0 3.4 %collective-permute-start = (bf16[64,2048]{1,0:T(8,128)(2,1)S(1)}, bf16[64,2048]{1,0:T(8,128)(2,1)S(1)}, u32[]{:S(2)}, u32[]{:S(2)}) collective-permute-start(bf16[64,2048]{1,0:T(8,128)(2,1)S(1)} %get-tuple-element.24), channel_id=1, source_target_pairs={{0,51},{48,1},{16,32},{32,16},{1,48},{49,2},{17,33},{33,17},{2,49}... | collective-permute-start | bytes 786440 | tf_op jit(solution)/shard_map/ppermute | solution.py:187
  18.4 1.9 %collective-permute-start.2 = (bf16[64,2048]{1,0:T(8,128)(2,1)S(1)}, bf16[64,2048]{1,0:T(8,128)(2,1)S(1)}, u32[]{:S(2)}, u32[]{:S(2)}) collective-permute-start(bf16[64,2048]{1,0:T(8,128)(2,1)S(1)} %get-tuple-element.23), channel_id=1, source_target_pairs={{0,115},{48,65},{16,96},{32,80},{1,112},{49,66},{17,97},{33,81},{2... | collective-permute-start | bytes 786440 | tf_op jit(solution)/shard_map/ppermute | solution.py:188
  20.3 1.5 %shard_map.38 = bf16[2,64,2048]{2,1,0:T(8,128)(2,1)S(1)} custom-call(bf16[32,64,256]{2,1,0:T(8,128)(2,1)} %shard_map.37.out_ref), custom_call_target="tpu_custom_call" | custom-call | tf_op jit(solution)/shard_map/pallas_call | solution.py:182
  21.8 3.6 %collective-permute-done.d10 = bf16[64,2048]{1,0:T(8,128)(2,1)S(1)} collective-permute-done((bf16[64,2048]{1,0:T(8,128)(2,1)S(1)}, bf16[64,2048]{1,0:T(8,128)(2,1)S(1)}, u32[]{:S(2)}, u32[]{:S(2)}) %collective-permute-start) | collective-permute-done | bytes 262176 | tf_op jit(solution)/shard_map/ppermute | solution.py:187
  25.4 1.9 %collective-permute-start.1 = (bf16[64,2048]{1,0:T(8,128)(2,1)S(1)}, bf16[64,2048]{1,0:T(8,128)(2,1)S(1)}, u32[]{:S(2)}, u32[]{:S(2)}) collective-permute-start(bf16[64,2048]{1,0:T(8,128)(2,1)S(1)} %get-tuple-element.14), channel_id=1, source_target_pairs={{0,64},{64,0},{1,65},{65,1},{2,66},{66,2},{3,67},{67,3},{4,68},{68... | collective-permute-start | bytes 786440 | tf_op jit(solution)/shard_map/ppermute | solution.py:161
  27.4 1.9 %collective-permute-done.2.d11 = bf16[64,2048]{1,0:T(8,128)(2,1)S(1)} collective-permute-done((bf16[64,2048]{1,0:T(8,128)(2,1)S(1)}, bf16[64,2048]{1,0:T(8,128)(2,1)S(1)}, u32[]{:S(2)}, u32[]{:S(2)}) %collective-permute-start.2) | collective-permute-done | bytes 262176 | tf_op jit(solution)/shard_map/ppermute | solution.py:188
  29.3 2.0 %shard_map.40 = (bf16[4,64,2048]{2,1,0:T(8,128)(2,1)S(1)}, bf16[64,2048]{1,0:T(8,128)(2,1)S(1)}, f32[4,64]{1,0:T(4,128)S(1)}) custom-call(bf16[32,64,256]{2,1,0:T(8,128)(2,1)S(1)} %all-to-all-done.recv_ref, bf16[64,2048]{1,0:T(8,128)(2,1)S(1)} %get-tuple-element.26.d00, bf16[64,2048]{1,0:T(8,128)(2,1)S(1)} %collective-permute-done.1.d01, ...), custom_call_target="tpu_custom_call" | custom-call | tf_op jit(solution)/shard_map/pallas_call | solution.py:191
  31.3 4.7 %collective-permute-start.9 = (bf16[256,2048]{1,0:T(8,128)(2,1)S(1)}, bf16[256,2048]{1,0:T(8,128)(2,1)}, u32[]{:S(2)}, u32[]{:S(2)}) collective-permute-start(bf16[256,2048]{1,0:T(8,128)(2,1)S(1)} %bitcast.26), channel_id=1, source_target_pairs={{0,384},{128,0},{256,128},{384,256},{1,385},{129,1},{257,129},{385... | collective-permute-start | bytes 3145736 | tf_op jit(solution)/shard_map/ppermute | solution.py:213
  35.9 1.9 %collective-permute-start.7 = (bf16[256,2048]{1,0:T(8,128)(2,1)S(1)}, bf16[256,2048]{1,0:T(8,128)(2,1)S(1)}, u32[]{:S(2)}, u32[]{:S(2)}) collective-permute-start(bf16[256,2048]{1,0:T(8,128)(2,1)S(1)} %bitcast.27), channel_id=1, source_target_pairs={{0,128},{128,256},{256,384},{384,0},{1,129},{129,257},{257,385},{3... | collective-permute-start | bytes 3145736 | tf_op jit(solution)/shard_map/ppermute | solution.py:213
  37.9 9.9 %collective-permute-start.3 = (bf16[64,2048]{1,0:T(8,128)(2,1)S(1)}, bf16[64,2048]{1,0:T(8,128)(2,1)S(1)}, u32[]{:S(2)}, u32[]{:S(2)}) collective-permute-start(bf16[64,2048]{1,0:T(8,128)(2,1)S(1)} %get-tuple-element.16), channel_id=1, source_target_pairs={{0,16},{16,0},{1,17},{17,1},{2,18},{18,2},{3,19},{19,3},{4,20},{20... | collective-permute-start | bytes 786440 | tf_op jit(solution)/shard_map/ppermute | solution.py:211
  48.4 9.7 %all-to-all-start.1 = ((f32[128,1,64]{2,1,0:T(1,128)}), f32[128,1,64]{2,1,0:T(1,128)S(1)}, u32[]{:S(2)}, u32[]{:S(2)}) async-start(f32[128,1,64]{2,1,0:T(1,128)} %bitcast.6), calls=%async_computation.1 | async-start | bytes 131072 | tf_op jit(solution)/shard_map/all_to_all | solution.py:217
  58.2 3.4 %collective-permute-start.4 = (bf16[128,2048]{1,0:T(8,128)(2,1)S(1)}, bf16[128,2048]{1,0:T(8,128)(2,1)S(1)}, u32[]{:S(2)}, u32[]{:S(2)}) collective-permute-start(bf16[128,2048]{1,0:T(8,128)(2,1)S(1)} %constant_dynamic-update-slice_fusion.refs_0_), channel_id=1, source_target_pairs={{0,4},{4,8},{8,12},{12,0},{1,5},{5,9},{9,13},{13,1},{2,6},{6,10},{... | collective-permute-start | bytes 1572872 | tf_op jit(solution)/shard_map/ppermute | solution.py:231
  61.6 4.6 %collective-permute-start.5 = (bf16[128,2048]{1,0:T(8,128)(2,1)S(1)}, bf16[128,2048]{1,0:T(8,128)(2,1)}, u32[]{:S(2)}, u32[]{:S(2)}) collective-permute-start(bf16[128,2048]{1,0:T(8,128)(2,1)S(1)} %constant_dynamic-update-slice_fusion.refs_0_), channel_id=1, source_target_pairs={{0,8},{4,12},{8,0},{12,4},{1,9},{5,13},{9,1},{13,5},{2,10},{6,14},... | collective-permute-start | bytes 1572872 | tf_op jit(solution)/shard_map/ppermute | solution.py:231
  66.2 3.4 %collective-permute-start.6 = (bf16[128,2048]{1,0:T(8,128)(2,1)S(1)}, bf16[128,2048]{1,0:T(8,128)(2,1)}, u32[]{:S(2)}, u32[]{:S(2)}) collective-permute-start(bf16[128,2048]{1,0:T(8,128)(2,1)S(1)} %constant_dynamic-update-slice_fusion.refs_0_), channel_id=1, source_target_pairs={{0,12},{4,0},{8,4},{12,8},{1,13},{5,1},{9,5},{13,9},{2,14},{6,2},{... | collective-permute-start | bytes 1572872 | tf_op jit(solution)/shard_map/ppermute | solution.py:231
  69.6 1.9 %slice.39 = bf16[128,2048]{1,0:T(8,128)(2,1)} slice(bf16[256,2048]{1,0:T(8,128)(2,1)} %collective-permute-done.9.refs_8_), slice={[128:256], [0:2048]} | slice | bytes 1048576 | tf_op jit(solution)/shard_map/slice | solution.py:239
  71.5 5.1 %collective-permute-start.10 = (bf16[128,2048]{1,0:T(8,128)(2,1)}, bf16[128,2048]{1,0:T(8,128)(2,1)}, u32[]{:S(2)}, u32[]{:S(2)}) collective-permute-start(bf16[128,2048]{1,0:T(8,128)(2,1)} %slice.39), channel_id=1, source_target_pairs={{0,384},{128,0},{256,128},{384,256},{1,385},{129,1},{257,129},{385... | collective-permute-start | bytes 1572872 | tf_op jit(solution)/shard_map/ppermute | solution.py:213
  77.5 1.9 %collective-permute-start.8 = (bf16[128,2048]{1,0:T(8,128)(2,1)}, bf16[128,2048]{1,0:T(8,128)(2,1)}, u32[]{:S(2)}, u32[]{:S(2)}) collective-permute-start(bf16[128,2048]{1,0:T(8,128)(2,1)} %slice.38), channel_id=1, source_target_pairs={{0,128},{128,256},{256,384},{384,0},{1,129},{129,257},{257,385},{3... | collective-permute-start | bytes 1572872 | tf_op jit(solution)/shard_map/ppermute | solution.py:213
  79.5 8.3 %collective-permute-done.5.refs_2_ = bf16[128,2048]{1,0:T(8,128)(2,1)} collective-permute-done((bf16[128,2048]{1,0:T(8,128)(2,1)S(1)}, bf16[128,2048]{1,0:T(8,128)(2,1)}, u32[]{:S(2)}, u32[]{:S(2)}) %collective-permute-start.5) | collective-permute-done | bytes 524320 | tf_op jit(solution)/shard_map/ppermute | solution.py:231
  87.9 1.3 collective-permute-done.6.refs_3_
  89.2 4.6 %collective-permute-done.8.refs_6_ = bf16[128,2048]{1,0:T(8,128)(2,1)} collective-permute-done((bf16[128,2048]{1,0:T(8,128)(2,1)}, bf16[128,2048]{1,0:T(8,128)(2,1)}, u32[]{:S(2)}, u32[]{:S(2)}) %collective-permute-start.8) | collective-permute-done | bytes 524320 | tf_op jit(solution)/shard_map/ppermute | solution.py:213
  93.8 3.2 %shard_map.42 = (f32[16,16,512]{2,1,0:T(8,128)S(1)}, bf16[16,16,512]{2,1,0:T(8,128)(2,1)S(1)}) custom-call(bf16[128,2048]{1,0:T(8,128)(2,1)S(1)} %constant_dynamic-update-slice_fusion.refs_0_, bf16[128,2048]{1,0:T(8,128)(2,1)S(1)} %collective-permute-done.4.refs_1_, bf16[128,2048]{1,0:T(8,128)(2,1)} %collective-permute-done.5.refs_2_, ...), custom_call_target="tpu_custom_call" | custom-call | tf_op jit(solution)/shard_map/pallas_call | solution.py:243
  97.0 1.9 %collective-permute-start.12 = (bf16[16,16,512]{2,1,0:T(8,128)(2,1)S(1)}, bf16[16,16,512]{2,1,0:T(8,128)(2,1)S(1)}, u32[]{:S(2)}, u32[]{:S(2)}) collective-permute-start(bf16[16,16,512]{2,1,0:T(8,128)(2,1)S(1)} %get-tuple-element.22), channel_id=1, source_target_pairs={{0,64},{64,0},{1,65},{65,1},{2,66},{66,2},{3,67},{67,3},{4,68},{68... | collective-permute-start | bytes 786440 | tf_op jit(solution)/shard_map/ppermute | solution.py:161
  98.9 1.5 %collective-permute-done.12 = bf16[16,16,512]{2,1,0:T(8,128)(2,1)S(1)} collective-permute-done((bf16[16,16,512]{2,1,0:T(8,128)(2,1)S(1)}, bf16[16,16,512]{2,1,0:T(8,128)(2,1)S(1)}, u32[]{:S(2)}, u32[]{:S(2)}) %collective-permute-start.12) | collective-permute-done | bytes 262176 | tf_op jit(solution)/shard_map/ppermute | solution.py:161
  101.3 4.2 %all-to-all-start.2 = ((bf16[2,16,16,512]{3,2,1,0:T(8,128)(2,1)}), bf16[2,16,16,512]{3,2,1,0:T(8,128)(2,1)}, u32[]{:S(2)}, u32[]{:S(2)}) async-start(bf16[2,16,16,512]{3,2,1,0:T(8,128)(2,1)} %pad_maximum_fusion), calls=%async_computation.2 | async-start | bytes 1048576 | tf_op jit(solution)/shard_map/all_to_all | solution.py:253
  107.4 3.2 %shard_map.41 = (f32[16,16,512]{2,1,0:T(8,128)S(1)}, bf16[16,16,512]{2,1,0:T(8,128)(2,1)S(1)}) custom-call(bf16[128,2048]{1,0:T(8,128)(2,1)S(1)} %constant_dynamic-update-slice_fusion.refs_0_, bf16[128,2048]{1,0:T(8,128)(2,1)S(1)} %collective-permute-done.4.refs_1_, bf16[128,2048]{1,0:T(8,128)(2,1)} %collective-permute-done.5.refs_2_, ...), custom_call_target="tpu_custom_call" | custom-call | tf_op jit(solution)/shard_map/pallas_call | solution.py:243
  111.4 2.0 %collective-permute-start.11 = (bf16[16,16,512]{2,1,0:T(8,128)(2,1)S(1)}, bf16[16,16,512]{2,1,0:T(8,128)(2,1)S(1)}, u32[]{:S(2)}, u32[]{:S(2)}) collective-permute-start(bf16[16,16,512]{2,1,0:T(8,128)(2,1)S(1)} %get-tuple-element.20), channel_id=1, source_target_pairs={{0,64},{64,0},{1,65},{65,1},{2,66},{66,2},{3,67},{67,3},{4,68},{68... | collective-permute-start | bytes 786440 | tf_op jit(solution)/shard_map/ppermute | solution.py:161
  114.8 5.0 %all-to-all-done.2 = bf16[2,16,16,512]{3,2,1,0:T(8,128)(2,1)} async-done(((bf16[2,16,16,512]{3,2,1,0:T(8,128)(2,1)}), bf16[2,16,16,512]{3,2,1,0:T(8,128)(2,1)}, u32[]{:S(2)}, u32[]{:S(2)}) %all-to-all-start.2) | async-done | bytes 524320 | tf_op jit(solution)/shard_map/all_to_all | solution.py:253
  119.8 1.2 fusion.1
  121.1 23.6 %all_to_all.24 = f32[32,4,128]{2,1,0:T(4,128)S(1)} all-to-all(f32[32,4,128]{2,1,0:T(4,128)S(1)} %broadcast_in_dim.22), channel_id=1, replica_groups=mesh['x'=4,'core'=2,'z1'=2,'z0'=2,'y'=4,'zhi'=4] {'x','core','zhi'}, dimensions={0} | all-to-all | bytes 131072 | tf_op jit(solution)/shard_map/all_to_all | solution.py:165
  (41 shorter events, 9.6 us)
Async XLA Ops:
  0.0 1.2 copy-start
  1.2 0.8 copy-start.2
  4.3 24.9 %all-to-all-start = ((bf16[32,64,256]{2,1,0:T(8,128)(2,1)}), bf16[32,64,256]{2,1,0:T(8,128)(2,1)S(1)}, u32[]{:S(2)}, u32[]{:S(2)}) async-start(bf16[32,64,256]{2,1,0:T(8,128)(2,1)} %shard_map.37.out_ref), calls=%async_computation | async-start | bytes 2097152 | tf_op jit(solution)/shard_map/all_to_all | solution.py:180
  15.0 10.5 %collective-permute-start = (bf16[64,2048]{1,0:T(8,128)(2,1)S(1)}, bf16[64,2048]{1,0:T(8,128)(2,1)S(1)}, u32[]{:S(2)}, u32[]{:S(2)}) collective-permute-start(bf16[64,2048]{1,0:T(8,128)(2,1)S(1)} %get-tuple-element.24), channel_id=1, source_target_pairs={{0,51},{48,1},{16,32},{32,16},{1,48},{49,2},{17,33},{33,17},{2,49}... | collective-permute-start | bytes 786440 | tf_op jit(solution)/shard_map/ppermute | solution.py:187
  18.4 10.9 %collective-permute-start.2 = (bf16[64,2048]{1,0:T(8,128)(2,1)S(1)}, bf16[64,2048]{1,0:T(8,128)(2,1)S(1)}, u32[]{:S(2)}, u32[]{:S(2)}) collective-permute-start(bf16[64,2048]{1,0:T(8,128)(2,1)S(1)} %get-tuple-element.23), channel_id=1, source_target_pairs={{0,115},{48,65},{16,96},{32,80},{1,112},{49,66},{17,97},{33,81},{2... | collective-permute-start | bytes 786440 | tf_op jit(solution)/shard_map/ppermute | solution.py:188
  25.4 3.8 %collective-permute-start.1 = (bf16[64,2048]{1,0:T(8,128)(2,1)S(1)}, bf16[64,2048]{1,0:T(8,128)(2,1)S(1)}, u32[]{:S(2)}, u32[]{:S(2)}) collective-permute-start(bf16[64,2048]{1,0:T(8,128)(2,1)S(1)} %get-tuple-element.14), channel_id=1, source_target_pairs={{0,64},{64,0},{1,65},{65,1},{2,66},{66,2},{3,67},{67,3},{4,68},{68... | collective-permute-start | bytes 786440 | tf_op jit(solution)/shard_map/ppermute | solution.py:161
  31.3 38.3 %collective-permute-start.9 = (bf16[256,2048]{1,0:T(8,128)(2,1)S(1)}, bf16[256,2048]{1,0:T(8,128)(2,1)}, u32[]{:S(2)}, u32[]{:S(2)}) collective-permute-start(bf16[256,2048]{1,0:T(8,128)(2,1)S(1)} %bitcast.26), channel_id=1, source_target_pairs={{0,384},{128,0},{256,128},{384,256},{1,385},{129,1},{257,129},{385... | collective-permute-start | bytes 3145736 | tf_op jit(solution)/shard_map/ppermute | solution.py:213
  35.9 40.7 %collective-permute-start.7 = (bf16[256,2048]{1,0:T(8,128)(2,1)S(1)}, bf16[256,2048]{1,0:T(8,128)(2,1)S(1)}, u32[]{:S(2)}, u32[]{:S(2)}) collective-permute-start(bf16[256,2048]{1,0:T(8,128)(2,1)S(1)} %bitcast.27), channel_id=1, source_target_pairs={{0,128},{128,256},{256,384},{384,0},{1,129},{129,257},{257,385},{3... | collective-permute-start | bytes 3145736 | tf_op jit(solution)/shard_map/ppermute | solution.py:213
  37.9 20.3 %collective-permute-start.3 = (bf16[64,2048]{1,0:T(8,128)(2,1)S(1)}, bf16[64,2048]{1,0:T(8,128)(2,1)S(1)}, u32[]{:S(2)}, u32[]{:S(2)}) collective-permute-start(bf16[64,2048]{1,0:T(8,128)(2,1)S(1)} %get-tuple-element.16), channel_id=1, source_target_pairs={{0,16},{16,0},{1,17},{17,1},{2,18},{18,2},{3,19},{19,3},{4,20},{20... | collective-permute-start | bytes 786440 | tf_op jit(solution)/shard_map/ppermute | solution.py:211
  48.4 31.0 %all-to-all-start.1 = ((f32[128,1,64]{2,1,0:T(1,128)}), f32[128,1,64]{2,1,0:T(1,128)S(1)}, u32[]{:S(2)}, u32[]{:S(2)}) async-start(f32[128,1,64]{2,1,0:T(1,128)} %bitcast.6), calls=%async_computation.1 | async-start | bytes 131072 | tf_op jit(solution)/shard_map/all_to_all | solution.py:217
  58.2 21.3 %collective-permute-start.4 = (bf16[128,2048]{1,0:T(8,128)(2,1)S(1)}, bf16[128,2048]{1,0:T(8,128)(2,1)S(1)}, u32[]{:S(2)}, u32[]{:S(2)}) collective-permute-start(bf16[128,2048]{1,0:T(8,128)(2,1)S(1)} %constant_dynamic-update-slice_fusion.refs_0_), channel_id=1, source_target_pairs={{0,4},{4,8},{8,12},{12,0},{1,5},{5,9},{9,13},{13,1},{2,6},{6,10},{... | collective-permute-start | bytes 1572872 | tf_op jit(solution)/shard_map/ppermute | solution.py:231
  61.6 26.3 %collective-permute-start.5 = (bf16[128,2048]{1,0:T(8,128)(2,1)S(1)}, bf16[128,2048]{1,0:T(8,128)(2,1)}, u32[]{:S(2)}, u32[]{:S(2)}) collective-permute-start(bf16[128,2048]{1,0:T(8,128)(2,1)S(1)} %constant_dynamic-update-slice_fusion.refs_0_), channel_id=1, source_target_pairs={{0,8},{4,12},{8,0},{12,4},{1,9},{5,13},{9,1},{13,5},{2,10},{6,14},... | collective-permute-start | bytes 1572872 | tf_op jit(solution)/shard_map/ppermute | solution.py:231
  66.2 23.0 %collective-permute-start.6 = (bf16[128,2048]{1,0:T(8,128)(2,1)S(1)}, bf16[128,2048]{1,0:T(8,128)(2,1)}, u32[]{:S(2)}, u32[]{:S(2)}) collective-permute-start(bf16[128,2048]{1,0:T(8,128)(2,1)S(1)} %constant_dynamic-update-slice_fusion.refs_0_), channel_id=1, source_target_pairs={{0,12},{4,0},{8,4},{12,8},{1,13},{5,1},{9,5},{13,9},{2,14},{6,2},{... | collective-permute-start | bytes 1572872 | tf_op jit(solution)/shard_map/ppermute | solution.py:231
  71.5 17.7 %collective-permute-start.10 = (bf16[128,2048]{1,0:T(8,128)(2,1)}, bf16[128,2048]{1,0:T(8,128)(2,1)}, u32[]{:S(2)}, u32[]{:S(2)}) collective-permute-start(bf16[128,2048]{1,0:T(8,128)(2,1)} %slice.39), channel_id=1, source_target_pairs={{0,384},{128,0},{256,128},{384,256},{1,385},{129,1},{257,129},{385... | collective-permute-start | bytes 1572872 | tf_op jit(solution)/shard_map/ppermute | solution.py:213
  77.5 16.3 %collective-permute-start.8 = (bf16[128,2048]{1,0:T(8,128)(2,1)}, bf16[128,2048]{1,0:T(8,128)(2,1)}, u32[]{:S(2)}, u32[]{:S(2)}) collective-permute-start(bf16[128,2048]{1,0:T(8,128)(2,1)} %slice.38), channel_id=1, source_target_pairs={{0,128},{128,256},{256,384},{384,0},{1,129},{129,257},{257,385},{3... | collective-permute-start | bytes 1572872 | tf_op jit(solution)/shard_map/ppermute | solution.py:213
  97.0 3.4 %collective-permute-start.12 = (bf16[16,16,512]{2,1,0:T(8,128)(2,1)S(1)}, bf16[16,16,512]{2,1,0:T(8,128)(2,1)S(1)}, u32[]{:S(2)}, u32[]{:S(2)}) collective-permute-start(bf16[16,16,512]{2,1,0:T(8,128)(2,1)S(1)} %get-tuple-element.22), channel_id=1, source_target_pairs={{0,64},{64,0},{1,65},{65,1},{2,66},{66,2},{3,67},{67,3},{4,68},{68... | collective-permute-start | bytes 786440 | tf_op jit(solution)/shard_map/ppermute | solution.py:161
  101.3 18.5 %all-to-all-start.2 = ((bf16[2,16,16,512]{3,2,1,0:T(8,128)(2,1)}), bf16[2,16,16,512]{3,2,1,0:T(8,128)(2,1)}, u32[]{:S(2)}, u32[]{:S(2)}) async-start(bf16[2,16,16,512]{3,2,1,0:T(8,128)(2,1)} %pad_maximum_fusion), calls=%async_computation.2 | async-start | bytes 1048576 | tf_op jit(solution)/shard_map/all_to_all | solution.py:253
  105.6 0.8 copy-start.3
  110.6 0.8 copy-start.1
  111.4 3.4 %collective-permute-start.11 = (bf16[16,16,512]{2,1,0:T(8,128)(2,1)S(1)}, bf16[16,16,512]{2,1,0:T(8,128)(2,1)S(1)}, u32[]{:S(2)}, u32[]{:S(2)}) collective-permute-start(bf16[16,16,512]{2,1,0:T(8,128)(2,1)S(1)} %get-tuple-element.20), channel_id=1, source_target_pairs={{0,64},{64,0},{1,65},{65,1},{2,66},{66,2},{3,67},{67,3},{4,68},{68... | collective-permute-start | bytes 786440 | tf_op jit(solution)/shard_map/ppermute | solution.py:161

commit v9 on v8

--- a/solution.py
+++ b/solution.py
@@ -212,21 +212,14 @@
     def step_x(piece, d):
         return lax.ppermute(piece, "x", [(i, (i + d) % nx) for i in range(nx)])
 
-    partial = row_sum.reshape(1, 2, 2, 1, 1, rows_dev)
-    partial = jnp.broadcast_to(partial, (nx, 2, 2, 2, ny, rows_dev))
+    partial = jnp.broadcast_to(row_sum.reshape(2, 2, 1, 1, rows_dev), (2, 2, 2, ny, rows_dev))
     partial = lax.all_to_all(
-        partial.reshape(2 * members * 2, rows_dev),
-        ("x", "core", "z1", "z0", "y"),
+        partial.reshape(8 * ny, rows_dev),
+        ("core", "z1", "z0", "y"),
         split_axis=0,
         concat_axis=0,
         tiled=True,
     )
-    partial = jnp.sum(partial.reshape(nx, 2, 2, 2, ny, rows_dev), axis=1)
-    degree = jnp.where(
-        z1 == 0,
-        partial[:, 0] + partial[:, 1, ::-1],
-        partial[:, 1] + partial[:, 0, ::-1],
-    ).reshape(1, inner)
     rows = [near] + [
         lax.ppermute(near, "y", [(i, (i + d) % ny) for i in range(ny)]) for d in range(1, ny)
     ]
@@ -235,8 +228,15 @@
     blocks = [own_block, step_x(own_block, 1)]
     if nx == 4:
         after = step_x(own_block, -1)
-        before = blocks[1]
+        before, after, partial = lax.optimization_barrier((blocks[1], after, partial))
         blocks = [own_block, before, step_x(before[:BLK], 1), step_x(after[BLK:], -1), after]
+
+    partial = jnp.sum(partial.reshape(2, 2, 2, ny, rows_dev), axis=0)
+    degree = jnp.where(
+        z1 == 0, partial[0] + partial[1, ::-1], partial[1] + partial[0, ::-1]
+    )
+    degree = spread(degree.reshape(-1, BLK), "x", nx).reshape(1, inner)
+
     tile_cols = nx * BLK
 
     def product(group):

time: 147 us -> 144 us (0.980)
  waiting for transfers between devices: 26.5 us -> 21.5 us
  blocking collectives: 23.6 us -> 25.6 us
    ppermute x4, waiting for transfers between devices: 4.64 us -> 0.01 us  [step_x(): return lax.ppermute(piece, 'x', [(i, (i + d) % nx) for i in range(nx)])]
    ppermute x3, waiting for transfers between devices: 9.62 us -> 6.27 us  [on_device(): lax.ppermute(near, 'y', [(i, (i + d) % ny) for i in range(ny)])]
    all_to_all x1 -> x2, waiting for transfers between devices: 0.01 us -> 2.93 us  [the longest x1 2.93 us: spread(): return lax.all_to_all(wide, axes, split_axis=0, concat_axis=0, tiled=True)]
    all_to_all x1, blocking collectives: 23.6 us -> 25.6 us  [spread(): return lax.all_to_all(wide, axes, split_axis=0, concat_axis=0, tiled=True)]
    all_to_all x1 -> x2, starting transfers between devices: 9.72 us -> 9.89 us  [the longest x1 5.86 us: on_device(): lax.all_to_all(partial.reshape(8 * ny, rows_dev), ('core', 'z1', 'z0', 'y...]
  transfers between devices with their start and end apart: 16 -> 17, of which waited for: 8 -> 8; matrix products, arithmetic and copies ran while one was open for 4% -> 4% of each run, Pallas kernels for 4% -> 4%
where the time goes in v9:
time: 144 us; the launch traced here: 143 us
  starting transfers between devices  68.5 us (48%)
  blocking collectives  25.6 us (18%)
  waiting for transfers between devices  21.5 us (15%)
  Pallas kernels  13.7 us (10%)
  local copies, waits for them, and re-layouts  9.85 us (7%)
  other arithmetic  3.16 us (2%)
    all_to_all x1, blocking collectives, spread(): return lax.all_to_all(wide, axes, split_axis=0, concat_axis=0, tiled=True)  25.6 us
    ppermute x4, starting transfers between devices, step_x(): return lax.ppermute(piece, 'x', [(i, (i + d) % nx) for i in range(nx)])  12.9 us
    ppermute x3, starting transfers between devices, on_device(): lax.ppermute(near, 'y', [(i, (i + d) % ny) for i in range(ny)])  11.3 us
    ppermute x1, starting transfers between devices, on_device(): near = jnp.concatenate([shard, lax.ppermute(shard, 'z0', SWAP)], axis=0)  9.94 us
    all_to_all x1, starting transfers between devices, on_device(): lax.all_to_all(outgoing, group, split_axis=0, concat_axis=0, tiled=True)  9.08 us
    pallas_call x2, Pallas kernels, product(): call(functools.partial(product_kernel, group, ny), in_specs=[vmem] * (ny...  6.39 us
    ppermute x3, waiting for transfers between devices, on_device(): lax.ppermute(near, 'y', [(i, (i + d) % ny) for i in range(ny)])  6.27 us
    all_to_all x1, starting transfers between devices, on_device(): lax.all_to_all(partial.reshape(8 * ny, rows_dev), ('core', 'z1', 'z0', 'y...  5.86 us
  transfers between devices with their start and end apart: 17, of which 8 were waited for; matrix products, arithmetic and copies ran while one was open for 4% of the time, Pallas kernels for 4%

profile of v9, /device:TPU:32, one launch (start us, length us, event | category | flops | bytes accessed | tf_op | source)
XLA Modules:
  0.0 142.6 jit_solution(5983886272816155924)
XLA Ops:
  2.0 2.3 %shard_map.37.out_ref = bf16[32,64,256]{2,1,0:T(8,128)(2,1)} custom-call(s32[64,64]{1,0:T(8,128)S(1)} %copy-done.2, bf16[1,64,8192]{2,1,0:T(8,128)(2,1)S(1)} %copy-done), custom_call_target="tpu_custom_call" | custom-call | tf_op jit(solution)/shard_map/pallas_call | solution.py:174
  4.3 9.1 %all-to-all-start = ((bf16[32,64,256]{2,1,0:T(8,128)(2,1)}), bf16[32,64,256]{2,1,0:T(8,128)(2,1)S(1)}, u32[]{:S(2)}, u32[]{:S(2)}) async-start(bf16[32,64,256]{2,1,0:T(8,128)(2,1)} %shard_map.37.out_ref), calls=%async_computation | async-start | bytes 2097152 | tf_op jit(solution)/shard_map/all_to_all | solution.py:180
  13.4 1.5 %shard_map.39 = bf16[2,64,2048]{2,1,0:T(8,128)(2,1)S(1)} custom-call(bf16[32,64,256]{2,1,0:T(8,128)(2,1)} %shard_map.37.out_ref), custom_call_target="tpu_custom_call" | custom-call | tf_op jit(solution)/shard_map/pallas_call | solution.py:182
  15.0 3.4 %collective-permute-start = (bf16[64,2048]{1,0:T(8,128)(2,1)S(1)}, bf16[64,2048]{1,0:T(8,128)(2,1)S(1)}, u32[]{:S(2)}, u32[]{:S(2)}) collective-permute-start(bf16[64,2048]{1,0:T(8,128)(2,1)S(1)} %get-tuple-element.30), channel_id=1, source_target_pairs={{0,51},{48,1},{16,32},{32,16},{1,48},{49,2},{17,33},{33,17},{2,49}... | collective-permute-start | bytes 786440 | tf_op jit(solution)/shard_map/ppermute | solution.py:187
  18.4 1.9 %collective-permute-start.2 = (bf16[64,2048]{1,0:T(8,128)(2,1)S(1)}, bf16[64,2048]{1,0:T(8,128)(2,1)S(1)}, u32[]{:S(2)}, u32[]{:S(2)}) collective-permute-start(bf16[64,2048]{1,0:T(8,128)(2,1)S(1)} %get-tuple-element.29), channel_id=1, source_target_pairs={{0,115},{48,65},{16,96},{32,80},{1,112},{49,66},{17,97},{33,81},{2... | collective-permute-start | bytes 786440 | tf_op jit(solution)/shard_map/ppermute | solution.py:188
  20.3 1.5 %shard_map.38 = bf16[2,64,2048]{2,1,0:T(8,128)(2,1)S(1)} custom-call(bf16[32,64,256]{2,1,0:T(8,128)(2,1)} %shard_map.37.out_ref), custom_call_target="tpu_custom_call" | custom-call | tf_op jit(solution)/shard_map/pallas_call | solution.py:182
  21.8 3.6 %collective-permute-done.d10 = bf16[64,2048]{1,0:T(8,128)(2,1)S(1)} collective-permute-done((bf16[64,2048]{1,0:T(8,128)(2,1)S(1)}, bf16[64,2048]{1,0:T(8,128)(2,1)S(1)}, u32[]{:S(2)}, u32[]{:S(2)}) %collective-permute-start) | collective-permute-done | bytes 262176 | tf_op jit(solution)/shard_map/ppermute | solution.py:187
  25.5 1.9 %collective-permute-start.1 = (bf16[64,2048]{1,0:T(8,128)(2,1)S(1)}, bf16[64,2048]{1,0:T(8,128)(2,1)S(1)}, u32[]{:S(2)}, u32[]{:S(2)}) collective-permute-start(bf16[64,2048]{1,0:T(8,128)(2,1)S(1)} %get-tuple-element.17), channel_id=1, source_target_pairs={{0,64},{64,0},{1,65},{65,1},{2,66},{66,2},{3,67},{67,3},{4,68},{68... | collective-permute-start | bytes 786440 | tf_op jit(solution)/shard_map/ppermute | solution.py:161
  27.4 1.9 %collective-permute-done.2.d11 = bf16[64,2048]{1,0:T(8,128)(2,1)S(1)} collective-permute-done((bf16[64,2048]{1,0:T(8,128)(2,1)S(1)}, bf16[64,2048]{1,0:T(8,128)(2,1)S(1)}, u32[]{:S(2)}, u32[]{:S(2)}) %collective-permute-start.2) | collective-permute-done | bytes 262176 | tf_op jit(solution)/shard_map/ppermute | solution.py:188
  29.3 2.0 %shard_map.40 = (bf16[4,64,2048]{2,1,0:T(8,128)(2,1)S(1)}, bf16[64,2048]{1,0:T(8,128)(2,1)S(1)}, f32[4,64]{1,0:T(4,128)S(1)}) custom-call(bf16[32,64,256]{2,1,0:T(8,128)(2,1)S(1)} %all-to-all-done.recv_ref, bf16[64,2048]{1,0:T(8,128)(2,1)S(1)} %get-tuple-element.32.d00, bf16[64,2048]{1,0:T(8,128)(2,1)S(1)} %collective-permute-done.1.d01, ...), custom_call_target="tpu_custom_call" | custom-call | tf_op jit(solution)/shard_map/pallas_call | solution.py:191
  31.3 3.4 %collective-permute-start.7 = (bf16[256,2048]{1,0:T(8,128)(2,1)S(1)}, bf16[256,2048]{1,0:T(8,128)(2,1)S(1)}, u32[]{:S(2)}, u32[]{:S(2)}) collective-permute-start(bf16[256,2048]{1,0:T(8,128)(2,1)S(1)} %bitcast.28), channel_id=1, source_target_pairs={{0,128},{128,256},{256,384},{384,0},{1,129},{129,257},{257,385},{3... | collective-permute-start | bytes 3145736 | tf_op jit(solution)/shard_map/ppermute | solution.py:213
  34.7 3.6 %collective-permute-start.8 = (bf16[256,2048]{1,0:T(8,128)(2,1)S(1)}, bf16[256,2048]{1,0:T(8,128)(2,1)}, u32[]{:S(2)}, u32[]{:S(2)}) collective-permute-start(bf16[256,2048]{1,0:T(8,128)(2,1)S(1)} %bitcast.29), channel_id=1, source_target_pairs={{0,384},{128,0},{256,128},{384,256},{1,385},{129,1},{257,129},{385... | collective-permute-start | bytes 3145736 | tf_op jit(solution)/shard_map/ppermute | solution.py:213
  38.3 9.9 %collective-permute-start.3 = (bf16[64,2048]{1,0:T(8,128)(2,1)S(1)}, bf16[64,2048]{1,0:T(8,128)(2,1)S(1)}, u32[]{:S(2)}, u32[]{:S(2)}) collective-permute-start(bf16[64,2048]{1,0:T(8,128)(2,1)S(1)} %get-tuple-element.19), channel_id=1, source_target_pairs={{0,16},{16,0},{1,17},{17,1},{2,18},{18,2},{3,19},{19,3},{4,20},{20... | collective-permute-start | bytes 786440 | tf_op jit(solution)/shard_map/ppermute | solution.py:211
  48.9 5.9 %all-to-all-start.1 = ((f32[32,1,64]{2,1,0:T(1,128)}), f32[32,1,64]{2,1,0:T(1,128)S(1)}, u32[]{:S(2)}, u32[]{:S(2)}) async-start(f32[32,1,64]{2,1,0:T(1,128)} %bitcast.6), calls=%async_computation.1 | async-start | bytes 32768 | tf_op jit(solution)/shard_map/all_to_all | solution.py:216
  54.8 3.4 %collective-permute-start.4 = (bf16[128,2048]{1,0:T(8,128)(2,1)S(1)}, bf16[128,2048]{1,0:T(8,128)(2,1)S(1)}, u32[]{:S(2)}, u32[]{:S(2)}) collective-permute-start(bf16[128,2048]{1,0:T(8,128)(2,1)S(1)} %constant_dynamic-update-slice_fusion.refs_0_), channel_id=1, source_target_pairs={{0,4},{4,8},{8,12},{12,0},{1,5},{5,9},{9,13},{13,1},{2,6},{6,10},{... | collective-permute-start | bytes 1572872 | tf_op jit(solution)/shard_map/ppermute | solution.py:224
  58.2 4.6 %collective-permute-start.5 = (bf16[128,2048]{1,0:T(8,128)(2,1)S(1)}, bf16[128,2048]{1,0:T(8,128)(2,1)}, u32[]{:S(2)}, u32[]{:S(2)}) collective-permute-start(bf16[128,2048]{1,0:T(8,128)(2,1)S(1)} %constant_dynamic-update-slice_fusion.refs_0_), channel_id=1, source_target_pairs={{0,8},{4,12},{8,0},{12,4},{1,9},{5,13},{9,1},{13,5},{2,10},{6,14},... | collective-permute-start | bytes 1572872 | tf_op jit(solution)/shard_map/ppermute | solution.py:224
  62.8 3.4 %collective-permute-start.6 = (bf16[128,2048]{1,0:T(8,128)(2,1)S(1)}, bf16[128,2048]{1,0:T(8,128)(2,1)}, u32[]{:S(2)}, u32[]{:S(2)}) collective-permute-start(bf16[128,2048]{1,0:T(8,128)(2,1)S(1)} %constant_dynamic-update-slice_fusion.refs_0_), channel_id=1, source_target_pairs={{0,12},{4,0},{8,4},{12,8},{1,13},{5,1},{9,5},{13,9},{2,14},{6,2},{... | collective-permute-start | bytes 1572872 | tf_op jit(solution)/shard_map/ppermute | solution.py:224
  66.2 1.9 %slice.31 = bf16[128,2048]{1,0:T(8,128)(2,1)} slice(bf16[256,2048]{1,0:T(8,128)(2,1)} %collective-permute-done.8.refs_8_), slice={[128:256], [0:2048]} | slice | bytes 1048576 | tf_op jit(solution)/shard_map/slice | solution.py:232
  68.1 3.4 %collective-permute-start.10 = (bf16[128,2048]{1,0:T(8,128)(2,1)}, bf16[128,2048]{1,0:T(8,128)(2,1)}, u32[]{:S(2)}, u32[]{:S(2)}) collective-permute-start(bf16[128,2048]{1,0:T(8,128)(2,1)} %slice.31), channel_id=1, source_target_pairs={{0,384},{128,0},{256,128},{384,256},{1,385},{129,1},{257,129},{385... | collective-permute-start | bytes 1572872 | tf_op jit(solution)/shard_map/ppermute | solution.py:213
  72.4 2.4 %collective-permute-start.9 = (bf16[128,2048]{1,0:T(8,128)(2,1)}, bf16[128,2048]{1,0:T(8,128)(2,1)}, u32[]{:S(2)}, u32[]{:S(2)}) collective-permute-start(bf16[128,2048]{1,0:T(8,128)(2,1)} %slice.30), channel_id=1, source_target_pairs={{0,128},{128,256},{256,384},{384,0},{1,129},{129,257},{257,385},{3... | collective-permute-start | bytes 1572872 | tf_op jit(solution)/shard_map/ppermute | solution.py:213
  75.5 4.0 %all-to-all-start.2 = ((f32[4,4,128]{2,1,0:T(4,128)}), f32[4,4,128]{2,1,0:T(4,128)S(1)}, u32[]{:S(2)}, u32[]{:S(2)}) async-start(f32[4,4,128]{2,1,0:T(4,128)} %broadcast_in_dim.25), calls=%async_computation.2 | async-start | bytes 16384 | tf_op jit(solution)/shard_map/all_to_all | solution.py:165
  79.5 4.6 %collective-permute-done.5.refs_2_ = bf16[128,2048]{1,0:T(8,128)(2,1)} collective-permute-done((bf16[128,2048]{1,0:T(8,128)(2,1)S(1)}, bf16[128,2048]{1,0:T(8,128)(2,1)}, u32[]{:S(2)}, u32[]{:S(2)}) %collective-permute-start.5) | collective-permute-done | bytes 524320 | tf_op jit(solution)/shard_map/ppermute | solution.py:224
  84.2 1.6 %collective-permute-done.6.refs_3_ = bf16[128,2048]{1,0:T(8,128)(2,1)} collective-permute-done((bf16[128,2048]{1,0:T(8,128)(2,1)S(1)}, bf16[128,2048]{1,0:T(8,128)(2,1)}, u32[]{:S(2)}, u32[]{:S(2)}) %collective-permute-start.6) | collective-permute-done | bytes 524320 | tf_op jit(solution)/shard_map/ppermute | solution.py:224
  85.8 2.9 %all-to-all-done.2 = f32[4,4,128]{2,1,0:T(4,128)S(1)} async-done(((f32[4,4,128]{2,1,0:T(4,128)}), f32[4,4,128]{2,1,0:T(4,128)S(1)}, u32[]{:S(2)}, u32[]{:S(2)}) %all-to-all-start.2) | async-done | bytes 8224 | tf_op jit(solution)/shard_map/all_to_all | solution.py:165
  88.7 3.2 %shard_map.42 = (f32[16,16,512]{2,1,0:T(8,128)S(1)}, bf16[16,16,512]{2,1,0:T(8,128)(2,1)S(1)}) custom-call(bf16[128,2048]{1,0:T(8,128)(2,1)S(1)} %constant_dynamic-update-slice_fusion.refs_0_, bf16[128,2048]{1,0:T(8,128)(2,1)S(1)} %collective-permute-done.4.refs_1_, bf16[128,2048]{1,0:T(8,128)(2,1)} %collective-permute-done.5.refs_2_, ...), custom_call_target="tpu_custom_call" | custom-call | tf_op jit(solution)/shard_map/pallas_call | solution.py:243
  91.9 1.9 %collective-permute-start.12 = (bf16[16,16,512]{2,1,0:T(8,128)(2,1)S(1)}, bf16[16,16,512]{2,1,0:T(8,128)(2,1)S(1)}, u32[]{:S(2)}, u32[]{:S(2)}) collective-permute-start(bf16[16,16,512]{2,1,0:T(8,128)(2,1)S(1)} %get-tuple-element.28), channel_id=1, source_target_pairs={{0,64},{64,0},{1,65},{65,1},{2,66},{66,2},{3,67},{67,3},{4,68},{68... | collective-permute-start | bytes 786440 | tf_op jit(solution)/shard_map/ppermute | solution.py:161
  93.8 1.5 %collective-permute-done.12 = bf16[16,16,512]{2,1,0:T(8,128)(2,1)S(1)} collective-permute-done((bf16[16,16,512]{2,1,0:T(8,128)(2,1)S(1)}, bf16[16,16,512]{2,1,0:T(8,128)(2,1)S(1)}, u32[]{:S(2)}, u32[]{:S(2)}) %collective-permute-start.12) | collective-permute-done | bytes 262176 | tf_op jit(solution)/shard_map/ppermute | solution.py:161
  96.3 4.2 %all-to-all-start.3 = ((bf16[2,16,16,512]{3,2,1,0:T(8,128)(2,1)}), bf16[2,16,16,512]{3,2,1,0:T(8,128)(2,1)}, u32[]{:S(2)}, u32[]{:S(2)}) async-start(bf16[2,16,16,512]{3,2,1,0:T(8,128)(2,1)} %pad_maximum_fusion), calls=%async_computation.3 | async-start | bytes 1048576 | tf_op jit(solution)/shard_map/all_to_all | solution.py:253
  102.3 3.2 %shard_map.41 = (f32[16,16,512]{2,1,0:T(8,128)S(1)}, bf16[16,16,512]{2,1,0:T(8,128)(2,1)S(1)}) custom-call(bf16[128,2048]{1,0:T(8,128)(2,1)S(1)} %constant_dynamic-update-slice_fusion.refs_0_, bf16[128,2048]{1,0:T(8,128)(2,1)S(1)} %collective-permute-done.4.refs_1_, bf16[128,2048]{1,0:T(8,128)(2,1)} %collective-permute-done.5.refs_2_, ...), custom_call_target="tpu_custom_call" | custom-call | tf_op jit(solution)/shard_map/pallas_call | solution.py:243
  106.3 2.0 %collective-permute-start.11 = (bf16[16,16,512]{2,1,0:T(8,128)(2,1)S(1)}, bf16[16,16,512]{2,1,0:T(8,128)(2,1)S(1)}, u32[]{:S(2)}, u32[]{:S(2)}) collective-permute-start(bf16[16,16,512]{2,1,0:T(8,128)(2,1)S(1)} %get-tuple-element.26), channel_id=1, source_target_pairs={{0,64},{64,0},{1,65},{65,1},{2,66},{66,2},{3,67},{67,3},{4,68},{68... | collective-permute-start | bytes 786440 | tf_op jit(solution)/shard_map/ppermute | solution.py:161
  109.7 5.0 %all-to-all-done.3 = bf16[2,16,16,512]{3,2,1,0:T(8,128)(2,1)} async-done(((bf16[2,16,16,512]{3,2,1,0:T(8,128)(2,1)}), bf16[2,16,16,512]{3,2,1,0:T(8,128)(2,1)}, u32[]{:S(2)}, u32[]{:S(2)}) %all-to-all-start.3) | async-done | bytes 524320 | tf_op jit(solution)/shard_map/all_to_all | solution.py:253
  116.0 25.6 %all_to_all.32 = f32[32,4,128]{2,1,0:T(4,128)S(1)} all-to-all(f32[32,4,128]{2,1,0:T(4,128)S(1)} %broadcast_in_dim.28), channel_id=1, replica_groups=mesh['x'=4,'core'=2,'z1'=2,'z0'=2,'y'=4,'zhi'=4] {'x','core','zhi'}, dimensions={0} | all-to-all | bytes 131072 | tf_op jit(solution)/shard_map/all_to_all | solution.py:165
  (44 shorter events, 11.4 us)
Async XLA Ops:
  0.0 1.2 copy-start
  1.2 0.8 copy-start.2
  4.3 24.9 %all-to-all-start = ((bf16[32,64,256]{2,1,0:T(8,128)(2,1)}), bf16[32,64,256]{2,1,0:T(8,128)(2,1)S(1)}, u32[]{:S(2)}, u32[]{:S(2)}) async-start(bf16[32,64,256]{2,1,0:T(8,128)(2,1)} %shard_map.37.out_ref), calls=%async_computation | async-start | bytes 2097152 | tf_op jit(solution)/shard_map/all_to_all | solution.py:180
  15.0 10.5 %collective-permute-start = (bf16[64,2048]{1,0:T(8,128)(2,1)S(1)}, bf16[64,2048]{1,0:T(8,128)(2,1)S(1)}, u32[]{:S(2)}, u32[]{:S(2)}) collective-permute-start(bf16[64,2048]{1,0:T(8,128)(2,1)S(1)} %get-tuple-element.30), channel_id=1, source_target_pairs={{0,51},{48,1},{16,32},{32,16},{1,48},{49,2},{17,33},{33,17},{2,49}... | collective-permute-start | bytes 786440 | tf_op jit(solution)/shard_map/ppermute | solution.py:187
  18.4 10.9 %collective-permute-start.2 = (bf16[64,2048]{1,0:T(8,128)(2,1)S(1)}, bf16[64,2048]{1,0:T(8,128)(2,1)S(1)}, u32[]{:S(2)}, u32[]{:S(2)}) collective-permute-start(bf16[64,2048]{1,0:T(8,128)(2,1)S(1)} %get-tuple-element.29), channel_id=1, source_target_pairs={{0,115},{48,65},{16,96},{32,80},{1,112},{49,66},{17,97},{33,81},{2... | collective-permute-start | bytes 786440 | tf_op jit(solution)/shard_map/ppermute | solution.py:188
  25.5 3.8 %collective-permute-start.1 = (bf16[64,2048]{1,0:T(8,128)(2,1)S(1)}, bf16[64,2048]{1,0:T(8,128)(2,1)S(1)}, u32[]{:S(2)}, u32[]{:S(2)}) collective-permute-start(bf16[64,2048]{1,0:T(8,128)(2,1)S(1)} %get-tuple-element.17), channel_id=1, source_target_pairs={{0,64},{64,0},{1,65},{65,1},{2,66},{66,2},{3,67},{67,3},{4,68},{68... | collective-permute-start | bytes 786440 | tf_op jit(solution)/shard_map/ppermute | solution.py:161
  31.3 34.9 %collective-permute-start.7 = (bf16[256,2048]{1,0:T(8,128)(2,1)S(1)}, bf16[256,2048]{1,0:T(8,128)(2,1)S(1)}, u32[]{:S(2)}, u32[]{:S(2)}) collective-permute-start(bf16[256,2048]{1,0:T(8,128)(2,1)S(1)} %bitcast.28), channel_id=1, source_target_pairs={{0,128},{128,256},{256,384},{384,0},{1,129},{129,257},{257,385},{3... | collective-permute-start | bytes 3145736 | tf_op jit(solution)/shard_map/ppermute | solution.py:213
  34.7 31.5 %collective-permute-start.8 = (bf16[256,2048]{1,0:T(8,128)(2,1)S(1)}, bf16[256,2048]{1,0:T(8,128)(2,1)}, u32[]{:S(2)}, u32[]{:S(2)}) collective-permute-start(bf16[256,2048]{1,0:T(8,128)(2,1)S(1)} %bitcast.29), channel_id=1, source_target_pairs={{0,384},{128,0},{256,128},{384,256},{1,385},{129,1},{257,129},{385... | collective-permute-start | bytes 3145736 | tf_op jit(solution)/shard_map/ppermute | solution.py:213
  38.3 16.5 %collective-permute-start.3 = (bf16[64,2048]{1,0:T(8,128)(2,1)S(1)}, bf16[64,2048]{1,0:T(8,128)(2,1)S(1)}, u32[]{:S(2)}, u32[]{:S(2)}) collective-permute-start(bf16[64,2048]{1,0:T(8,128)(2,1)S(1)} %get-tuple-element.19), channel_id=1, source_target_pairs={{0,16},{16,0},{1,17},{17,1},{2,18},{18,2},{3,19},{19,3},{4,20},{20... | collective-permute-start | bytes 786440 | tf_op jit(solution)/shard_map/ppermute | solution.py:211
  48.9 17.3 %all-to-all-start.1 = ((f32[32,1,64]{2,1,0:T(1,128)}), f32[32,1,64]{2,1,0:T(1,128)S(1)}, u32[]{:S(2)}, u32[]{:S(2)}) async-start(f32[32,1,64]{2,1,0:T(1,128)} %bitcast.6), calls=%async_computation.1 | async-start | bytes 32768 | tf_op jit(solution)/shard_map/all_to_all | solution.py:216
  54.8 24.7 %collective-permute-start.4 = (bf16[128,2048]{1,0:T(8,128)(2,1)S(1)}, bf16[128,2048]{1,0:T(8,128)(2,1)S(1)}, u32[]{:S(2)}, u32[]{:S(2)}) collective-permute-start(bf16[128,2048]{1,0:T(8,128)(2,1)S(1)} %constant_dynamic-update-slice_fusion.refs_0_), channel_id=1, source_target_pairs={{0,4},{4,8},{8,12},{12,0},{1,5},{5,9},{9,13},{13,1},{2,6},{6,10},{... | collective-permute-start | bytes 1572872 | tf_op jit(solution)/shard_map/ppermute | solution.py:224
  58.2 26.0 %collective-permute-start.5 = (bf16[128,2048]{1,0:T(8,128)(2,1)S(1)}, bf16[128,2048]{1,0:T(8,128)(2,1)}, u32[]{:S(2)}, u32[]{:S(2)}) collective-permute-start(bf16[128,2048]{1,0:T(8,128)(2,1)S(1)} %constant_dynamic-update-slice_fusion.refs_0_), channel_id=1, source_target_pairs={{0,8},{4,12},{8,0},{12,4},{1,9},{5,13},{9,1},{13,5},{2,10},{6,14},... | collective-permute-start | bytes 1572872 | tf_op jit(solution)/shard_map/ppermute | solution.py:224
  62.8 23.0 %collective-permute-start.6 = (bf16[128,2048]{1,0:T(8,128)(2,1)S(1)}, bf16[128,2048]{1,0:T(8,128)(2,1)}, u32[]{:S(2)}, u32[]{:S(2)}) collective-permute-start(bf16[128,2048]{1,0:T(8,128)(2,1)S(1)} %constant_dynamic-update-slice_fusion.refs_0_), channel_id=1, source_target_pairs={{0,12},{4,0},{8,4},{12,8},{1,13},{5,1},{9,5},{13,9},{2,14},{6,2},{... | collective-permute-start | bytes 1572872 | tf_op jit(solution)/shard_map/ppermute | solution.py:224
  68.1 20.6 %collective-permute-start.10 = (bf16[128,2048]{1,0:T(8,128)(2,1)}, bf16[128,2048]{1,0:T(8,128)(2,1)}, u32[]{:S(2)}, u32[]{:S(2)}) collective-permute-start(bf16[128,2048]{1,0:T(8,128)(2,1)} %slice.31), channel_id=1, source_target_pairs={{0,384},{128,0},{256,128},{384,256},{1,385},{129,1},{257,129},{385... | collective-permute-start | bytes 1572872 | tf_op jit(solution)/shard_map/ppermute | solution.py:213
  72.4 16.3 %collective-permute-start.9 = (bf16[128,2048]{1,0:T(8,128)(2,1)}, bf16[128,2048]{1,0:T(8,128)(2,1)}, u32[]{:S(2)}, u32[]{:S(2)}) collective-permute-start(bf16[128,2048]{1,0:T(8,128)(2,1)} %slice.30), channel_id=1, source_target_pairs={{0,128},{128,256},{256,384},{384,0},{1,129},{129,257},{257,385},{3... | collective-permute-start | bytes 1572872 | tf_op jit(solution)/shard_map/ppermute | solution.py:213
  75.5 13.2 %all-to-all-start.2 = ((f32[4,4,128]{2,1,0:T(4,128)}), f32[4,4,128]{2,1,0:T(4,128)S(1)}, u32[]{:S(2)}, u32[]{:S(2)}) async-start(f32[4,4,128]{2,1,0:T(4,128)} %broadcast_in_dim.25), calls=%async_computation.2 | async-start | bytes 16384 | tf_op jit(solution)/shard_map/all_to_all | solution.py:165
  91.9 3.4 %collective-permute-start.12 = (bf16[16,16,512]{2,1,0:T(8,128)(2,1)S(1)}, bf16[16,16,512]{2,1,0:T(8,128)(2,1)S(1)}, u32[]{:S(2)}, u32[]{:S(2)}) collective-permute-start(bf16[16,16,512]{2,1,0:T(8,128)(2,1)S(1)} %get-tuple-element.28), channel_id=1, source_target_pairs={{0,64},{64,0},{1,65},{65,1},{2,66},{66,2},{3,67},{67,3},{4,68},{68... | collective-permute-start | bytes 786440 | tf_op jit(solution)/shard_map/ppermute | solution.py:161
  96.3 18.5 %all-to-all-start.3 = ((bf16[2,16,16,512]{3,2,1,0:T(8,128)(2,1)}), bf16[2,16,16,512]{3,2,1,0:T(8,128)(2,1)}, u32[]{:S(2)}, u32[]{:S(2)}) async-start(bf16[2,16,16,512]{3,2,1,0:T(8,128)(2,1)} %pad_maximum_fusion), calls=%async_computation.3 | async-start | bytes 1048576 | tf_op jit(solution)/shard_map/all_to_all | solution.py:253
  100.5 0.8 copy-start.3
  105.5 0.8 copy-start.1
  106.3 3.4 %collective-permute-start.11 = (bf16[16,16,512]{2,1,0:T(8,128)(2,1)S(1)}, bf16[16,16,512]{2,1,0:T(8,128)(2,1)S(1)}, u32[]{:S(2)}, u32[]{:S(2)}) collective-permute-start(bf16[16,16,512]{2,1,0:T(8,128)(2,1)S(1)} %get-tuple-element.26), channel_id=1, source_target_pairs={{0,64},{64,0},{1,65},{65,1},{2,66},{66,2},{3,67},{67,3},{4,68},{68... | collective-permute-start | bytes 786440 | tf_op jit(solution)/shard_map/ppermute | solution.py:161

commit v10 on v9

--- a/solution.py
+++ b/solution.py
@@ -73,8 +73,8 @@
 
     for p in range(ny):
         cols = slice(p * BLK, (p + 1) * BLK)
-        got = recv_ref[2 * p : 2 * p + 2].reshape(BLK, 2 * BLK).astype(F32)
-        flip_ref[...] = got.T.reshape(flip_ref.shape)
+        got = recv_ref[2 * p : 2 * p + 2].reshape(BLK, 2 * BLK)
+        flip_ref[...] = got.T.astype(F32).reshape(flip_ref.shape)
         for i, direct in enumerate((d00, d01, d10, d11)):
             b, c = i // 2, i % 2
             spot = jnp.where(z1 == b, 0, 2) + jnp.where(core == c, 0, 1)

time: 144 us -> 144 us (level)
  no operation moved by 1% of the time
where the time goes in v10:
time: 144 us; the launch traced here: 142 us
  starting transfers between devices  68.5 us (48%)
  blocking collectives  25.6 us (18%)
  waiting for transfers between devices  21.5 us (15%)
  Pallas kernels  13.4 us (9%)
  local copies, waits for them, and re-layouts  9.85 us (7%)
  other arithmetic  3.16 us (2%)
    all_to_all x1, blocking collectives, spread(): return lax.all_to_all(wide, axes, split_axis=0, concat_axis=0, tiled=True)  25.6 us
    ppermute x4, starting transfers between devices, step_x(): return lax.ppermute(piece, 'x', [(i, (i + d) % nx) for i in range(nx)])  12.9 us
    ppermute x3, starting transfers between devices, on_device(): lax.ppermute(near, 'y', [(i, (i + d) % ny) for i in range(ny)])  11.3 us
    ppermute x1, starting transfers between devices, on_device(): near = jnp.concatenate([shard, lax.ppermute(shard, 'z0', SWAP)], axis=0)  9.94 us
    all_to_all x1, starting transfers between devices, on_device(): lax.all_to_all(outgoing, group, split_axis=0, concat_axis=0, tiled=True)  9.08 us
    pallas_call x2, Pallas kernels, product(): call(functools.partial(product_kernel, group, ny), in_specs=[vmem] * (ny...  6.39 us
    ppermute x3, waiting for transfers between devices, on_device(): lax.ppermute(near, 'y', [(i, (i + d) % ny) for i in range(ny)])  6.27 us
    all_to_all x1, starting transfers between devices, on_device(): lax.all_to_all(partial.reshape(8 * ny, rows_dev), ('core', 'z1', 'z0', 'y...  5.86 us
  transfers between devices with their start and end apart: 17, of which 8 were waited for; matrix products, arithmetic and copies ran while one was open for 4% of the time, Pallas kernels for 4%

profile of v10, /device:TPU:32, one launch (start us, length us, event | category | flops | bytes accessed | tf_op | source)
XLA Modules:
  0.0 142.3 jit_solution(13487589362821298660)
XLA Ops:
  2.0 2.3 %shard_map.37.out_ref = bf16[32,64,256]{2,1,0:T(8,128)(2,1)} custom-call(s32[64,64]{1,0:T(8,128)S(1)} %copy-done.2, bf16[1,64,8192]{2,1,0:T(8,128)(2,1)S(1)} %copy-done), custom_call_target="tpu_custom_call" | custom-call | tf_op jit(solution)/shard_map/pallas_call | solution.py:174
  4.3 9.1 %all-to-all-start = ((bf16[32,64,256]{2,1,0:T(8,128)(2,1)}), bf16[32,64,256]{2,1,0:T(8,128)(2,1)S(1)}, u32[]{:S(2)}, u32[]{:S(2)}) async-start(bf16[32,64,256]{2,1,0:T(8,128)(2,1)} %shard_map.37.out_ref), calls=%async_computation | async-start | bytes 2097152 | tf_op jit(solution)/shard_map/all_to_all | solution.py:180
  13.4 1.5 %shard_map.39 = bf16[2,64,2048]{2,1,0:T(8,128)(2,1)S(1)} custom-call(bf16[32,64,256]{2,1,0:T(8,128)(2,1)} %shard_map.37.out_ref), custom_call_target="tpu_custom_call" | custom-call | tf_op jit(solution)/shard_map/pallas_call | solution.py:182
  15.0 3.4 %collective-permute-start = (bf16[64,2048]{1,0:T(8,128)(2,1)S(1)}, bf16[64,2048]{1,0:T(8,128)(2,1)S(1)}, u32[]{:S(2)}, u32[]{:S(2)}) collective-permute-start(bf16[64,2048]{1,0:T(8,128)(2,1)S(1)} %get-tuple-element.30), channel_id=1, source_target_pairs={{0,51},{48,1},{16,32},{32,16},{1,48},{49,2},{17,33},{33,17},{2,49}... | collective-permute-start | bytes 786440 | tf_op jit(solution)/shard_map/ppermute | solution.py:187
  18.4 1.9 %collective-permute-start.2 = (bf16[64,2048]{1,0:T(8,128)(2,1)S(1)}, bf16[64,2048]{1,0:T(8,128)(2,1)S(1)}, u32[]{:S(2)}, u32[]{:S(2)}) collective-permute-start(bf16[64,2048]{1,0:T(8,128)(2,1)S(1)} %get-tuple-element.29), channel_id=1, source_target_pairs={{0,115},{48,65},{16,96},{32,80},{1,112},{49,66},{17,97},{33,81},{2... | collective-permute-start | bytes 786440 | tf_op jit(solution)/shard_map/ppermute | solution.py:188
  20.3 1.5 %shard_map.38 = bf16[2,64,2048]{2,1,0:T(8,128)(2,1)S(1)} custom-call(bf16[32,64,256]{2,1,0:T(8,128)(2,1)} %shard_map.37.out_ref), custom_call_target="tpu_custom_call" | custom-call | tf_op jit(solution)/shard_map/pallas_call | solution.py:182
  21.8 3.6 %collective-permute-done.d10 = bf16[64,2048]{1,0:T(8,128)(2,1)S(1)} collective-permute-done((bf16[64,2048]{1,0:T(8,128)(2,1)S(1)}, bf16[64,2048]{1,0:T(8,128)(2,1)S(1)}, u32[]{:S(2)}, u32[]{:S(2)}) %collective-permute-start) | collective-permute-done | bytes 262176 | tf_op jit(solution)/shard_map/ppermute | solution.py:187
  25.5 1.9 %collective-permute-start.1 = (bf16[64,2048]{1,0:T(8,128)(2,1)S(1)}, bf16[64,2048]{1,0:T(8,128)(2,1)S(1)}, u32[]{:S(2)}, u32[]{:S(2)}) collective-permute-start(bf16[64,2048]{1,0:T(8,128)(2,1)S(1)} %get-tuple-element.17), channel_id=1, source_target_pairs={{0,64},{64,0},{1,65},{65,1},{2,66},{66,2},{3,67},{67,3},{4,68},{68... | collective-permute-start | bytes 786440 | tf_op jit(solution)/shard_map/ppermute | solution.py:161
  27.4 1.9 %collective-permute-done.2.d11 = bf16[64,2048]{1,0:T(8,128)(2,1)S(1)} collective-permute-done((bf16[64,2048]{1,0:T(8,128)(2,1)S(1)}, bf16[64,2048]{1,0:T(8,128)(2,1)S(1)}, u32[]{:S(2)}, u32[]{:S(2)}) %collective-permute-start.2) | collective-permute-done | bytes 262176 | tf_op jit(solution)/shard_map/ppermute | solution.py:188
  29.3 1.7 %shard_map.40 = (bf16[4,64,2048]{2,1,0:T(8,128)(2,1)S(1)}, bf16[64,2048]{1,0:T(8,128)(2,1)S(1)}, f32[4,64]{1,0:T(4,128)S(1)}) custom-call(bf16[32,64,256]{2,1,0:T(8,128)(2,1)S(1)} %all-to-all-done.recv_ref, bf16[64,2048]{1,0:T(8,128)(2,1)S(1)} %get-tuple-element.32.d00, bf16[64,2048]{1,0:T(8,128)(2,1)S(1)} %collective-permute-done.1.d01, ...), custom_call_target="tpu_custom_call" | custom-call | tf_op jit(solution)/shard_map/pallas_call | solution.py:191
  31.0 3.4 %collective-permute-start.7 = (bf16[256,2048]{1,0:T(8,128)(2,1)S(1)}, bf16[256,2048]{1,0:T(8,128)(2,1)S(1)}, u32[]{:S(2)}, u32[]{:S(2)}) collective-permute-start(bf16[256,2048]{1,0:T(8,128)(2,1)S(1)} %bitcast.28), channel_id=1, source_target_pairs={{0,128},{128,256},{256,384},{384,0},{1,129},{129,257},{257,385},{3... | collective-permute-start | bytes 3145736 | tf_op jit(solution)/shard_map/ppermute | solution.py:213
  34.4 3.6 %collective-permute-start.8 = (bf16[256,2048]{1,0:T(8,128)(2,1)S(1)}, bf16[256,2048]{1,0:T(8,128)(2,1)}, u32[]{:S(2)}, u32[]{:S(2)}) collective-permute-start(bf16[256,2048]{1,0:T(8,128)(2,1)S(1)} %bitcast.29), channel_id=1, source_target_pairs={{0,384},{128,0},{256,128},{384,256},{1,385},{129,1},{257,129},{385... | collective-permute-start | bytes 3145736 | tf_op jit(solution)/shard_map/ppermute | solution.py:213
  38.0 9.9 %collective-permute-start.3 = (bf16[64,2048]{1,0:T(8,128)(2,1)S(1)}, bf16[64,2048]{1,0:T(8,128)(2,1)S(1)}, u32[]{:S(2)}, u32[]{:S(2)}) collective-permute-start(bf16[64,2048]{1,0:T(8,128)(2,1)S(1)} %get-tuple-element.19), channel_id=1, source_target_pairs={{0,16},{16,0},{1,17},{17,1},{2,18},{18,2},{3,19},{19,3},{4,20},{20... | collective-permute-start | bytes 786440 | tf_op jit(solution)/shard_map/ppermute | solution.py:211
  48.6 5.9 %all-to-all-start.1 = ((f32[32,1,64]{2,1,0:T(1,128)}), f32[32,1,64]{2,1,0:T(1,128)S(1)}, u32[]{:S(2)}, u32[]{:S(2)}) async-start(f32[32,1,64]{2,1,0:T(1,128)} %bitcast.6), calls=%async_computation.1 | async-start | bytes 32768 | tf_op jit(solution)/shard_map/all_to_all | solution.py:216
  54.5 3.4 %collective-permute-start.4 = (bf16[128,2048]{1,0:T(8,128)(2,1)S(1)}, bf16[128,2048]{1,0:T(8,128)(2,1)S(1)}, u32[]{:S(2)}, u32[]{:S(2)}) collective-permute-start(bf16[128,2048]{1,0:T(8,128)(2,1)S(1)} %constant_dynamic-update-slice_fusion.refs_0_), channel_id=1, source_target_pairs={{0,4},{4,8},{8,12},{12,0},{1,5},{5,9},{9,13},{13,1},{2,6},{6,10},{... | collective-permute-start | bytes 1572872 | tf_op jit(solution)/shard_map/ppermute | solution.py:224
  57.9 4.6 %collective-permute-start.5 = (bf16[128,2048]{1,0:T(8,128)(2,1)S(1)}, bf16[128,2048]{1,0:T(8,128)(2,1)}, u32[]{:S(2)}, u32[]{:S(2)}) collective-permute-start(bf16[128,2048]{1,0:T(8,128)(2,1)S(1)} %constant_dynamic-update-slice_fusion.refs_0_), channel_id=1, source_target_pairs={{0,8},{4,12},{8,0},{12,4},{1,9},{5,13},{9,1},{13,5},{2,10},{6,14},... | collective-permute-start | bytes 1572872 | tf_op jit(solution)/shard_map/ppermute | solution.py:224
  62.5 3.4 %collective-permute-start.6 = (bf16[128,2048]{1,0:T(8,128)(2,1)S(1)}, bf16[128,2048]{1,0:T(8,128)(2,1)}, u32[]{:S(2)}, u32[]{:S(2)}) collective-permute-start(bf16[128,2048]{1,0:T(8,128)(2,1)S(1)} %constant_dynamic-update-slice_fusion.refs_0_), channel_id=1, source_target_pairs={{0,12},{4,0},{8,4},{12,8},{1,13},{5,1},{9,5},{13,9},{2,14},{6,2},{... | collective-permute-start | bytes 1572872 | tf_op jit(solution)/shard_map/ppermute | solution.py:224
  65.9 1.9 %slice.31 = bf16[128,2048]{1,0:T(8,128)(2,1)} slice(bf16[256,2048]{1,0:T(8,128)(2,1)} %collective-permute-done.8.refs_8_), slice={[128:256], [0:2048]} | slice | bytes 1048576 | tf_op jit(solution)/shard_map/slice | solution.py:232
  67.8 3.4 %collective-permute-start.10 = (bf16[128,2048]{1,0:T(8,128)(2,1)}, bf16[128,2048]{1,0:T(8,128)(2,1)}, u32[]{:S(2)}, u32[]{:S(2)}) collective-permute-start(bf16[128,2048]{1,0:T(8,128)(2,1)} %slice.31), channel_id=1, source_target_pairs={{0,384},{128,0},{256,128},{384,256},{1,385},{129,1},{257,129},{385... | collective-permute-start | bytes 1572872 | tf_op jit(solution)/shard_map/ppermute | solution.py:213
  72.1 2.4 %collective-permute-start.9 = (bf16[128,2048]{1,0:T(8,128)(2,1)}, bf16[128,2048]{1,0:T(8,128)(2,1)}, u32[]{:S(2)}, u32[]{:S(2)}) collective-permute-start(bf16[128,2048]{1,0:T(8,128)(2,1)} %slice.30), channel_id=1, source_target_pairs={{0,128},{128,256},{256,384},{384,0},{1,129},{129,257},{257,385},{3... | collective-permute-start | bytes 1572872 | tf_op jit(solution)/shard_map/ppermute | solution.py:213
  75.2 4.0 %all-to-all-start.2 = ((f32[4,4,128]{2,1,0:T(4,128)}), f32[4,4,128]{2,1,0:T(4,128)S(1)}, u32[]{:S(2)}, u32[]{:S(2)}) async-start(f32[4,4,128]{2,1,0:T(4,128)} %broadcast_in_dim.25), calls=%async_computation.2 | async-start | bytes 16384 | tf_op jit(solution)/shard_map/all_to_all | solution.py:165
  79.2 4.6 %collective-permute-done.5.refs_2_ = bf16[128,2048]{1,0:T(8,128)(2,1)} collective-permute-done((bf16[128,2048]{1,0:T(8,128)(2,1)S(1)}, bf16[128,2048]{1,0:T(8,128)(2,1)}, u32[]{:S(2)}, u32[]{:S(2)}) %collective-permute-start.5) | collective-permute-done | bytes 524320 | tf_op jit(solution)/shard_map/ppermute | solution.py:224
  83.9 1.6 %collective-permute-done.6.refs_3_ = bf16[128,2048]{1,0:T(8,128)(2,1)} collective-permute-done((bf16[128,2048]{1,0:T(8,128)(2,1)S(1)}, bf16[128,2048]{1,0:T(8,128)(2,1)}, u32[]{:S(2)}, u32[]{:S(2)}) %collective-permute-start.6) | collective-permute-done | bytes 524320 | tf_op jit(solution)/shard_map/ppermute | solution.py:224
  85.5 2.9 %all-to-all-done.2 = f32[4,4,128]{2,1,0:T(4,128)S(1)} async-done(((f32[4,4,128]{2,1,0:T(4,128)}), f32[4,4,128]{2,1,0:T(4,128)S(1)}, u32[]{:S(2)}, u32[]{:S(2)}) %all-to-all-start.2) | async-done | bytes 8224 | tf_op jit(solution)/shard_map/all_to_all | solution.py:165
  88.4 3.2 %shard_map.42 = (f32[16,16,512]{2,1,0:T(8,128)S(1)}, bf16[16,16,512]{2,1,0:T(8,128)(2,1)S(1)}) custom-call(bf16[128,2048]{1,0:T(8,128)(2,1)S(1)} %constant_dynamic-update-slice_fusion.refs_0_, bf16[128,2048]{1,0:T(8,128)(2,1)S(1)} %collective-permute-done.4.refs_1_, bf16[128,2048]{1,0:T(8,128)(2,1)} %collective-permute-done.5.refs_2_, ...), custom_call_target="tpu_custom_call" | custom-call | tf_op jit(solution)/shard_map/pallas_call | solution.py:243
  91.6 1.9 %collective-permute-start.12 = (bf16[16,16,512]{2,1,0:T(8,128)(2,1)S(1)}, bf16[16,16,512]{2,1,0:T(8,128)(2,1)S(1)}, u32[]{:S(2)}, u32[]{:S(2)}) collective-permute-start(bf16[16,16,512]{2,1,0:T(8,128)(2,1)S(1)} %get-tuple-element.28), channel_id=1, source_target_pairs={{0,64},{64,0},{1,65},{65,1},{2,66},{66,2},{3,67},{67,3},{4,68},{68... | collective-permute-start | bytes 786440 | tf_op jit(solution)/shard_map/ppermute | solution.py:161
  93.6 1.5 %collective-permute-done.12 = bf16[16,16,512]{2,1,0:T(8,128)(2,1)S(1)} collective-permute-done((bf16[16,16,512]{2,1,0:T(8,128)(2,1)S(1)}, bf16[16,16,512]{2,1,0:T(8,128)(2,1)S(1)}, u32[]{:S(2)}, u32[]{:S(2)}) %collective-permute-start.12) | collective-permute-done | bytes 262176 | tf_op jit(solution)/shard_map/ppermute | solution.py:161
  96.0 4.2 %all-to-all-start.3 = ((bf16[2,16,16,512]{3,2,1,0:T(8,128)(2,1)}), bf16[2,16,16,512]{3,2,1,0:T(8,128)(2,1)}, u32[]{:S(2)}, u32[]{:S(2)}) async-start(bf16[2,16,16,512]{3,2,1,0:T(8,128)(2,1)} %pad_maximum_fusion), calls=%async_computation.3 | async-start | bytes 1048576 | tf_op jit(solution)/shard_map/all_to_all | solution.py:253
  102.0 3.2 %shard_map.41 = (f32[16,16,512]{2,1,0:T(8,128)S(1)}, bf16[16,16,512]{2,1,0:T(8,128)(2,1)S(1)}) custom-call(bf16[128,2048]{1,0:T(8,128)(2,1)S(1)} %constant_dynamic-update-slice_fusion.refs_0_, bf16[128,2048]{1,0:T(8,128)(2,1)S(1)} %collective-permute-done.4.refs_1_, bf16[128,2048]{1,0:T(8,128)(2,1)} %collective-permute-done.5.refs_2_, ...), custom_call_target="tpu_custom_call" | custom-call | tf_op jit(solution)/shard_map/pallas_call | solution.py:243
  106.0 2.0 %collective-permute-start.11 = (bf16[16,16,512]{2,1,0:T(8,128)(2,1)S(1)}, bf16[16,16,512]{2,1,0:T(8,128)(2,1)S(1)}, u32[]{:S(2)}, u32[]{:S(2)}) collective-permute-start(bf16[16,16,512]{2,1,0:T(8,128)(2,1)S(1)} %get-tuple-element.26), channel_id=1, source_target_pairs={{0,64},{64,0},{1,65},{65,1},{2,66},{66,2},{3,67},{67,3},{4,68},{68... | collective-permute-start | bytes 786440 | tf_op jit(solution)/shard_map/ppermute | solution.py:161
  109.5 5.0 %all-to-all-done.3 = bf16[2,16,16,512]{3,2,1,0:T(8,128)(2,1)} async-done(((bf16[2,16,16,512]{3,2,1,0:T(8,128)(2,1)}), bf16[2,16,16,512]{3,2,1,0:T(8,128)(2,1)}, u32[]{:S(2)}, u32[]{:S(2)}) %all-to-all-start.3) | async-done | bytes 524320 | tf_op jit(solution)/shard_map/all_to_all | solution.py:253
  115.7 25.6 %all_to_all.32 = f32[32,4,128]{2,1,0:T(4,128)S(1)} all-to-all(f32[32,4,128]{2,1,0:T(4,128)S(1)} %broadcast_in_dim.28), channel_id=1, replica_groups=mesh['x'=4,'core'=2,'z1'=2,'z0'=2,'y'=4,'zhi'=4] {'x','core','zhi'}, dimensions={0} | all-to-all | bytes 131072 | tf_op jit(solution)/shard_map/all_to_all | solution.py:165
  (44 shorter events, 11.4 us)
Async XLA Ops:
  0.0 1.2 copy-start
  1.2 0.8 copy-start.2
  4.3 24.9 %all-to-all-start = ((bf16[32,64,256]{2,1,0:T(8,128)(2,1)}), bf16[32,64,256]{2,1,0:T(8,128)(2,1)S(1)}, u32[]{:S(2)}, u32[]{:S(2)}) async-start(bf16[32,64,256]{2,1,0:T(8,128)(2,1)} %shard_map.37.out_ref), calls=%async_computation | async-start | bytes 2097152 | tf_op jit(solution)/shard_map/all_to_all | solution.py:180
  15.0 10.5 %collective-permute-start = (bf16[64,2048]{1,0:T(8,128)(2,1)S(1)}, bf16[64,2048]{1,0:T(8,128)(2,1)S(1)}, u32[]{:S(2)}, u32[]{:S(2)}) collective-permute-start(bf16[64,2048]{1,0:T(8,128)(2,1)S(1)} %get-tuple-element.30), channel_id=1, source_target_pairs={{0,51},{48,1},{16,32},{32,16},{1,48},{49,2},{17,33},{33,17},{2,49}... | collective-permute-start | bytes 786440 | tf_op jit(solution)/shard_map/ppermute | solution.py:187
  18.4 10.9 %collective-permute-start.2 = (bf16[64,2048]{1,0:T(8,128)(2,1)S(1)}, bf16[64,2048]{1,0:T(8,128)(2,1)S(1)}, u32[]{:S(2)}, u32[]{:S(2)}) collective-permute-start(bf16[64,2048]{1,0:T(8,128)(2,1)S(1)} %get-tuple-element.29), channel_id=1, source_target_pairs={{0,115},{48,65},{16,96},{32,80},{1,112},{49,66},{17,97},{33,81},{2... | collective-permute-start | bytes 786440 | tf_op jit(solution)/shard_map/ppermute | solution.py:188
  25.5 3.8 %collective-permute-start.1 = (bf16[64,2048]{1,0:T(8,128)(2,1)S(1)}, bf16[64,2048]{1,0:T(8,128)(2,1)S(1)}, u32[]{:S(2)}, u32[]{:S(2)}) collective-permute-start(bf16[64,2048]{1,0:T(8,128)(2,1)S(1)} %get-tuple-element.17), channel_id=1, source_target_pairs={{0,64},{64,0},{1,65},{65,1},{2,66},{66,2},{3,67},{67,3},{4,68},{68... | collective-permute-start | bytes 786440 | tf_op jit(solution)/shard_map/ppermute | solution.py:161
  31.0 34.9 %collective-permute-start.7 = (bf16[256,2048]{1,0:T(8,128)(2,1)S(1)}, bf16[256,2048]{1,0:T(8,128)(2,1)S(1)}, u32[]{:S(2)}, u32[]{:S(2)}) collective-permute-start(bf16[256,2048]{1,0:T(8,128)(2,1)S(1)} %bitcast.28), channel_id=1, source_target_pairs={{0,128},{128,256},{256,384},{384,0},{1,129},{129,257},{257,385},{3... | collective-permute-start | bytes 3145736 | tf_op jit(solution)/shard_map/ppermute | solution.py:213
  34.4 31.5 %collective-permute-start.8 = (bf16[256,2048]{1,0:T(8,128)(2,1)S(1)}, bf16[256,2048]{1,0:T(8,128)(2,1)}, u32[]{:S(2)}, u32[]{:S(2)}) collective-permute-start(bf16[256,2048]{1,0:T(8,128)(2,1)S(1)} %bitcast.29), channel_id=1, source_target_pairs={{0,384},{128,0},{256,128},{384,256},{1,385},{129,1},{257,129},{385... | collective-permute-start | bytes 3145736 | tf_op jit(solution)/shard_map/ppermute | solution.py:213
  38.0 16.5 %collective-permute-start.3 = (bf16[64,2048]{1,0:T(8,128)(2,1)S(1)}, bf16[64,2048]{1,0:T(8,128)(2,1)S(1)}, u32[]{:S(2)}, u32[]{:S(2)}) collective-permute-start(bf16[64,2048]{1,0:T(8,128)(2,1)S(1)} %get-tuple-element.19), channel_id=1, source_target_pairs={{0,16},{16,0},{1,17},{17,1},{2,18},{18,2},{3,19},{19,3},{4,20},{20... | collective-permute-start | bytes 786440 | tf_op jit(solution)/shard_map/ppermute | solution.py:211
  48.6 17.3 %all-to-all-start.1 = ((f32[32,1,64]{2,1,0:T(1,128)}), f32[32,1,64]{2,1,0:T(1,128)S(1)}, u32[]{:S(2)}, u32[]{:S(2)}) async-start(f32[32,1,64]{2,1,0:T(1,128)} %bitcast.6), calls=%async_computation.1 | async-start | bytes 32768 | tf_op jit(solution)/shard_map/all_to_all | solution.py:216
  54.5 24.7 %collective-permute-start.4 = (bf16[128,2048]{1,0:T(8,128)(2,1)S(1)}, bf16[128,2048]{1,0:T(8,128)(2,1)S(1)}, u32[]{:S(2)}, u32[]{:S(2)}) collective-permute-start(bf16[128,2048]{1,0:T(8,128)(2,1)S(1)} %constant_dynamic-update-slice_fusion.refs_0_), channel_id=1, source_target_pairs={{0,4},{4,8},{8,12},{12,0},{1,5},{5,9},{9,13},{13,1},{2,6},{6,10},{... | collective-permute-start | bytes 1572872 | tf_op jit(solution)/shard_map/ppermute | solution.py:224
  57.9 26.0 %collective-permute-start.5 = (bf16[128,2048]{1,0:T(8,128)(2,1)S(1)}, bf16[128,2048]{1,0:T(8,128)(2,1)}, u32[]{:S(2)}, u32[]{:S(2)}) collective-permute-start(bf16[128,2048]{1,0:T(8,128)(2,1)S(1)} %constant_dynamic-update-slice_fusion.refs_0_), channel_id=1, source_target_pairs={{0,8},{4,12},{8,0},{12,4},{1,9},{5,13},{9,1},{13,5},{2,10},{6,14},... | collective-permute-start | bytes 1572872 | tf_op jit(solution)/shard_map/ppermute | solution.py:224
  62.5 23.0 %collective-permute-start.6 = (bf16[128,2048]{1,0:T(8,128)(2,1)S(1)}, bf16[128,2048]{1,0:T(8,128)(2,1)}, u32[]{:S(2)}, u32[]{:S(2)}) collective-permute-start(bf16[128,2048]{1,0:T(8,128)(2,1)S(1)} %constant_dynamic-update-slice_fusion.refs_0_), channel_id=1, source_target_pairs={{0,12},{4,0},{8,4},{12,8},{1,13},{5,1},{9,5},{13,9},{2,14},{6,2},{... | collective-permute-start | bytes 1572872 | tf_op jit(solution)/shard_map/ppermute | solution.py:224
  67.8 20.6 %collective-permute-start.10 = (bf16[128,2048]{1,0:T(8,128)(2,1)}, bf16[128,2048]{1,0:T(8,128)(2,1)}, u32[]{:S(2)}, u32[]{:S(2)}) collective-permute-start(bf16[128,2048]{1,0:T(8,128)(2,1)} %slice.31), channel_id=1, source_target_pairs={{0,384},{128,0},{256,128},{384,256},{1,385},{129,1},{257,129},{385... | collective-permute-start | bytes 1572872 | tf_op jit(solution)/shard_map/ppermute | solution.py:213
  72.1 16.3 %collective-permute-start.9 = (bf16[128,2048]{1,0:T(8,128)(2,1)}, bf16[128,2048]{1,0:T(8,128)(2,1)}, u32[]{:S(2)}, u32[]{:S(2)}) collective-permute-start(bf16[128,2048]{1,0:T(8,128)(2,1)} %slice.30), channel_id=1, source_target_pairs={{0,128},{128,256},{256,384},{384,0},{1,129},{129,257},{257,385},{3... | collective-permute-start | bytes 1572872 | tf_op jit(solution)/shard_map/ppermute | solution.py:213
  75.2 13.2 %all-to-all-start.2 = ((f32[4,4,128]{2,1,0:T(4,128)}), f32[4,4,128]{2,1,0:T(4,128)S(1)}, u32[]{:S(2)}, u32[]{:S(2)}) async-start(f32[4,4,128]{2,1,0:T(4,128)} %broadcast_in_dim.25), calls=%async_computation.2 | async-start | bytes 16384 | tf_op jit(solution)/shard_map/all_to_all | solution.py:165
  91.6 3.4 %collective-permute-start.12 = (bf16[16,16,512]{2,1,0:T(8,128)(2,1)S(1)}, bf16[16,16,512]{2,1,0:T(8,128)(2,1)S(1)}, u32[]{:S(2)}, u32[]{:S(2)}) collective-permute-start(bf16[16,16,512]{2,1,0:T(8,128)(2,1)S(1)} %get-tuple-element.28), channel_id=1, source_target_pairs={{0,64},{64,0},{1,65},{65,1},{2,66},{66,2},{3,67},{67,3},{4,68},{68... | collective-permute-start | bytes 786440 | tf_op jit(solution)/shard_map/ppermute | solution.py:161
  96.0 18.5 %all-to-all-start.3 = ((bf16[2,16,16,512]{3,2,1,0:T(8,128)(2,1)}), bf16[2,16,16,512]{3,2,1,0:T(8,128)(2,1)}, u32[]{:S(2)}, u32[]{:S(2)}) async-start(bf16[2,16,16,512]{3,2,1,0:T(8,128)(2,1)} %pad_maximum_fusion), calls=%async_computation.3 | async-start | bytes 1048576 | tf_op jit(solution)/shard_map/all_to_all | solution.py:253
  100.2 0.8 copy-start.3
  105.2 0.8 copy-start.1
  106.0 3.4 %collective-permute-start.11 = (bf16[16,16,512]{2,1,0:T(8,128)(2,1)S(1)}, bf16[16,16,512]{2,1,0:T(8,128)(2,1)S(1)}, u32[]{:S(2)}, u32[]{:S(2)}) collective-permute-start(bf16[16,16,512]{2,1,0:T(8,128)(2,1)S(1)} %get-tuple-element.26), channel_id=1, source_target_pairs={{0,64},{64,0},{1,65},{65,1},{2,66},{66,2},{3,67},{67,3},{4,68},{68... | collective-permute-start | bytes 786440 | tf_op jit(solution)/shard_map/ppermute | solution.py:161

commit v11 on v10

--- a/solution.py
+++ b/solution.py
@@ -29,9 +29,9 @@
             base = (x * 2 + jnp.where(z1 == 0, low, 1 - low)) * ny
             for y in range(ny):
                 block = (z * ny + y) * nx + x
-                keep = mask_ref[row, block].astype(F32).astype(BF16)
-                out_ref[base + y, :, high * BLK : (high + 1) * BLK] = (
-                    adj_ref[0, :, block * BLK : (block + 1) * BLK] * keep
+                tile = adj_ref[0, :, block * BLK : (block + 1) * BLK]
+                out_ref[base + y, :, high * BLK : (high + 1) * BLK] = jnp.where(
+                    mask_ref[row, block] != 0, tile, jnp.zeros_like(tile)
                 )
 
 

time: 144 us -> 144 us (level)
  no operation moved by 1% of the time
where the time goes in v11:
time: 144 us; the launch traced here: 142 us
  starting transfers between devices  68.5 us (48%)
  blocking collectives  25.6 us (18%)
  waiting for transfers between devices  21.5 us (15%)
  Pallas kernels  13.4 us (9%)
  local copies, waits for them, and re-layouts  9.85 us (7%)
  other arithmetic  3.16 us (2%)
    all_to_all x1, blocking collectives, spread(): return lax.all_to_all(wide, axes, split_axis=0, concat_axis=0, tiled=True)  25.6 us
    ppermute x4, starting transfers between devices, step_x(): return lax.ppermute(piece, 'x', [(i, (i + d) % nx) for i in range(nx)])  12.9 us
    ppermute x3, starting transfers between devices, on_device(): lax.ppermute(near, 'y', [(i, (i + d) % ny) for i in range(ny)])  11.3 us
    ppermute x1, starting transfers between devices, on_device(): near = jnp.concatenate([shard, lax.ppermute(shard, 'z0', SWAP)], axis=0)  9.94 us
    all_to_all x1, starting transfers between devices, on_device(): lax.all_to_all(outgoing, group, split_axis=0, concat_axis=0, tiled=True)  9.08 us
    pallas_call x2, Pallas kernels, product(): call(functools.partial(product_kernel, group, ny), in_specs=[vmem] * (ny...  6.39 us
    ppermute x3, waiting for transfers between devices, on_device(): lax.ppermute(near, 'y', [(i, (i + d) % ny) for i in range(ny)])  6.27 us
    all_to_all x1, starting transfers between devices, on_device(): lax.all_to_all(partial.reshape(8 * ny, rows_dev), ('core', 'z1', 'z0', 'y...  5.86 us
  transfers between devices with their start and end apart: 17, of which 8 were waited for; matrix products, arithmetic and copies ran while one was open for 4% of the time, Pallas kernels for 4%

profile of v11, /device:TPU:32, one launch (start us, length us, event | category | flops | bytes accessed | tf_op | source)
XLA Modules:
  0.0 142.3 jit_solution(5824582684350857086)
XLA Ops:
  2.0 2.3 %shard_map.37.out_ref = bf16[32,64,256]{2,1,0:T(8,128)(2,1)} custom-call(s32[64,64]{1,0:T(8,128)S(1)} %copy-done.2, bf16[1,64,8192]{2,1,0:T(8,128)(2,1)S(1)} %copy-done), custom_call_target="tpu_custom_call" | custom-call | tf_op jit(solution)/shard_map/pallas_call | solution.py:174
  4.3 9.1 %all-to-all-start = ((bf16[32,64,256]{2,1,0:T(8,128)(2,1)}), bf16[32,64,256]{2,1,0:T(8,128)(2,1)S(1)}, u32[]{:S(2)}, u32[]{:S(2)}) async-start(bf16[32,64,256]{2,1,0:T(8,128)(2,1)} %shard_map.37.out_ref), calls=%async_computation | async-start | bytes 2097152 | tf_op jit(solution)/shard_map/all_to_all | solution.py:180
  13.4 1.5 %shard_map.39 = bf16[2,64,2048]{2,1,0:T(8,128)(2,1)S(1)} custom-call(bf16[32,64,256]{2,1,0:T(8,128)(2,1)} %shard_map.37.out_ref), custom_call_target="tpu_custom_call" | custom-call | tf_op jit(solution)/shard_map/pallas_call | solution.py:182
  15.0 3.4 %collective-permute-start = (bf16[64,2048]{1,0:T(8,128)(2,1)S(1)}, bf16[64,2048]{1,0:T(8,128)(2,1)S(1)}, u32[]{:S(2)}, u32[]{:S(2)}) collective-permute-start(bf16[64,2048]{1,0:T(8,128)(2,1)S(1)} %get-tuple-element.30), channel_id=1, source_target_pairs={{0,51},{48,1},{16,32},{32,16},{1,48},{49,2},{17,33},{33,17},{2,49}... | collective-permute-start | bytes 786440 | tf_op jit(solution)/shard_map/ppermute | solution.py:187
  18.4 1.9 %collective-permute-start.2 = (bf16[64,2048]{1,0:T(8,128)(2,1)S(1)}, bf16[64,2048]{1,0:T(8,128)(2,1)S(1)}, u32[]{:S(2)}, u32[]{:S(2)}) collective-permute-start(bf16[64,2048]{1,0:T(8,128)(2,1)S(1)} %get-tuple-element.29), channel_id=1, source_target_pairs={{0,115},{48,65},{16,96},{32,80},{1,112},{49,66},{17,97},{33,81},{2... | collective-permute-start | bytes 786440 | tf_op jit(solution)/shard_map/ppermute | solution.py:188
  20.3 1.5 %shard_map.38 = bf16[2,64,2048]{2,1,0:T(8,128)(2,1)S(1)} custom-call(bf16[32,64,256]{2,1,0:T(8,128)(2,1)} %shard_map.37.out_ref), custom_call_target="tpu_custom_call" | custom-call | tf_op jit(solution)/shard_map/pallas_call | solution.py:182
  21.8 3.6 %collective-permute-done.d10 = bf16[64,2048]{1,0:T(8,128)(2,1)S(1)} collective-permute-done((bf16[64,2048]{1,0:T(8,128)(2,1)S(1)}, bf16[64,2048]{1,0:T(8,128)(2,1)S(1)}, u32[]{:S(2)}, u32[]{:S(2)}) %collective-permute-start) | collective-permute-done | bytes 262176 | tf_op jit(solution)/shard_map/ppermute | solution.py:187
  25.5 1.9 %collective-permute-start.1 = (bf16[64,2048]{1,0:T(8,128)(2,1)S(1)}, bf16[64,2048]{1,0:T(8,128)(2,1)S(1)}, u32[]{:S(2)}, u32[]{:S(2)}) collective-permute-start(bf16[64,2048]{1,0:T(8,128)(2,1)S(1)} %get-tuple-element.17), channel_id=1, source_target_pairs={{0,64},{64,0},{1,65},{65,1},{2,66},{66,2},{3,67},{67,3},{4,68},{68... | collective-permute-start | bytes 786440 | tf_op jit(solution)/shard_map/ppermute | solution.py:161
  27.4 1.9 %collective-permute-done.2.d11 = bf16[64,2048]{1,0:T(8,128)(2,1)S(1)} collective-permute-done((bf16[64,2048]{1,0:T(8,128)(2,1)S(1)}, bf16[64,2048]{1,0:T(8,128)(2,1)S(1)}, u32[]{:S(2)}, u32[]{:S(2)}) %collective-permute-start.2) | collective-permute-done | bytes 262176 | tf_op jit(solution)/shard_map/ppermute | solution.py:188
  29.3 1.7 %shard_map.40 = (bf16[4,64,2048]{2,1,0:T(8,128)(2,1)S(1)}, bf16[64,2048]{1,0:T(8,128)(2,1)S(1)}, f32[4,64]{1,0:T(4,128)S(1)}) custom-call(bf16[32,64,256]{2,1,0:T(8,128)(2,1)S(1)} %all-to-all-done.recv_ref, bf16[64,2048]{1,0:T(8,128)(2,1)S(1)} %get-tuple-element.32.d00, bf16[64,2048]{1,0:T(8,128)(2,1)S(1)} %collective-permute-done.1.d01, ...), custom_call_target="tpu_custom_call" | custom-call | tf_op jit(solution)/shard_map/pallas_call | solution.py:191
  31.0 3.4 %collective-permute-start.7 = (bf16[256,2048]{1,0:T(8,128)(2,1)S(1)}, bf16[256,2048]{1,0:T(8,128)(2,1)S(1)}, u32[]{:S(2)}, u32[]{:S(2)}) collective-permute-start(bf16[256,2048]{1,0:T(8,128)(2,1)S(1)} %bitcast.28), channel_id=1, source_target_pairs={{0,128},{128,256},{256,384},{384,0},{1,129},{129,257},{257,385},{3... | collective-permute-start | bytes 3145736 | tf_op jit(solution)/shard_map/ppermute | solution.py:213
  34.4 3.6 %collective-permute-start.8 = (bf16[256,2048]{1,0:T(8,128)(2,1)S(1)}, bf16[256,2048]{1,0:T(8,128)(2,1)}, u32[]{:S(2)}, u32[]{:S(2)}) collective-permute-start(bf16[256,2048]{1,0:T(8,128)(2,1)S(1)} %bitcast.29), channel_id=1, source_target_pairs={{0,384},{128,0},{256,128},{384,256},{1,385},{129,1},{257,129},{385... | collective-permute-start | bytes 3145736 | tf_op jit(solution)/shard_map/ppermute | solution.py:213
  38.0 9.9 %collective-permute-start.3 = (bf16[64,2048]{1,0:T(8,128)(2,1)S(1)}, bf16[64,2048]{1,0:T(8,128)(2,1)S(1)}, u32[]{:S(2)}, u32[]{:S(2)}) collective-permute-start(bf16[64,2048]{1,0:T(8,128)(2,1)S(1)} %get-tuple-element.19), channel_id=1, source_target_pairs={{0,16},{16,0},{1,17},{17,1},{2,18},{18,2},{3,19},{19,3},{4,20},{20... | collective-permute-start | bytes 786440 | tf_op jit(solution)/shard_map/ppermute | solution.py:211
  48.6 5.9 %all-to-all-start.1 = ((f32[32,1,64]{2,1,0:T(1,128)}), f32[32,1,64]{2,1,0:T(1,128)S(1)}, u32[]{:S(2)}, u32[]{:S(2)}) async-start(f32[32,1,64]{2,1,0:T(1,128)} %bitcast.6), calls=%async_computation.1 | async-start | bytes 32768 | tf_op jit(solution)/shard_map/all_to_all | solution.py:216
  54.5 3.4 %collective-permute-start.4 = (bf16[128,2048]{1,0:T(8,128)(2,1)S(1)}, bf16[128,2048]{1,0:T(8,128)(2,1)S(1)}, u32[]{:S(2)}, u32[]{:S(2)}) collective-permute-start(bf16[128,2048]{1,0:T(8,128)(2,1)S(1)} %constant_dynamic-update-slice_fusion.refs_0_), channel_id=1, source_target_pairs={{0,4},{4,8},{8,12},{12,0},{1,5},{5,9},{9,13},{13,1},{2,6},{6,10},{... | collective-permute-start | bytes 1572872 | tf_op jit(solution)/shard_map/ppermute | solution.py:224
  57.9 4.6 %collective-permute-start.5 = (bf16[128,2048]{1,0:T(8,128)(2,1)S(1)}, bf16[128,2048]{1,0:T(8,128)(2,1)}, u32[]{:S(2)}, u32[]{:S(2)}) collective-permute-start(bf16[128,2048]{1,0:T(8,128)(2,1)S(1)} %constant_dynamic-update-slice_fusion.refs_0_), channel_id=1, source_target_pairs={{0,8},{4,12},{8,0},{12,4},{1,9},{5,13},{9,1},{13,5},{2,10},{6,14},... | collective-permute-start | bytes 1572872 | tf_op jit(solution)/shard_map/ppermute | solution.py:224
  62.5 3.4 %collective-permute-start.6 = (bf16[128,2048]{1,0:T(8,128)(2,1)S(1)}, bf16[128,2048]{1,0:T(8,128)(2,1)}, u32[]{:S(2)}, u32[]{:S(2)}) collective-permute-start(bf16[128,2048]{1,0:T(8,128)(2,1)S(1)} %constant_dynamic-update-slice_fusion.refs_0_), channel_id=1, source_target_pairs={{0,12},{4,0},{8,4},{12,8},{1,13},{5,1},{9,5},{13,9},{2,14},{6,2},{... | collective-permute-start | bytes 1572872 | tf_op jit(solution)/shard_map/ppermute | solution.py:224
  65.9 1.9 %slice.31 = bf16[128,2048]{1,0:T(8,128)(2,1)} slice(bf16[256,2048]{1,0:T(8,128)(2,1)} %collective-permute-done.8.refs_8_), slice={[128:256], [0:2048]} | slice | bytes 1048576 | tf_op jit(solution)/shard_map/slice | solution.py:232
  67.8 3.4 %collective-permute-start.10 = (bf16[128,2048]{1,0:T(8,128)(2,1)}, bf16[128,2048]{1,0:T(8,128)(2,1)}, u32[]{:S(2)}, u32[]{:S(2)}) collective-permute-start(bf16[128,2048]{1,0:T(8,128)(2,1)} %slice.31), channel_id=1, source_target_pairs={{0,384},{128,0},{256,128},{384,256},{1,385},{129,1},{257,129},{385... | collective-permute-start | bytes 1572872 | tf_op jit(solution)/shard_map/ppermute | solution.py:213
  72.1 2.4 %collective-permute-start.9 = (bf16[128,2048]{1,0:T(8,128)(2,1)}, bf16[128,2048]{1,0:T(8,128)(2,1)}, u32[]{:S(2)}, u32[]{:S(2)}) collective-permute-start(bf16[128,2048]{1,0:T(8,128)(2,1)} %slice.30), channel_id=1, source_target_pairs={{0,128},{128,256},{256,384},{384,0},{1,129},{129,257},{257,385},{3... | collective-permute-start | bytes 1572872 | tf_op jit(solution)/shard_map/ppermute | solution.py:213
  75.2 4.0 %all-to-all-start.2 = ((f32[4,4,128]{2,1,0:T(4,128)}), f32[4,4,128]{2,1,0:T(4,128)S(1)}, u32[]{:S(2)}, u32[]{:S(2)}) async-start(f32[4,4,128]{2,1,0:T(4,128)} %broadcast_in_dim.25), calls=%async_computation.2 | async-start | bytes 16384 | tf_op jit(solution)/shard_map/all_to_all | solution.py:165
  79.2 4.6 %collective-permute-done.5.refs_2_ = bf16[128,2048]{1,0:T(8,128)(2,1)} collective-permute-done((bf16[128,2048]{1,0:T(8,128)(2,1)S(1)}, bf16[128,2048]{1,0:T(8,128)(2,1)}, u32[]{:S(2)}, u32[]{:S(2)}) %collective-permute-start.5) | collective-permute-done | bytes 524320 | tf_op jit(solution)/shard_map/ppermute | solution.py:224
  83.9 1.6 %collective-permute-done.6.refs_3_ = bf16[128,2048]{1,0:T(8,128)(2,1)} collective-permute-done((bf16[128,2048]{1,0:T(8,128)(2,1)S(1)}, bf16[128,2048]{1,0:T(8,128)(2,1)}, u32[]{:S(2)}, u32[]{:S(2)}) %collective-permute-start.6) | collective-permute-done | bytes 524320 | tf_op jit(solution)/shard_map/ppermute | solution.py:224
  85.5 2.9 %all-to-all-done.2 = f32[4,4,128]{2,1,0:T(4,128)S(1)} async-done(((f32[4,4,128]{2,1,0:T(4,128)}), f32[4,4,128]{2,1,0:T(4,128)S(1)}, u32[]{:S(2)}, u32[]{:S(2)}) %all-to-all-start.2) | async-done | bytes 8224 | tf_op jit(solution)/shard_map/all_to_all | solution.py:165
  88.4 3.2 %shard_map.42 = (f32[16,16,512]{2,1,0:T(8,128)S(1)}, bf16[16,16,512]{2,1,0:T(8,128)(2,1)S(1)}) custom-call(bf16[128,2048]{1,0:T(8,128)(2,1)S(1)} %constant_dynamic-update-slice_fusion.refs_0_, bf16[128,2048]{1,0:T(8,128)(2,1)S(1)} %collective-permute-done.4.refs_1_, bf16[128,2048]{1,0:T(8,128)(2,1)} %collective-permute-done.5.refs_2_, ...), custom_call_target="tpu_custom_call" | custom-call | tf_op jit(solution)/shard_map/pallas_call | solution.py:243
  91.6 1.9 %collective-permute-start.12 = (bf16[16,16,512]{2,1,0:T(8,128)(2,1)S(1)}, bf16[16,16,512]{2,1,0:T(8,128)(2,1)S(1)}, u32[]{:S(2)}, u32[]{:S(2)}) collective-permute-start(bf16[16,16,512]{2,1,0:T(8,128)(2,1)S(1)} %get-tuple-element.28), channel_id=1, source_target_pairs={{0,64},{64,0},{1,65},{65,1},{2,66},{66,2},{3,67},{67,3},{4,68},{68... | collective-permute-start | bytes 786440 | tf_op jit(solution)/shard_map/ppermute | solution.py:161
  93.6 1.5 %collective-permute-done.12 = bf16[16,16,512]{2,1,0:T(8,128)(2,1)S(1)} collective-permute-done((bf16[16,16,512]{2,1,0:T(8,128)(2,1)S(1)}, bf16[16,16,512]{2,1,0:T(8,128)(2,1)S(1)}, u32[]{:S(2)}, u32[]{:S(2)}) %collective-permute-start.12) | collective-permute-done | bytes 262176 | tf_op jit(solution)/shard_map/ppermute | solution.py:161
  96.0 4.2 %all-to-all-start.3 = ((bf16[2,16,16,512]{3,2,1,0:T(8,128)(2,1)}), bf16[2,16,16,512]{3,2,1,0:T(8,128)(2,1)}, u32[]{:S(2)}, u32[]{:S(2)}) async-start(bf16[2,16,16,512]{3,2,1,0:T(8,128)(2,1)} %pad_maximum_fusion), calls=%async_computation.3 | async-start | bytes 1048576 | tf_op jit(solution)/shard_map/all_to_all | solution.py:253
  102.0 3.2 %shard_map.41 = (f32[16,16,512]{2,1,0:T(8,128)S(1)}, bf16[16,16,512]{2,1,0:T(8,128)(2,1)S(1)}) custom-call(bf16[128,2048]{1,0:T(8,128)(2,1)S(1)} %constant_dynamic-update-slice_fusion.refs_0_, bf16[128,2048]{1,0:T(8,128)(2,1)S(1)} %collective-permute-done.4.refs_1_, bf16[128,2048]{1,0:T(8,128)(2,1)} %collective-permute-done.5.refs_2_, ...), custom_call_target="tpu_custom_call" | custom-call | tf_op jit(solution)/shard_map/pallas_call | solution.py:243
  106.0 2.0 %collective-permute-start.11 = (bf16[16,16,512]{2,1,0:T(8,128)(2,1)S(1)}, bf16[16,16,512]{2,1,0:T(8,128)(2,1)S(1)}, u32[]{:S(2)}, u32[]{:S(2)}) collective-permute-start(bf16[16,16,512]{2,1,0:T(8,128)(2,1)S(1)} %get-tuple-element.26), channel_id=1, source_target_pairs={{0,64},{64,0},{1,65},{65,1},{2,66},{66,2},{3,67},{67,3},{4,68},{68... | collective-permute-start | bytes 786440 | tf_op jit(solution)/shard_map/ppermute | solution.py:161
  109.5 5.0 %all-to-all-done.3 = bf16[2,16,16,512]{3,2,1,0:T(8,128)(2,1)} async-done(((bf16[2,16,16,512]{3,2,1,0:T(8,128)(2,1)}), bf16[2,16,16,512]{3,2,1,0:T(8,128)(2,1)}, u32[]{:S(2)}, u32[]{:S(2)}) %all-to-all-start.3) | async-done | bytes 524320 | tf_op jit(solution)/shard_map/all_to_all | solution.py:253
  115.8 25.6 %all_to_all.32 = f32[32,4,128]{2,1,0:T(4,128)S(1)} all-to-all(f32[32,4,128]{2,1,0:T(4,128)S(1)} %broadcast_in_dim.28), channel_id=1, replica_groups=mesh['x'=4,'core'=2,'z1'=2,'z0'=2,'y'=4,'zhi'=4] {'x','core','zhi'}, dimensions={0} | all-to-all | bytes 131072 | tf_op jit(solution)/shard_map/all_to_all | solution.py:165
  (44 shorter events, 11.4 us)
Async XLA Ops:
  0.0 1.2 copy-start
  1.2 0.8 copy-start.2
  4.3 24.9 %all-to-all-start = ((bf16[32,64,256]{2,1,0:T(8,128)(2,1)}), bf16[32,64,256]{2,1,0:T(8,128)(2,1)S(1)}, u32[]{:S(2)}, u32[]{:S(2)}) async-start(bf16[32,64,256]{2,1,0:T(8,128)(2,1)} %shard_map.37.out_ref), calls=%async_computation | async-start | bytes 2097152 | tf_op jit(solution)/shard_map/all_to_all | solution.py:180
  15.0 10.5 %collective-permute-start = (bf16[64,2048]{1,0:T(8,128)(2,1)S(1)}, bf16[64,2048]{1,0:T(8,128)(2,1)S(1)}, u32[]{:S(2)}, u32[]{:S(2)}) collective-permute-start(bf16[64,2048]{1,0:T(8,128)(2,1)S(1)} %get-tuple-element.30), channel_id=1, source_target_pairs={{0,51},{48,1},{16,32},{32,16},{1,48},{49,2},{17,33},{33,17},{2,49}... | collective-permute-start | bytes 786440 | tf_op jit(solution)/shard_map/ppermute | solution.py:187
  18.4 10.9 %collective-permute-start.2 = (bf16[64,2048]{1,0:T(8,128)(2,1)S(1)}, bf16[64,2048]{1,0:T(8,128)(2,1)S(1)}, u32[]{:S(2)}, u32[]{:S(2)}) collective-permute-start(bf16[64,2048]{1,0:T(8,128)(2,1)S(1)} %get-tuple-element.29), channel_id=1, source_target_pairs={{0,115},{48,65},{16,96},{32,80},{1,112},{49,66},{17,97},{33,81},{2... | collective-permute-start | bytes 786440 | tf_op jit(solution)/shard_map/ppermute | solution.py:188
  25.5 3.8 %collective-permute-start.1 = (bf16[64,2048]{1,0:T(8,128)(2,1)S(1)}, bf16[64,2048]{1,0:T(8,128)(2,1)S(1)}, u32[]{:S(2)}, u32[]{:S(2)}) collective-permute-start(bf16[64,2048]{1,0:T(8,128)(2,1)S(1)} %get-tuple-element.17), channel_id=1, source_target_pairs={{0,64},{64,0},{1,65},{65,1},{2,66},{66,2},{3,67},{67,3},{4,68},{68... | collective-permute-start | bytes 786440 | tf_op jit(solution)/shard_map/ppermute | solution.py:161
  31.0 34.9 %collective-permute-start.7 = (bf16[256,2048]{1,0:T(8,128)(2,1)S(1)}, bf16[256,2048]{1,0:T(8,128)(2,1)S(1)}, u32[]{:S(2)}, u32[]{:S(2)}) collective-permute-start(bf16[256,2048]{1,0:T(8,128)(2,1)S(1)} %bitcast.28), channel_id=1, source_target_pairs={{0,128},{128,256},{256,384},{384,0},{1,129},{129,257},{257,385},{3... | collective-permute-start | bytes 3145736 | tf_op jit(solution)/shard_map/ppermute | solution.py:213
  34.4 31.5 %collective-permute-start.8 = (bf16[256,2048]{1,0:T(8,128)(2,1)S(1)}, bf16[256,2048]{1,0:T(8,128)(2,1)}, u32[]{:S(2)}, u32[]{:S(2)}) collective-permute-start(bf16[256,2048]{1,0:T(8,128)(2,1)S(1)} %bitcast.29), channel_id=1, source_target_pairs={{0,384},{128,0},{256,128},{384,256},{1,385},{129,1},{257,129},{385... | collective-permute-start | bytes 3145736 | tf_op jit(solution)/shard_map/ppermute | solution.py:213
  38.0 16.5 %collective-permute-start.3 = (bf16[64,2048]{1,0:T(8,128)(2,1)S(1)}, bf16[64,2048]{1,0:T(8,128)(2,1)S(1)}, u32[]{:S(2)}, u32[]{:S(2)}) collective-permute-start(bf16[64,2048]{1,0:T(8,128)(2,1)S(1)} %get-tuple-element.19), channel_id=1, source_target_pairs={{0,16},{16,0},{1,17},{17,1},{2,18},{18,2},{3,19},{19,3},{4,20},{20... | collective-permute-start | bytes 786440 | tf_op jit(solution)/shard_map/ppermute | solution.py:211
  48.6 17.3 %all-to-all-start.1 = ((f32[32,1,64]{2,1,0:T(1,128)}), f32[32,1,64]{2,1,0:T(1,128)S(1)}, u32[]{:S(2)}, u32[]{:S(2)}) async-start(f32[32,1,64]{2,1,0:T(1,128)} %bitcast.6), calls=%async_computation.1 | async-start | bytes 32768 | tf_op jit(solution)/shard_map/all_to_all | solution.py:216
  54.5 24.7 %collective-permute-start.4 = (bf16[128,2048]{1,0:T(8,128)(2,1)S(1)}, bf16[128,2048]{1,0:T(8,128)(2,1)S(1)}, u32[]{:S(2)}, u32[]{:S(2)}) collective-permute-start(bf16[128,2048]{1,0:T(8,128)(2,1)S(1)} %constant_dynamic-update-slice_fusion.refs_0_), channel_id=1, source_target_pairs={{0,4},{4,8},{8,12},{12,0},{1,5},{5,9},{9,13},{13,1},{2,6},{6,10},{... | collective-permute-start | bytes 1572872 | tf_op jit(solution)/shard_map/ppermute | solution.py:224
  57.9 26.0 %collective-permute-start.5 = (bf16[128,2048]{1,0:T(8,128)(2,1)S(1)}, bf16[128,2048]{1,0:T(8,128)(2,1)}, u32[]{:S(2)}, u32[]{:S(2)}) collective-permute-start(bf16[128,2048]{1,0:T(8,128)(2,1)S(1)} %constant_dynamic-update-slice_fusion.refs_0_), channel_id=1, source_target_pairs={{0,8},{4,12},{8,0},{12,4},{1,9},{5,13},{9,1},{13,5},{2,10},{6,14},... | collective-permute-start | bytes 1572872 | tf_op jit(solution)/shard_map/ppermute | solution.py:224
  62.5 23.0 %collective-permute-start.6 = (bf16[128,2048]{1,0:T(8,128)(2,1)S(1)}, bf16[128,2048]{1,0:T(8,128)(2,1)}, u32[]{:S(2)}, u32[]{:S(2)}) collective-permute-start(bf16[128,2048]{1,0:T(8,128)(2,1)S(1)} %constant_dynamic-update-slice_fusion.refs_0_), channel_id=1, source_target_pairs={{0,12},{4,0},{8,4},{12,8},{1,13},{5,1},{9,5},{13,9},{2,14},{6,2},{... | collective-permute-start | bytes 1572872 | tf_op jit(solution)/shard_map/ppermute | solution.py:224
  67.8 20.6 %collective-permute-start.10 = (bf16[128,2048]{1,0:T(8,128)(2,1)}, bf16[128,2048]{1,0:T(8,128)(2,1)}, u32[]{:S(2)}, u32[]{:S(2)}) collective-permute-start(bf16[128,2048]{1,0:T(8,128)(2,1)} %slice.31), channel_id=1, source_target_pairs={{0,384},{128,0},{256,128},{384,256},{1,385},{129,1},{257,129},{385... | collective-permute-start | bytes 1572872 | tf_op jit(solution)/shard_map/ppermute | solution.py:213
  72.1 16.3 %collective-permute-start.9 = (bf16[128,2048]{1,0:T(8,128)(2,1)}, bf16[128,2048]{1,0:T(8,128)(2,1)}, u32[]{:S(2)}, u32[]{:S(2)}) collective-permute-start(bf16[128,2048]{1,0:T(8,128)(2,1)} %slice.30), channel_id=1, source_target_pairs={{0,128},{128,256},{256,384},{384,0},{1,129},{129,257},{257,385},{3... | collective-permute-start | bytes 1572872 | tf_op jit(solution)/shard_map/ppermute | solution.py:213
  75.2 13.2 %all-to-all-start.2 = ((f32[4,4,128]{2,1,0:T(4,128)}), f32[4,4,128]{2,1,0:T(4,128)S(1)}, u32[]{:S(2)}, u32[]{:S(2)}) async-start(f32[4,4,128]{2,1,0:T(4,128)} %broadcast_in_dim.25), calls=%async_computation.2 | async-start | bytes 16384 | tf_op jit(solution)/shard_map/all_to_all | solution.py:165
  91.6 3.4 %collective-permute-start.12 = (bf16[16,16,512]{2,1,0:T(8,128)(2,1)S(1)}, bf16[16,16,512]{2,1,0:T(8,128)(2,1)S(1)}, u32[]{:S(2)}, u32[]{:S(2)}) collective-permute-start(bf16[16,16,512]{2,1,0:T(8,128)(2,1)S(1)} %get-tuple-element.28), channel_id=1, source_target_pairs={{0,64},{64,0},{1,65},{65,1},{2,66},{66,2},{3,67},{67,3},{4,68},{68... | collective-permute-start | bytes 786440 | tf_op jit(solution)/shard_map/ppermute | solution.py:161
  96.0 18.5 %all-to-all-start.3 = ((bf16[2,16,16,512]{3,2,1,0:T(8,128)(2,1)}), bf16[2,16,16,512]{3,2,1,0:T(8,128)(2,1)}, u32[]{:S(2)}, u32[]{:S(2)}) async-start(bf16[2,16,16,512]{3,2,1,0:T(8,128)(2,1)} %pad_maximum_fusion), calls=%async_computation.3 | async-start | bytes 1048576 | tf_op jit(solution)/shard_map/all_to_all | solution.py:253
  100.2 0.8 copy-start.3
  105.2 0.8 copy-start.1
  106.0 3.4 %collective-permute-start.11 = (bf16[16,16,512]{2,1,0:T(8,128)(2,1)S(1)}, bf16[16,16,512]{2,1,0:T(8,128)(2,1)S(1)}, u32[]{:S(2)}, u32[]{:S(2)}) collective-permute-start(bf16[16,16,512]{2,1,0:T(8,128)(2,1)S(1)} %get-tuple-element.26), channel_id=1, source_target_pairs={{0,64},{64,0},{1,65},{65,1},{2,66},{66,2},{3,67},{67,3},{4,68},{68... | collective-permute-start | bytes 786440 | tf_op jit(solution)/shard_map/ppermute | solution.py:161
